TPU v7x, 128 devices: a whole 4x4x4 slice. The times are simulated.
128 devices in a mesh: fit: 8 (over x, core), pair: 16 (over z, y).
Axes of the slice: x: 4, y: 4, z: 4, core: 2. Of those that a mesh axis runs over, the one named last changes fastest.
Arguments:
- ints: bfloat16 [2048, 8, 128, 128], P(('fit', 'pair')), may hold values from -6 to 6
- tile_mu: int32 [2048], P(('fit', 'pair')), may hold values from 0 to 15
- tile_lam: int32 [2048], P(('fit', 'pair')), may hold values from 0 to 15
- tile_live: int32 [2048], P(('fit', 'pair')), may hold values 0 or 1
- coefficients: bfloat16 [2048, 1024], replicated, may hold values from -0.5 to 0.5
- occ_ids: int32 [2], replicated, may hold values from 0 to 7
Outputs:
- exchange: float32 [2048, 2048], P('pair', 'fit')
All inputs are finite; a program needn't handle non-finite values. No bound on the sum of `tile_live` on one device may be relied on, other than what follows from the above.
Results may differ from a plain program's by a relative error of at most 0.00045.
Values sent between devices are 32-bit elements; how exact they have to be, the bound alone decides.
No kernel may reach another device: no remote copies, remote signals or barrier semaphores. Data moves between devices by JAX's collectives and lax.ppermute only.
A program may use at most 256 MiB of HBM per device.

v0:
```python
import math

import jax
import jax.numpy as jnp
from jax import lax
from jax.sharding import PartitionSpec as P

OCC = 128
OBLK = 2


def on_device(ints, tile_mu, tile_lam, tile_live, coefficients, occ_ids):
    count_fit = lax.axis_size("fit")
    count_pair = lax.axis_size("pair")
    fitting = ints.shape[1]
    tile_width = ints.shape[2]
    basis_count = coefficients.shape[0]
    basis_tiles = basis_count // tile_width
    rows_own = basis_count // count_pair
    k_scale = 1.0 / math.sqrt(count_fit * count_pair * fitting * OCC * OBLK)
    positions = jnp.arange(basis_tiles, dtype=jnp.int32)
    onehot = (tile_mu[:, None] == positions[None, :]).astype(jnp.float32) * tile_live[
        :, None
    ].astype(jnp.float32)

    def half_transform(occ_block):
        first_col = occ_ids[occ_block] * OCC
        cblock = lax.dynamic_slice_in_dim(coefficients, first_col, OCC, 1).reshape(
            basis_tiles, tile_width, OCC
        )
        lam_rows = cblock[tile_lam]
        products = jnp.einsum("tpml,tli->tpmi", ints, lam_rows, preferred_element_type=jnp.float32)
        buffer = jnp.einsum("tn,tpmi->pnmi", onehot, products, precision=lax.Precision.HIGHEST)
        return buffer.astype(jnp.bfloat16).reshape(fitting, basis_count, OCC)

    half_list = [half_transform(occ_block) for occ_block in range(OBLK)]
    summed = jnp.zeros((lax.axis_size("pair") * rows_own, basis_count), jnp.float32)
    for half_block in half_list:
        summed = summed + jnp.einsum(
            "pmi,pni->mn", half_block, half_block, preferred_element_type=jnp.float32
        )
    owned = lax.psum_scatter(summed * k_scale, "pair", scatter_dimension=0, tiled=True)
    return lax.psum_scatter(owned, "fit", scatter_dimension=1, tiled=True)


def solution(mesh):
    return jax.shard_map(
        on_device,
        mesh=mesh,
        in_specs=(
            P(("fit", "pair"), None, None, None),
            P(("fit", "pair")),
            P(("fit", "pair")),
            P(("fit", "pair")),
            P(),
            P(),
        ),
        out_specs=P("pair", "fit"),
        check_vma=False,
    )
```

profile of v0, /device:TPU:6, one launch (start us, length us, event | category | flops | bytes accessed | tf_op | source)
XLA Modules:
  0.0 246.7 jit_solution(4889387948141394103)
XLA Ops:
  6.5 0.0 reduce-scatter.3.cloned.1.call-start
  6.5 1.3 fusion.25
  9.1 0.7 convert_element_type.17
  9.7 0.7 compare_select_fusion
  10.4 1.3 constant_dynamic-slice_fusion
  11.7 0.6 gather_fusion.1
  12.3 0.6 gather_fusion
  13.0 6.7 %fusion.11 = f32[16,128,8,128]{3,1,2,0:T(8,128)} fusion(bf16[16,8,128,128]{3,2,1,0:T(8,128)(2,1)} %param.6, bf16[16,128,128]{2,1,0:T(8,128)(2,1)S(1)} %gather_fusion), kind=kOutput, calls=%fused_computation.12 | convolution fusion | flops 536870912 | bytes 13107200 | tf_op jit(solution)/shard_map/tpml,tli->tpmi/dot_general | solution.py:32
  19.7 0.0 copy-start.2
  19.7 9.2 %copy.10 = f32[16,128,8,128]{1,0,3,2:T(8,128)} copy(f32[16,128,8,128]{3,1,2,0:T(8,128)} %fusion.11) | data formatting | bytes 16777216 | tf_op jit(solution)/shard_map/tpml,tli->tpmi/dot_general | solution.py:32
  28.9 0.0 copy-done.2
  28.9 9.6 %convert_bitcast_fusion.1 = bf16[8,16,128,128]{3,1,2,0:T(8,128)(2,1)S(1)} fusion(f32[16,128,8,128]{1,0,3,2:T(8,128)} %copy.10, f32[16]{0:T(128)S(1)} %convert_element_type.17, s32[16]{0:T(128)S(1)} %copy-done.2), kind=kOutput, calls=%fused_computation.9 | convolution fusion | flops 404750848 | bytes 12583040 | tf_op jit(solution)/shard_map/tn,tpmi->pnmi/dot_general | solution.py:33
  38.6 0.0 copy-start
  38.6 3.1 %copy.7 = bf16[8,16,128,128]{3,2,1,0:T(8,128)(2,1)} copy(bf16[8,16,128,128]{3,1,2,0:T(8,128)(2,1)S(1)} %convert_bitcast_fusion.1) | data formatting | bytes 8388608 | tf_op jit(solution)/shard_map/convert_element_type | solution.py:34
  41.7 0.0 copy-done
  41.7 4.5 %fusion.9 = f32[16,128,8,128]{3,1,2,0:T(8,128)} fusion(bf16[16,8,128,128]{3,2,1,0:T(8,128)(2,1)S(1)} %copy-done, bf16[16,128,128]{2,1,0:T(8,128)(2,1)S(1)} %gather_fusion.1), kind=kOutput, calls=%fused_computation.10 | convolution fusion | flops 536870912 | bytes 13107200 | tf_op jit(solution)/shard_map/tpml,tli->tpmi/dot_general | solution.py:32
  46.2 9.2 %copy.13 = f32[16,128,8,128]{1,0,3,2:T(8,128)} copy(f32[16,128,8,128]{3,1,2,0:T(8,128)} %fusion.9) | data formatting | bytes 16777216 | tf_op jit(solution)/shard_map/tpml,tli->tpmi/dot_general | solution.py:32
  55.4 9.8 %convert_bitcast_fusion = bf16[8,16,128,128]{3,1,2,0:T(8,128)(2,1)S(1)} fusion(f32[16,128,8,128]{1,0,3,2:T(8,128)} %copy.13, f32[16]{0:T(128)S(1)} %convert_element_type.17, s32[16]{0:T(128)S(1)} %copy-done.2), kind=kOutput, calls=%fused_computation.8 | convolution fusion | flops 404750848 | bytes 12583040 | tf_op jit(solution)/shard_map/tn,tpmi->pnmi/dot_general | solution.py:33
  65.2 0.0 copy-start.1
  65.2 1.2 copy.8
  66.4 1.0 copy-done.1
  67.4 11.7 %fusion.26 = f32[2048,2048,1]{1,0,2:T(8,128)} fusion(bf16[8,2048,128]{2,1,0:T(8,128)(2,1)S(1)} %bitcast.49), kind=kOutput, calls=%fused_computation.32 | convolution fusion | flops 8589934592 | bytes 20971520 | tf_op jit(solution)/shard_map/pmi,pni->mn/dot_general | solution.py:39
  79.1 17.0 %fusion = f32[2048,2048]{1,0:T(8,128)} fusion(f32[2048,2048,1]{1,0,2:T(8,128)} %fusion.26, bf16[8,2048,128]{2,1,0:T(8,128)(2,1)S(1)} %bitcast.50), kind=kOutput, calls=%fused_computation.3 | convolution fusion | flops 8598323200 | bytes 37748736 | tf_op jit(solution)/shard_map/pmi,pni->mn/dot_general | solution.py:39
  96.1 0.0 reduce-scatter.3.cloned.1.call-update
  96.2 0.0 reduce-scatter.5.cloned.1.call-start
  96.2 113.2 %reduce-scatter.3.cloned.1.call-done = f32[128,2048]{1,0:T(8,128)} async-done(((f32[2048,2048]{1,0:T(8,128)}), f32[128,2048]{1,0:T(8,128)}) %reduce-scatter.3.cloned.1.call-update) | async-done | bytes 1048592 | tf_op jit(solution)/shard_map/reduce_scatter | solution.py:42
  209.4 0.0 reduce-scatter.5.cloned.1.call-update
  209.4 30.4 %reduce-scatter.5.cloned.1.call-done = f32[128,256]{1,0:T(8,128)} async-done(((f32[128,2048]{1,0:T(8,128)}), f32[128,256]{1,0:T(8,128)}) %reduce-scatter.5.cloned.1.call-update) | async-done | bytes 131088 | tf_op jit(solution)/shard_map/reduce_scatter | solution.py:43
  (1 shorter events, 0.0 us)
Async XLA Ops:
  6.5 202.9 %reduce-scatter.3.cloned.1.call-start = ((), (), s32[]{:S(2)}) async-start(), calls=%async_computation.2 | async-start | bytes 17825792 | tf_op jit(solution)/shard_map/reduce_scatter | solution.py:42
  19.7 9.2 %copy-start.2 = (s32[16]{0:T(128)S(1)}, s32[16]{0:T(128)}, u32[]{:S(2)}) copy-start(s32[16]{0:T(128)} %param.7) | copy-start | bytes 196
  38.6 3.1 %copy-start = (bf16[16,8,128,128]{3,2,1,0:T(8,128)(2,1)S(1)}, bf16[16,8,128,128]{3,2,1,0:T(8,128)(2,1)}, u32[]{:S(2)}) copy-start(bf16[16,8,128,128]{3,2,1,0:T(8,128)(2,1)} %param.6) | copy-start | bytes 12582916
  65.2 2.2 copy-start.1
  96.2 143.7 %reduce-scatter.5.cloned.1.call-start = ((), (), s32[]{:S(2)}) async-start(), calls=%async_computation.3 | async-start | bytes 1179648 | tf_op jit(solution)/shard_map/reduce_scatter | solution.py:43
Sparse Core Ops, SparseCore 0:
  96.3 113.0 reduce-scatter.2
  211.8 28.0 reduce-scatter.4
where the time goes:
time: 250 us; the launch traced here: 247 us
  waiting for transfers between devices  144 us (58%)
  matrix products  59.4 us (24%)
  local copies, waits for them, and re-layouts  27.6 us (11%)
  between operations  14.7 us (6%)
    reduce_scatter x1, waiting for transfers between devices, on_device(): lax.psum_scatter(summed * k_scale, 'pair', scatter_dimension=0, tiled=True)  113 us
    reduce_scatter x1, waiting for transfers between devices, on_device(): return lax.psum_scatter(owned, 'fit', scatter_dimension=1, tiled=True)  30.4 us
    dot_general x2, matrix products, on_device(): jnp.einsum('pmi,pni->mn', half_block, half_block, preferred_element_type=...  28.7 us
    dot_general x2, matrix products, half_transform(): jnp.einsum('tn,tpmi->pnmi', onehot, products, precision=lax.Precision.HIG...  19.4 us
    dot_general x2, local copies, waits for them, and re-layouts, half_transform(): jnp.einsum('tpml,tli->tpmi', ints, lam_rows, preferred_element_type=jnp.f...  18.4 us
    dot_general x2, matrix products, half_transform(): jnp.einsum('tpml,tli->tpmi', ints, lam_rows, preferred_element_type=jnp.f...  11.3 us
  transfers between devices with their start and end apart: 2, of which 2 were waited for; matrix products, arithmetic and copies ran while one was open for 0% of the time, Pallas kernels for 0%

commit v1 on v0

v1 whole, which is shorter than its diff:
```python
import functools
import math

import jax
import jax.numpy as jnp
from jax import lax
from jax.experimental import pallas as pl
from jax.experimental.pallas import tpu as pltpu
from jax.sharding import PartitionSpec as P

OCC = 128
OBLK = 2
BT = 128
EXTRA = 8
COLOURS = ((0, 24), (24, 48), (48, 72), (72, 104), (104, 128))
AXES = ("fit", "pair")
NDEV = 128
SHARES = NDEV // 2
PARTS = len(COLOURS)
KERNEL_VMEM = 28 * 1024 * 1024
LIST = 32
PARTNERS = ((), (1,), (0,), (0, 1))


def coords(index):
    return index >> 5, (index >> 4) & 1, (index >> 2) & 3, index & 3


def index_of(x, core, z, y):
    return (x << 5) | (core << 4) | (z << 2) | y


def flipped(index, axes, second):
    x, core, z, y = coords(index)
    flip = 3 if (core == 1) != second else 1
    place = [x, z, y]
    for axis in axes:
        place[axis] ^= flip
    return index_of(place[0], core, place[1], place[2])


def axis_pairs(axes, second):
    return [(index, flipped(index, axes, second)) for index in range(NDEV)]


def core_pairs():
    return [(index, index ^ 16) for index in range(NDEV)]


def mirror(index):
    x, core, z, y = coords(index)
    row, col = z * 4 + y, x * 2 + core
    high = row >> 1
    if high < col:
        row, col = 2 * col + (row & 1), high
    elif high > col:
        row, col = 2 * col + 1 - (row & 1), high
    else:
        row ^= 1
    return index_of(col >> 1, col & 1, row >> 2, row & 3)


def bits_of(r, core):
    top, mixed = r >> 1, (r >> 1) ^ (r & 1)
    return jnp.where(core == 0, mixed, top), jnp.where(core == 0, top, mixed)


def row_place(row, core, my_z, my_y):
    z_high, z_low = bits_of((row >> 2) ^ my_z, core)
    y_high, y_low = bits_of((row & 3) ^ my_y, core)
    return z_high * 16 + y_high * 8 + z_low * 2 + y_low


def col_place(col, my_x):
    x_high, x_low = bits_of((col >> 1) ^ my_x, col & 1)
    return x_high * 32 + x_low * 4


def my_place():
    fit, pair = lax.axis_index("fit"), lax.axis_index("pair")
    return fit >> 1, fit & 1, pair >> 2, pair & 3


def packed_place(pair, me):
    my_x, _, my_z, my_y = me
    return row_place(2 * pair + 1, pair & 1, my_z, my_y) + col_place(pair, my_x)


def partial_kernel(mu_hbm, lam_hbm, live_hbm, occ_hbm, ints, coeff, *refs):
    keeps, sends, refs = refs[:PARTS], refs[PARTS : 2 * PARTS], refs[2 * PARTS :]
    (
        ints_v, coeff_v, acc, half, diag, info, mu, lam, live, occ,
        order, first, count, place, ints_sem, coeff_sem, small_sem,
    ) = refs
    slots, fitting = ints.shape[0], ints.shape[1]
    tiles = coeff.shape[0] // BT
    me = my_place()
    my_x, my_core, my_z, my_y = me

    def coeff_copy(b):
        start = pl.multiple_of(occ[b] * OCC, OCC)
        return pltpu.make_async_copy(
            coeff.at[:, pl.ds(start, OCC)], coeff_v.at[:, pl.ds(b * OCC, OCC)], coeff_sem.at[b]
        )

    def ints_copy(t):
        return pltpu.make_async_copy(ints.at[t], ints_v.at[t], ints_sem.at[t])

    small = [
        pltpu.make_async_copy(source, target, small_sem.at[i])
        for i, (source, target) in enumerate(((occ_hbm, occ), (mu_hbm, mu), (live_hbm, live), (lam_hbm, lam)))
    ]
    for copy in small:
        copy.start()
    small[0].wait()
    for b in range(OBLK):
        coeff_copy(b).start()
    for copy in small[1:]:
        copy.wait()

    for m in range(tiles):
        place[m] = 0
    for t in range(slots):
        place[mu[t]] = place[mu[t]] + live[t]
    n_slots, n_tiles = jnp.int32(0), jnp.int32(0)
    for m in range(tiles):
        here = place[m]
        info[n_tiles] = m
        first[n_tiles] = n_slots
        count[n_tiles] = here
        place[m] = n_slots
        n_slots = n_slots + here
        n_tiles = n_tiles + (here > 0).astype(jnp.int32)
    for t in range(slots):
        at = place[mu[t]]
        order[jnp.where(live[t] == 1, at, LIST - 1)] = t
        place[mu[t]] = at + live[t]

    def fetch(s, carry):
        ints_copy(order[s]).start()
        return carry

    lax.fori_loop(0, n_slots, fetch, 0)
    for r in range(tiles):
        name = jnp.where(r < n_tiles, info[r], 0)
        info[r] = name
        info[LIST + r] = row_place(name, 0, my_z, my_y)
        info[2 * LIST + r] = row_place(name, 1, my_z, my_y)
        info[3 * LIST + r] = col_place(name >> 1, my_x)

    for ref in keeps + sends + (diag,):
        ref[...] = jnp.zeros_like(ref)
    for b in range(OBLK):
        coeff_copy(b).wait()

    def coeff_rows(t):
        return coeff_v[pl.ds(pl.multiple_of(lam[t] * BT, BT), BT), :]

    def one_tile(r):
        start, many = first[r], count[r]
        one = order[start]
        two = order[start + jnp.where(many > 1, 1, 0)]
        left = jnp.concatenate(
            [ints_v[one].reshape(fitting * BT, BT), ints_v[two].reshape(fitting * BT, BT)], axis=1
        )
        rows = coeff_rows(two)
        right = jnp.concatenate(
            [coeff_rows(one), jnp.where(many > 1, rows, jnp.zeros_like(rows))], axis=0
        )
        value = jnp.dot(left, right, preferred_element_type=jnp.float32)
        for p in range(fitting):
            half[r, :, pl.ds(p * OBLK * OCC, OBLK * OCC)] = value[p * BT : (p + 1) * BT].astype(half.dtype)

    def crowded_tile(r):
        acc[...] = jnp.zeros_like(acc)

        def add(s, carry):
            t = order[s]
            acc[...] += jnp.dot(
                ints_v[t].reshape(fitting * BT, BT), coeff_rows(t), preferred_element_type=jnp.float32
            )
            return carry

        lax.fori_loop(first[r], first[r] + count[r], add, 0)
        for p in range(fitting):
            half[r, :, pl.ds(p * OBLK * OCC, OBLK * OCC)] = acc[pl.ds(p * BT, BT), :].astype(half.dtype)

    def tile_pair(k, carry):
        ranks = (2 * k, jnp.minimum(2 * k + 1, n_tiles - 1))

        def arrive(s, inner):
            ints_copy(order[s]).wait()
            return inner

        lax.fori_loop(first[ranks[0]], first[ranks[1]] + count[ranks[1]], arrive, 0)
        for r in ranks:
            one_tile(r)
        for r in ranks:

            @pl.when(count[r] > 2)
            def _():
                crowded_tile(r)

        return carry

    lax.fori_loop(0, (n_tiles + 1) >> 1, tile_pair, 0)

    keep_spare, send_spare = packed_place(my_core, me), packed_place(1 - my_core, me)

    def strip(v):
        left = half[0 : 2 * v + 2].reshape((2 * v + 2) * BT, half.shape[2])
        right = half[2 * v : 2 * v + 2].reshape(2 * BT, half.shape[2])
        value = lax.dot_general(left, right, (((1,), (1,)), ((), ())), preferred_element_type=jnp.float32)
        for j in (2 * v, 2 * v + 1):
            b, valid = info[j], j < n_tiles
            cols = slice((j - 2 * v) * BT, (j - 2 * v + 1) * BT)
            for i in range(j):
                a = info[i]
                mixed = ((a >> 1) != (b >> 1)) & (((a ^ b) & 1) == 1)
                row_rank, col_rank = jnp.where(mixed, j, i), jnp.where(mixed, i, j)
                core = (jnp.where(mixed, a, b) >> 1) & 1
                target = info[LIST * (1 + core) + row_rank] + info[3 * LIST + col_rank]
                keep_at = jnp.where(valid & (core == my_core), target, keep_spare)
                send_at = jnp.where(valid & (core != my_core), target, send_spare)
                for (start, end), keep, send in zip(COLOURS, keeps, sends):
                    block = value[i * BT + start : i * BT + end, cols]
                    keep[keep_at, 0 : end - start, :] = block
                    send[send_at, 0 : end - start, :] = block
            diag[jnp.where(valid, b, tiles)] = value[j * BT : (j + 1) * BT, cols]

    for v in range(tiles // 2):
        pl.when(2 * v < n_tiles)(functools.partial(strip, v))

    at_row = lax.broadcasted_iota(jnp.int32, (BT, BT), 0)
    at_col = lax.broadcasted_iota(jnp.int32, (BT, BT), 1)
    for pair in range(tiles // 2):
        even, odd = diag[2 * pair], diag[2 * pair + 1]
        packed = jnp.where(at_row <= at_col, even, odd)
        line = jnp.sum(jnp.where(at_row == at_col, odd, 0.0), axis=0, keepdims=True)
        packed = jnp.concatenate([packed, jnp.broadcast_to(line, (EXTRA, BT))], axis=0)
        target = packed_place(pair, me)
        for ours, refs in ((True, keeps), (False, sends)):

            @pl.when((my_core == pair & 1) == ours)
            def _():
                for (start, end), ref in zip(COLOURS, refs):
                    ref[target] = packed[start : start + ref.shape[1]]


def held(array, space):
    return pltpu.with_memory_space_constraint(array, space)


def partial_sums(ints, tile_mu, tile_lam, tile_live, coefficients, occ_ids):
    slots, fitting = ints.shape[0], ints.shape[1]
    tiles = coefficients.shape[0] // BT
    hbm = pl.BlockSpec(memory_space=pltpu.HBM)
    vmem = pl.BlockSpec(memory_space=pltpu.VMEM)
    shares = [
        pltpu.VMEM((SHARES, end - start + (EXTRA if end == BT else 0), BT), jnp.float32)
        for start, end in COLOURS
    ]
    listed = pltpu.SMEM((LIST,), jnp.int32)
    out = pl.pallas_call(
        partial_kernel,
        out_shape=shares + shares,
        in_specs=[hbm] * 6,
        out_specs=[vmem] * (2 * PARTS),
        scratch_shapes=[
            pltpu.VMEM(ints.shape, ints.dtype),
            pltpu.VMEM((coefficients.shape[0], OBLK * OCC), coefficients.dtype),
            pltpu.VMEM((fitting * BT, OBLK * OCC), jnp.float32),
            pltpu.VMEM((tiles, BT, fitting * OBLK * OCC), jnp.bfloat16),
            pltpu.VMEM((tiles + 1, BT, BT), jnp.float32),
            pltpu.SMEM((4 * LIST,), jnp.int32),
            pltpu.SMEM(tile_mu.shape, jnp.int32),
            pltpu.SMEM(tile_lam.shape, jnp.int32),
            pltpu.SMEM(tile_live.shape, jnp.int32),
            pltpu.SMEM(occ_ids.shape, jnp.int32),
            listed,
            listed,
            listed,
            listed,
            pltpu.SemaphoreType.DMA((slots,)),
            pltpu.SemaphoreType.DMA((OBLK,)),
            pltpu.SemaphoreType.DMA((4,)),
        ],
        compiler_params=pltpu.CompilerParams(vmem_limit_bytes=KERNEL_VMEM),
        cost_estimate=pl.CostEstimate(flops=8 * 10**9, bytes_accessed=5 * 2**20, transcendentals=0),
        name="partial_sums",
    )(*[held(v, pltpu.HBM) for v in (tile_mu, tile_lam, tile_live, occ_ids, ints, coefficients)])
    return out[:PARTS], out[PARTS:]


def finish_kernel(mine, theirs, out, *, scale):
    fit, pair = lax.axis_index("fit"), lax.axis_index("pair")
    high, odd = pair >> 1, pair & 1
    own = lambda: mine[0:BT, :] * scale
    other = lambda: theirs[...] * scale

    @pl.when(high < fit)
    def _():
        for number in range(2):

            @pl.when(odd == number)
            def _():
                out[:, pl.ds(number * BT, BT)] = own()
                out[:, pl.ds((1 - number) * BT, BT)] = other()

    @pl.when(high > fit)
    def _():
        for number in range(2):

            @pl.when(odd == number)
            def _():
                out[:, pl.ds((1 - number) * BT, BT)] = own().T
                out[:, pl.ds(number * BT, BT)] = other().T

    @pl.when(high == fit)
    def _():
        rows = lax.broadcasted_iota(jnp.int32, (BT, BT), 0)
        cols = lax.broadcasted_iota(jnp.int32, (BT, BT), 1)

        @pl.when(odd == 0)
        def _():
            packed = other()
            out[:, 0:BT] = jnp.where(rows <= cols, packed, packed.T)
            out[:, BT:] = own()

        @pl.when(odd == 1)
        def _():
            line = mine[BT : BT + 1, :] * scale
            filled = jnp.where(rows == cols, line, own())
            out[:, 0:BT] = other().T
            out[:, BT:] = jnp.where(rows >= cols, filled, filled.T)


def on_device(ints, tile_mu, tile_lam, tile_live, coefficients, occ_ids):
    count = lax.axis_size("fit") * lax.axis_size("pair")
    scale = 1.0 / math.sqrt(count * ints.shape[1] * OCC * OBLK)

    def swap(array, pairs):
        return lax.ppermute(array, AXES, pairs)

    def after(array, *others):
        return lax.optimization_barrier((array, *others))[0]

    first_bits = (2, 2, 2, NDEV // 16)
    keeps, sends = partial_sums(ints, tile_mu, tile_lam, tile_live, coefficients, occ_ids)
    keeps = [v.reshape(first_bits + v.shape[1:]) for v in keeps]
    cames = [swap(v, core_pairs()).reshape(first_bits + v.shape[1:]) for v in sends]
    tie = ()
    for step in range(3):
        for number in range(PARTS):
            axis = (number + step) % 3
            theirs = after(cames[number], *tie)
            at = lambda v, bit: lax.index_in_dim(v, bit, axis, keepdims=True)
            out_going = at(keeps[number], 1) + at(theirs, 1)
            keeps[number] = at(keeps[number], 0) + at(theirs, 0)
            cames[number] = swap(out_going, axis_pairs((axis,), False))
            tie = (out_going,)
    merged = []
    for mine, theirs in zip(keeps, cames):
        mine = (mine + after(theirs, *tie)).reshape((4, 2) + mine.shape[-2:])
        merged.append(mine)
        tie = (mine,)
    mine = jnp.concatenate(merged, axis=2)

    came = [swap(mine[b], axis_pairs(PARTNERS[b], True)) for b in (3, 2, 1)]
    mine = mine[0] + came[0] + came[1] + came[2]
    own = mine[0] + swap(mine[1], axis_pairs((2,), True))
    other = swap(own[0:BT], [(i, mirror(i)) for i in range(NDEV)])
    return pl.pallas_call(
        functools.partial(finish_kernel, scale=scale),
        out_shape=jax.ShapeDtypeStruct((BT, 2 * BT), jnp.float32),
        name="finish",
    )(held(own, pltpu.VMEM), held(other, pltpu.VMEM))


def solution(mesh):
    return jax.shard_map(
        on_device,
        mesh=mesh,
        in_specs=(
            P(("fit", "pair"), None, None, None),
            P(("fit", "pair")),
            P(("fit", "pair")),
            P(("fit", "pair")),
            P(),
            P(),
        ),
        out_specs=P("pair", "fit"),
        check_vma=False,
    )
```

time: 250 us -> 70.8 us (0.28); the launches traced: 247 us -> 70.6 us
  waiting for transfers between devices: 144 us -> 31.5 us
  matrix products: 59.4 us -> 0 us
  local copies, waits for them, and re-layouts: 27.6 us -> 0.22 us
  starting transfers between devices: 0.04 us -> 23.7 us
  between operations: 14.7 us -> 0.27 us
  Pallas kernels: 0 us -> 13.7 us
    reduce_scatter x2 -> x0, waiting for transfers between devices: 144 us -> none  [the longest x1 113 us: on_device(): lax.psum_scatter(summed * k_scale, 'pair', scatter_dimension=0, tiled=True)]
    dot_general x6 -> x0, matrix products: 59.4 us -> none  [the longest x2 28.7 us: on_device(): jnp.einsum('pmi,pni->mn', half_block, half_block, preferred_element_type=...]
    ppermute x0 -> x25, waiting for transfers between devices: none -> 31.5 us  [swap(): return lax.ppermute(array, AXES, pairs)]
    ppermute x0 -> x25, starting transfers between devices: none -> 23.7 us  [swap(): return lax.ppermute(array, AXES, pairs)]
    dot_general x2 -> x0, local copies, waits for them, and re-layouts: 18.4 us -> none  [half_transform(): jnp.einsum('tpml,tli->tpmi', ints, lam_rows, preferred_element_type=jnp.f...]
    pallas_call x0 -> x2, Pallas kernels: none -> 13.7 us  [the longest x1 13.1 us: partial_sums(): pl.pallas_call(partial_kernel, out_shape=shares + shares, in_specs=[hbm]...]
    convert_element_type x2 -> x0, local copies, waits for them, and re-layouts: 4.27 us -> none  [half_transform(): return buffer.astype(jnp.bfloat16).reshape(fitting, basis_count, OCC)]
  transfers between devices with their start and end apart: 2 -> 25, of which waited for: 2 -> 19; matrix products, arithmetic and copies ran while one was open for 0% -> 2% of each run, Pallas kernels for 0% -> 0%
where the time goes in v1:
time: 70.8 us; the launch traced here: 70.6 us
  waiting for transfers between devices  31.5 us (44%)
  starting transfers between devices  23.7 us (33%)
  Pallas kernels  13.7 us (19%)
  other arithmetic  1.24 us (2%)
    ppermute x25, waiting for transfers between devices, swap(): return lax.ppermute(array, AXES, pairs)  31.5 us
    ppermute x25, starting transfers between devices, swap(): return lax.ppermute(array, AXES, pairs)  23.7 us
    pallas_call x1, Pallas kernels, partial_sums(): pl.pallas_call(partial_kernel, out_shape=shares + shares, in_specs=[hbm]...  13.1 us
  transfers between devices with their start and end apart: 25, of which 19 were waited for; matrix products, arithmetic and copies ran while one was open for 2% of the time, Pallas kernels for 0%

profile of v1, /device:TPU:6, one launch (start us, length us, event | category | flops | bytes accessed | tf_op | source)
XLA Modules:
  0.0 70.6 jit_solution(14394604736063954263)
XLA Ops:
  0.0 13.1 %partial_sums.1 = (f32[64,24,128]{2,1,0:T(8,128)S(1)}, f32[64,24,128]{2,1,0:T(8,128)S(1)}, f32[64,24,128]{2,1,0:T(8,128)S(1)}, f32[64,32,128]{2,1,0:T(8,128)S(1)...) custom-call(s32[16]{0:T(128)} %mu_hbm.1, ...), custom_call_target="tpu_custom_call" | custom-call | flops 8000000000 | bytes 5242880 | tf_op jit(solution)/shard_map/partial_sums/pallas_call | solution.py:264
  13.1 0.1 collective-permute-start
  13.2 0.5 collective-permute-start.4
  13.7 0.1 collective-permute-start.5
  13.8 0.4 collective-permute-start.2
  14.2 0.1 collective-permute-start.3
  14.4 1.0 %collective-permute-done = f32[64,24,128]{2,1,0:T(8,128)S(1)} collective-permute-done((f32[64,24,128]{2,1,0:T(8,128)S(1)}, f32[64,24,128]{2,1,0:T(8,128)S(1)}, u32[]{:S(2)}, u32[]{:S(2)}) %collective-permute-start) | collective-permute-done | bytes 786464 | tf_op jit(solution)/shard_map/ppermute | solution.py:343
  15.5 0.1 collective-permute-start.1
  15.6 2.1 %collective-permute-done.5 = f32[64,24,128]{2,1,0:T(8,128)S(1)} collective-permute-done((f32[64,24,128]{2,1,0:T(8,128)S(1)}, f32[64,24,128]{2,1,0:T(8,128)S(1)}, u32[]{:S(2)}, u32[]{:S(2)}) %collective-permute-start.5) | collective-permute-done | bytes 786464 | tf_op jit(solution)/shard_map/ppermute | solution.py:343
  17.8 0.1 collective-permute-start.10
  17.9 0.1 slice_add_fusion.5
  18.0 1.1 %collective-permute-start.9 = (f32[2,2,1,8,24,128]{5,4,3,2,1,0:T(8,128)S(1)}, f32[2,2,1,8,24,128]{5,4,3,2,1,0:T(8,128)S(1)}, u32[]{:S(2)}, u32[]{:S(2)}) collective-permute-start(f32[2,2,1,8,24,128]{5,4,3,2,1,0:T(8,128)S(1)} %get-tuple-element.68), channel_id=1, source_target_pairs={{0,1},{1,0},{2,3},{3,2},{4,5},{5,4},{6,7},{7,6},{8,9},{9,8},{10,11... | collective-permute-start | bytes 1179656 | tf_op jit(solution)/shard_map/ppermute | solution.py:343
  19.1 1.6 %collective-permute-done.3 = f32[64,32,128]{2,1,0:T(8,128)S(1)} collective-permute-done((f32[64,32,128]{2,1,0:T(8,128)S(1)}, f32[64,32,128]{2,1,0:T(8,128)S(1)}, u32[]{:S(2)}, u32[]{:S(2)}) %collective-permute-start.3) | collective-permute-done | bytes 1048608 | tf_op jit(solution)/shard_map/ppermute | solution.py:343
  20.7 0.3 slice_add_fusion.2
  21.0 0.1 collective-permute-start.8
  21.1 0.2 slice_add_fusion
  21.3 1.2 %collective-permute-start.7 = (f32[2,1,2,8,32,128]{5,4,3,2,1,0:T(8,128)S(1)}, f32[2,1,2,8,32,128]{5,4,3,2,1,0:T(8,128)S(1)}, u32[]{:S(2)}, u32[]{:S(2)}) collective-permute-start(f32[2,1,2,8,32,128]{5,4,3,2,1,0:T(8,128)S(1)} %get-tuple-element.64), channel_id=1, source_target_pairs={{0,4},{1,5},{2,6},{3,7},{4,0},{5,1},{6,2},{7,3},{8,12},{9,13},{10,... | collective-permute-start | bytes 1572872 | tf_op jit(solution)/shard_map/ppermute | solution.py:343
  22.5 0.9 %collective-permute-done.1 = f32[1,2,2,8,24,128]{5,4,3,2,1,0:T(8,128)S(1)} collective-permute-done((f32[1,2,2,8,24,128]{5,4,3,2,1,0:T(8,128)S(1)}, f32[1,2,2,8,24,128]{5,4,3,2,1,0:T(8,128)S(1)}, u32[]{:S(2)}, u32[]{:S(2)}) %collective-permute-start.1) | collective-permute-done | bytes 393248 | tf_op jit(solution)/shard_map/ppermute | solution.py:343
  23.4 0.1 collective-permute-start.6
  23.5 2.1 %collective-permute-done.10 = f32[2,1,2,8,24,128]{5,4,3,2,1,0:T(8,128)S(1)} collective-permute-done((f32[2,1,2,8,24,128]{5,4,3,2,1,0:T(8,128)S(1)}, f32[2,1,2,8,24,128]{5,4,3,2,1,0:T(8,128)S(1)}, u32[]{:S(2)}, u32[]{:S(2)}) %collective-permute-start.10) | collective-permute-done | bytes 393248 | tf_op jit(solution)/shard_map/ppermute | solution.py:343
  25.7 0.1 collective-permute-start.15
  25.9 1.2 %collective-permute-start.14 = (f32[1,2,1,8,24,128]{5,4,3,2,1,0:T(8,128)S(1)}, f32[1,2,1,8,24,128]{5,4,3,2,1,0:T(8,128)S(1)}, u32[]{:S(2)}, u32[]{:S(2)}) collective-permute-start(f32[1,2,1,8,24,128]{5,4,3,2,1,0:T(8,128)S(1)} %get-tuple-element.80), channel_id=1, source_target_pairs={{0,32},{1,33},{2,34},{3,35},{4,36},{5,37},{6,38},{7,39},{8,40},{9,... | collective-permute-start | bytes 589832 | tf_op jit(solution)/shard_map/ppermute | solution.py:343
  27.0 3.2 %collective-permute-done.8 = f32[1,2,2,8,32,128]{5,4,3,2,1,0:T(8,128)S(1)} collective-permute-done((f32[1,2,2,8,32,128]{5,4,3,2,1,0:T(8,128)S(1)}, f32[1,2,2,8,32,128]{5,4,3,2,1,0:T(8,128)S(1)}, u32[]{:S(2)}, u32[]{:S(2)}) %collective-permute-start.8) | collective-permute-done | bytes 524320 | tf_op jit(solution)/shard_map/ppermute | solution.py:343
  30.3 0.1 collective-permute-start.13
  30.4 0.9 %collective-permute-done.7 = f32[2,1,2,8,32,128]{5,4,3,2,1,0:T(8,128)S(1)} collective-permute-done((f32[2,1,2,8,32,128]{5,4,3,2,1,0:T(8,128)S(1)}, f32[2,1,2,8,32,128]{5,4,3,2,1,0:T(8,128)S(1)}, u32[]{:S(2)}, u32[]{:S(2)}) %collective-permute-start.7) | collective-permute-done | bytes 524320 | tf_op jit(solution)/shard_map/ppermute | solution.py:343
  31.3 0.6 collective-permute-start.12
  31.9 1.4 %collective-permute-done.6 = f32[1,1,2,8,24,128]{5,4,3,2,1,0:T(8,128)S(1)} collective-permute-done((f32[1,1,2,8,24,128]{5,4,3,2,1,0:T(8,128)S(1)}, f32[1,1,2,8,24,128]{5,4,3,2,1,0:T(8,128)S(1)}, u32[]{:S(2)}, u32[]{:S(2)}) %collective-permute-start.6) | collective-permute-done | bytes 196640 | tf_op jit(solution)/shard_map/ppermute | solution.py:343
  33.4 0.2 collective-permute-start.11
  33.6 1.4 %collective-permute-start.16 = (f32[1,1,1,8,24,128]{5,4,3,2,1,0:T(8,128)S(1)}, f32[1,1,1,8,24,128]{5,4,3,2,1,0:T(8,128)S(1)}, u32[]{:S(2)}, u32[]{:S(2)}) collective-permute-start(f32[1,1,1,8,24,128]{5,4,3,2,1,0:T(8,128)S(1)} %slice_add_fusion.26), channel_id=1, source_target_pairs={{0,32},{1,33},{2,34},{3,35},{4,36},{5,37},{6,38},{7,39},{8,40},{9,... | collective-permute-start | bytes 294920 | tf_op jit(solution)/shard_map/ppermute | solution.py:343
  34.9 1.4 %collective-permute-start.17 = (f32[1,1,1,8,24,128]{5,4,3,2,1,0:T(8,128)S(1)}, f32[1,1,1,8,24,128]{5,4,3,2,1,0:T(8,128)S(1)}, u32[]{:S(2)}, u32[]{:S(2)}) collective-permute-start(f32[1,1,1,8,24,128]{5,4,3,2,1,0:T(8,128)S(1)} %slice_add_fusion.27), channel_id=1, source_target_pairs={{0,4},{1,5},{2,6},{3,7},{4,0},{5,1},{6,2},{7,3},{8,12},{9,13},{10,... | collective-permute-start | bytes 294920 | tf_op jit(solution)/shard_map/ppermute | solution.py:343
  36.3 0.4 collective-permute-done.13
  36.8 0.3 collective-permute-start.18
  37.1 0.7 collective-permute-done.12
  37.8 1.4 %collective-permute-start.19 = (f32[1,1,1,8,32,128]{5,4,3,2,1,0:T(8,128)S(1)}, f32[1,1,1,8,32,128]{5,4,3,2,1,0:T(8,128)S(1)}, u32[]{:S(2)}, u32[]{:S(2)}) collective-permute-start(f32[1,1,1,8,32,128]{5,4,3,2,1,0:T(8,128)S(1)} %slice_add_fusion.23), channel_id=1, source_target_pairs={{0,32},{1,33},{2,34},{3,35},{4,36},{5,37},{6,38},{7,39},{8,40},{9,... | collective-permute-start | bytes 393224 | tf_op jit(solution)/shard_map/ppermute | solution.py:343
  39.3 0.4 collective-permute-done.17
  39.7 2.1 %collective-permute-done.18 = f32[1,1,1,8,32,128]{5,4,3,2,1,0:T(8,128)S(1)} collective-permute-done((f32[1,1,1,8,32,128]{5,4,3,2,1,0:T(8,128)S(1)}, f32[1,1,1,8,32,128]{5,4,3,2,1,0:T(8,128)S(1)}, u32[]{:S(2)}, u32[]{:S(2)}) %collective-permute-start.18) | collective-permute-done | bytes 131104 | tf_op jit(solution)/shard_map/ppermute | solution.py:343
  41.9 1.0 %collective-permute-done.19 = f32[1,1,1,8,32,128]{5,4,3,2,1,0:T(8,128)S(1)} collective-permute-done((f32[1,1,1,8,32,128]{5,4,3,2,1,0:T(8,128)S(1)}, f32[1,1,1,8,32,128]{5,4,3,2,1,0:T(8,128)S(1)}, u32[]{:S(2)}, u32[]{:S(2)}) %collective-permute-start.19) | collective-permute-done | bytes 131104 | tf_op jit(solution)/shard_map/ppermute | solution.py:343
  43.0 2.5 %collective-permute-start.20 = (f32[2,136,128]{2,1,0:T(8,128)S(1)}, f32[2,136,128]{2,1,0:T(8,128)S(1)}, u32[]{:S(2)}, u32[]{:S(2)}) collective-permute-start(f32[2,136,128]{2,1,0:T(8,128)S(1)} %get-tuple-element.87), channel_id=1, source_target_pairs={{0,108},{1,109},{2,110},{3,111},{4,104},{5,105},{6,106},{7,107},{8... | collective-permute-start | bytes 417800 | tf_op jit(solution)/shard_map/ppermute | solution.py:343
  45.5 1.9 %collective-permute-start.22 = (f32[2,136,128]{2,1,0:T(8,128)S(1)}, f32[2,136,128]{2,1,0:T(8,128)S(1)}, u32[]{:S(2)}, u32[]{:S(2)}) collective-permute-start(f32[2,136,128]{2,1,0:T(8,128)S(1)} %get-tuple-element.88), channel_id=1, source_target_pairs={{0,12},{1,13},{2,14},{3,15},{4,8},{5,9},{6,10},{7,11},{8,4},{9,5},... | collective-permute-start | bytes 417800 | tf_op jit(solution)/shard_map/ppermute | solution.py:343
  47.4 2.6 %collective-permute-start.21 = (f32[2,136,128]{2,1,0:T(8,128)S(1)}, f32[2,136,128]{2,1,0:T(8,128)S(1)}, u32[]{:S(2)}, u32[]{:S(2)}) collective-permute-start(f32[2,136,128]{2,1,0:T(8,128)S(1)} %get-tuple-element.89), channel_id=1, source_target_pairs={{0,96},{1,97},{2,98},{3,99},{4,100},{5,101},{6,102},{7,103},{8,104... | collective-permute-start | bytes 417800 | tf_op jit(solution)/shard_map/ppermute | solution.py:343
  50.0 1.5 %collective-permute-done.20 = f32[2,136,128]{2,1,0:T(8,128)S(1)} collective-permute-done((f32[2,136,128]{2,1,0:T(8,128)S(1)}, f32[2,136,128]{2,1,0:T(8,128)S(1)}, u32[]{:S(2)}, u32[]{:S(2)}) %collective-permute-start.20) | collective-permute-done | bytes 139296 | tf_op jit(solution)/shard_map/ppermute | solution.py:343
  51.5 1.4 %collective-permute-done.22 = f32[2,136,128]{2,1,0:T(8,128)S(1)} collective-permute-done((f32[2,136,128]{2,1,0:T(8,128)S(1)}, f32[2,136,128]{2,1,0:T(8,128)S(1)}, u32[]{:S(2)}, u32[]{:S(2)}) %collective-permute-start.22) | collective-permute-done | bytes 139296 | tf_op jit(solution)/shard_map/ppermute | solution.py:343
  52.9 1.6 %collective-permute-done.21 = f32[2,136,128]{2,1,0:T(8,128)S(1)} collective-permute-done((f32[2,136,128]{2,1,0:T(8,128)S(1)}, f32[2,136,128]{2,1,0:T(8,128)S(1)}, u32[]{:S(2)}, u32[]{:S(2)}) %collective-permute-start.21) | collective-permute-done | bytes 139296 | tf_op jit(solution)/shard_map/ppermute | solution.py:343
  54.6 1.8 %collective-permute-start.23 = (f32[136,128]{1,0:T(8,128)S(1)}, f32[136,128]{1,0:T(8,128)S(1)}, u32[]{:S(2)}, u32[]{:S(2)}) collective-permute-start(f32[136,128]{1,0:T(8,128)S(1)} %slice_bitcast_fusion.4), channel_id=1, source_target_pairs={{0,3},{1,2},{2,1},{3,0},{4,7},{5,6},{6,5},{7,4},{8,11},{9,10},{10,... | collective-permute-start | bytes 208904 | tf_op jit(solution)/shard_map/ppermute | solution.py:343
  56.3 3.8 %collective-permute-done.23 = f32[136,128]{1,0:T(8,128)S(1)} collective-permute-done((f32[136,128]{1,0:T(8,128)S(1)}, f32[136,128]{1,0:T(8,128)S(1)}, u32[]{:S(2)}, u32[]{:S(2)}) %collective-permute-start.23) | collective-permute-done | bytes 69664 | tf_op jit(solution)/shard_map/ppermute | solution.py:343
  60.2 4.5 %collective-permute-start.24 = (f32[128,128]{1,0:T(8,128)S(1)}, f32[128,128]{1,0:T(8,128)S(1)}, u32[]{:S(2)}, u32[]{:S(2)}) collective-permute-start(f32[128,128]{1,0:T(8,128)S(1)} %slice.318), channel_id=1, source_target_pairs={{0,1},{1,0},{2,17},{3,16},{4,33},{5,32},{6,49},{7,48},{8,65},{9,64... | collective-permute-start | bytes 196616 | tf_op jit(solution)/shard_map/ppermute | solution.py:343
  64.7 5.2 %collective-permute-done.24.theirs = f32[128,128]{1,0:T(8,128)S(1)} collective-permute-done((f32[128,128]{1,0:T(8,128)S(1)}, f32[128,128]{1,0:T(8,128)S(1)}, u32[]{:S(2)}, u32[]{:S(2)}) %collective-permute-start.24) | collective-permute-done | bytes 65568 | tf_op jit(solution)/shard_map/ppermute | solution.py:343
  69.9 0.7 finish.1
  (36 shorter events, 1.0 us)
Async XLA Ops:
  13.1 2.4 %collective-permute-start = (f32[64,24,128]{2,1,0:T(8,128)S(1)}, f32[64,24,128]{2,1,0:T(8,128)S(1)}, u32[]{:S(2)}, u32[]{:S(2)}) collective-permute-start(f32[64,24,128]{2,1,0:T(8,128)S(1)} %get-tuple-element.35), channel_id=1, source_target_pairs={{0,16},{1,17},{2,18},{3,19},{4,20},{5,21},{6,22},{7,23},{8,24},{9,... | collective-permute-start | bytes 2359304 | tf_op jit(solution)/shard_map/ppermute | solution.py:343
  13.2 4.7 %collective-permute-start.4 = (f32[64,24,128]{2,1,0:T(8,128)S(1)}, f32[64,24,128]{2,1,0:T(8,128)S(1)}, u32[]{:S(2)}, u32[]{:S(2)}) collective-permute-start(f32[64,24,128]{2,1,0:T(8,128)S(1)} %get-tuple-element.41), channel_id=1, source_target_pairs={{0,16},{1,17},{2,18},{3,19},{4,20},{5,21},{6,22},{7,23},{8,24},{9,... | collective-permute-start | bytes 2359304 | tf_op jit(solution)/shard_map/ppermute | solution.py:343
  13.7 4.0 %collective-permute-start.5 = (f32[64,24,128]{2,1,0:T(8,128)S(1)}, f32[64,24,128]{2,1,0:T(8,128)S(1)}, u32[]{:S(2)}, u32[]{:S(2)}) collective-permute-start(f32[64,24,128]{2,1,0:T(8,128)S(1)} %get-tuple-element.43), channel_id=1, source_target_pairs={{0,16},{1,17},{2,18},{3,19},{4,20},{5,21},{6,22},{7,23},{8,24},{9,... | collective-permute-start | bytes 2359304 | tf_op jit(solution)/shard_map/ppermute | solution.py:343
  13.8 7.3 %collective-permute-start.2 = (f32[64,32,128]{2,1,0:T(8,128)S(1)}, f32[64,32,128]{2,1,0:T(8,128)S(1)}, u32[]{:S(2)}, u32[]{:S(2)}) collective-permute-start(f32[64,32,128]{2,1,0:T(8,128)S(1)} %get-tuple-element.37), channel_id=1, source_target_pairs={{0,16},{1,17},{2,18},{3,19},{4,20},{5,21},{6,22},{7,23},{8,24},{9,... | collective-permute-start | bytes 3145736 | tf_op jit(solution)/shard_map/ppermute | solution.py:343
  14.2 6.5 %collective-permute-start.3 = (f32[64,32,128]{2,1,0:T(8,128)S(1)}, f32[64,32,128]{2,1,0:T(8,128)S(1)}, u32[]{:S(2)}, u32[]{:S(2)}) collective-permute-start(f32[64,32,128]{2,1,0:T(8,128)S(1)} %get-tuple-element.39), channel_id=1, source_target_pairs={{0,16},{1,17},{2,18},{3,19},{4,20},{5,21},{6,22},{7,23},{8,24},{9,... | collective-permute-start | bytes 3145736 | tf_op jit(solution)/shard_map/ppermute | solution.py:343
  15.5 7.9 %collective-permute-start.1 = (f32[1,2,2,8,24,128]{5,4,3,2,1,0:T(8,128)S(1)}, f32[1,2,2,8,24,128]{5,4,3,2,1,0:T(8,128)S(1)}, u32[]{:S(2)}, u32[]{:S(2)}) collective-permute-start(f32[1,2,2,8,24,128]{5,4,3,2,1,0:T(8,128)S(1)} %get-tuple-element.83), channel_id=1, source_target_pairs={{0,32},{1,33},{2,34},{3,35},{4,36},{5,37},{6,38},{7,39},{8,40},{9,... | collective-permute-start | bytes 1179656 | tf_op jit(solution)/shard_map/ppermute | solution.py:343
  17.8 7.9 %collective-permute-start.10 = (f32[2,1,2,8,24,128]{5,4,3,2,1,0:T(8,128)S(1)}, f32[2,1,2,8,24,128]{5,4,3,2,1,0:T(8,128)S(1)}, u32[]{:S(2)}, u32[]{:S(2)}) collective-permute-start(f32[2,1,2,8,24,128]{5,4,3,2,1,0:T(8,128)S(1)} %get-tuple-element.66), channel_id=1, source_target_pairs={{0,4},{1,5},{2,6},{3,7},{4,0},{5,1},{6,2},{7,3},{8,12},{9,13},{10,... | collective-permute-start | bytes 1179656 | tf_op jit(solution)/shard_map/ppermute | solution.py:343
  18.0 7.9 %collective-permute-start.9 = (f32[2,2,1,8,24,128]{5,4,3,2,1,0:T(8,128)S(1)}, f32[2,2,1,8,24,128]{5,4,3,2,1,0:T(8,128)S(1)}, u32[]{:S(2)}, u32[]{:S(2)}) collective-permute-start(f32[2,2,1,8,24,128]{5,4,3,2,1,0:T(8,128)S(1)} %get-tuple-element.68), channel_id=1, source_target_pairs={{0,1},{1,0},{2,3},{3,2},{4,5},{5,4},{6,7},{7,6},{8,9},{9,8},{10,11... | collective-permute-start | bytes 1179656 | tf_op jit(solution)/shard_map/ppermute | solution.py:343
  21.0 9.3 %collective-permute-start.8 = (f32[1,2,2,8,32,128]{5,4,3,2,1,0:T(8,128)S(1)}, f32[1,2,2,8,32,128]{5,4,3,2,1,0:T(8,128)S(1)}, u32[]{:S(2)}, u32[]{:S(2)}) collective-permute-start(f32[1,2,2,8,32,128]{5,4,3,2,1,0:T(8,128)S(1)} %get-tuple-element.74), channel_id=1, source_target_pairs={{0,32},{1,33},{2,34},{3,35},{4,36},{5,37},{6,38},{7,39},{8,40},{9,... | collective-permute-start | bytes 1572872 | tf_op jit(solution)/shard_map/ppermute | solution.py:343
  21.3 10.0 %collective-permute-start.7 = (f32[2,1,2,8,32,128]{5,4,3,2,1,0:T(8,128)S(1)}, f32[2,1,2,8,32,128]{5,4,3,2,1,0:T(8,128)S(1)}, u32[]{:S(2)}, u32[]{:S(2)}) collective-permute-start(f32[2,1,2,8,32,128]{5,4,3,2,1,0:T(8,128)S(1)} %get-tuple-element.64), channel_id=1, source_target_pairs={{0,4},{1,5},{2,6},{3,7},{4,0},{5,1},{6,2},{7,3},{8,12},{9,13},{10,... | collective-permute-start | bytes 1572872 | tf_op jit(solution)/shard_map/ppermute | solution.py:343
  23.4 9.9 %collective-permute-start.6 = (f32[1,1,2,8,24,128]{5,4,3,2,1,0:T(8,128)S(1)}, f32[1,1,2,8,24,128]{5,4,3,2,1,0:T(8,128)S(1)}, u32[]{:S(2)}, u32[]{:S(2)}) collective-permute-start(f32[1,1,2,8,24,128]{5,4,3,2,1,0:T(8,128)S(1)} %get-tuple-element.81), channel_id=1, source_target_pairs={{0,4},{1,5},{2,6},{3,7},{4,0},{5,1},{6,2},{7,3},{8,12},{9,13},{10,... | collective-permute-start | bytes 589832 | tf_op jit(solution)/shard_map/ppermute | solution.py:343
  25.7 7.9 %collective-permute-start.15 = (f32[2,1,1,8,24,128]{5,4,3,2,1,0:T(8,128)S(1)}, f32[2,1,1,8,24,128]{5,4,3,2,1,0:T(8,128)S(1)}, u32[]{:S(2)}, u32[]{:S(2)}) collective-permute-start(f32[2,1,1,8,24,128]{5,4,3,2,1,0:T(8,128)S(1)} %get-tuple-element.78), channel_id=1, source_target_pairs={{0,1},{1,0},{2,3},{3,2},{4,5},{5,4},{6,7},{7,6},{8,9},{9,8},{10,11... | collective-permute-start | bytes 589832 | tf_op jit(solution)/shard_map/ppermute | solution.py:343
  25.9 9.0 %collective-permute-start.14 = (f32[1,2,1,8,24,128]{5,4,3,2,1,0:T(8,128)S(1)}, f32[1,2,1,8,24,128]{5,4,3,2,1,0:T(8,128)S(1)}, u32[]{:S(2)}, u32[]{:S(2)}) collective-permute-start(f32[1,2,1,8,24,128]{5,4,3,2,1,0:T(8,128)S(1)} %get-tuple-element.80), channel_id=1, source_target_pairs={{0,32},{1,33},{2,34},{3,35},{4,36},{5,37},{6,38},{7,39},{8,40},{9,... | collective-permute-start | bytes 589832 | tf_op jit(solution)/shard_map/ppermute | solution.py:343
  30.3 6.5 %collective-permute-start.13 = (f32[1,1,2,8,32,128]{5,4,3,2,1,0:T(8,128)S(1)}, f32[1,1,2,8,32,128]{5,4,3,2,1,0:T(8,128)S(1)}, u32[]{:S(2)}, u32[]{:S(2)}) collective-permute-start(f32[1,1,2,8,32,128]{5,4,3,2,1,0:T(8,128)S(1)} %get-tuple-element.70), channel_id=1, source_target_pairs={{0,4},{1,5},{2,6},{3,7},{4,0},{5,1},{6,2},{7,3},{8,12},{9,13},{10,... | collective-permute-start | bytes 786440 | tf_op jit(solution)/shard_map/ppermute | solution.py:343
  31.3 6.5 %collective-permute-start.12 = (f32[2,1,1,8,32,128]{5,4,3,2,1,0:T(8,128)S(1)}, f32[2,1,1,8,32,128]{5,4,3,2,1,0:T(8,128)S(1)}, u32[]{:S(2)}, u32[]{:S(2)}) collective-permute-start(f32[2,1,1,8,32,128]{5,4,3,2,1,0:T(8,128)S(1)} %get-tuple-element.72), channel_id=1, source_target_pairs={{0,1},{1,0},{2,3},{3,2},{4,5},{5,4},{6,7},{7,6},{8,9},{9,8},{10,11... | collective-permute-start | bytes 786440 | tf_op jit(solution)/shard_map/ppermute | solution.py:343
  33.4 5.8 %collective-permute-start.11 = (f32[1,1,1,8,24,128]{5,4,3,2,1,0:T(8,128)S(1)}, f32[1,1,1,8,24,128]{5,4,3,2,1,0:T(8,128)S(1)}, u32[]{:S(2)}, u32[]{:S(2)}) collective-permute-start(f32[1,1,1,8,24,128]{5,4,3,2,1,0:T(8,128)S(1)} %slice_add_fusion.28), channel_id=1, source_target_pairs={{0,1},{1,0},{2,3},{3,2},{4,5},{5,4},{6,7},{7,6},{8,9},{9,8},{10,11... | collective-permute-start | bytes 294920 | tf_op jit(solution)/shard_map/ppermute | solution.py:343
  33.6 5.6 %collective-permute-start.16 = (f32[1,1,1,8,24,128]{5,4,3,2,1,0:T(8,128)S(1)}, f32[1,1,1,8,24,128]{5,4,3,2,1,0:T(8,128)S(1)}, u32[]{:S(2)}, u32[]{:S(2)}) collective-permute-start(f32[1,1,1,8,24,128]{5,4,3,2,1,0:T(8,128)S(1)} %slice_add_fusion.26), channel_id=1, source_target_pairs={{0,32},{1,33},{2,34},{3,35},{4,36},{5,37},{6,38},{7,39},{8,40},{9,... | collective-permute-start | bytes 294920 | tf_op jit(solution)/shard_map/ppermute | solution.py:343
  34.9 4.7 %collective-permute-start.17 = (f32[1,1,1,8,24,128]{5,4,3,2,1,0:T(8,128)S(1)}, f32[1,1,1,8,24,128]{5,4,3,2,1,0:T(8,128)S(1)}, u32[]{:S(2)}, u32[]{:S(2)}) collective-permute-start(f32[1,1,1,8,24,128]{5,4,3,2,1,0:T(8,128)S(1)} %slice_add_fusion.27), channel_id=1, source_target_pairs={{0,4},{1,5},{2,6},{3,7},{4,0},{5,1},{6,2},{7,3},{8,12},{9,13},{10,... | collective-permute-start | bytes 294920 | tf_op jit(solution)/shard_map/ppermute | solution.py:343
  36.8 5.0 %collective-permute-start.18 = (f32[1,1,1,8,32,128]{5,4,3,2,1,0:T(8,128)S(1)}, f32[1,1,1,8,32,128]{5,4,3,2,1,0:T(8,128)S(1)}, u32[]{:S(2)}, u32[]{:S(2)}) collective-permute-start(f32[1,1,1,8,32,128]{5,4,3,2,1,0:T(8,128)S(1)} %slice_add_fusion.22), channel_id=1, source_target_pairs={{0,1},{1,0},{2,3},{3,2},{4,5},{5,4},{6,7},{7,6},{8,9},{9,8},{10,11... | collective-permute-start | bytes 393224 | tf_op jit(solution)/shard_map/ppermute | solution.py:343
  37.8 5.0 %collective-permute-start.19 = (f32[1,1,1,8,32,128]{5,4,3,2,1,0:T(8,128)S(1)}, f32[1,1,1,8,32,128]{5,4,3,2,1,0:T(8,128)S(1)}, u32[]{:S(2)}, u32[]{:S(2)}) collective-permute-start(f32[1,1,1,8,32,128]{5,4,3,2,1,0:T(8,128)S(1)} %slice_add_fusion.23), channel_id=1, source_target_pairs={{0,32},{1,33},{2,34},{3,35},{4,36},{5,37},{6,38},{7,39},{8,40},{9,... | collective-permute-start | bytes 393224 | tf_op jit(solution)/shard_map/ppermute | solution.py:343
  43.0 8.6 %collective-permute-start.20 = (f32[2,136,128]{2,1,0:T(8,128)S(1)}, f32[2,136,128]{2,1,0:T(8,128)S(1)}, u32[]{:S(2)}, u32[]{:S(2)}) collective-permute-start(f32[2,136,128]{2,1,0:T(8,128)S(1)} %get-tuple-element.87), channel_id=1, source_target_pairs={{0,108},{1,109},{2,110},{3,111},{4,104},{5,105},{6,106},{7,107},{8... | collective-permute-start | bytes 417800 | tf_op jit(solution)/shard_map/ppermute | solution.py:343
  45.5 7.4 %collective-permute-start.22 = (f32[2,136,128]{2,1,0:T(8,128)S(1)}, f32[2,136,128]{2,1,0:T(8,128)S(1)}, u32[]{:S(2)}, u32[]{:S(2)}) collective-permute-start(f32[2,136,128]{2,1,0:T(8,128)S(1)} %get-tuple-element.88), channel_id=1, source_target_pairs={{0,12},{1,13},{2,14},{3,15},{4,8},{5,9},{6,10},{7,11},{8,4},{9,5},... | collective-permute-start | bytes 417800 | tf_op jit(solution)/shard_map/ppermute | solution.py:343
  47.4 7.1 %collective-permute-start.21 = (f32[2,136,128]{2,1,0:T(8,128)S(1)}, f32[2,136,128]{2,1,0:T(8,128)S(1)}, u32[]{:S(2)}, u32[]{:S(2)}) collective-permute-start(f32[2,136,128]{2,1,0:T(8,128)S(1)} %get-tuple-element.89), channel_id=1, source_target_pairs={{0,96},{1,97},{2,98},{3,99},{4,100},{5,101},{6,102},{7,103},{8,104... | collective-permute-start | bytes 417800 | tf_op jit(solution)/shard_map/ppermute | solution.py:343
  54.6 5.6 %collective-permute-start.23 = (f32[136,128]{1,0:T(8,128)S(1)}, f32[136,128]{1,0:T(8,128)S(1)}, u32[]{:S(2)}, u32[]{:S(2)}) collective-permute-start(f32[136,128]{1,0:T(8,128)S(1)} %slice_bitcast_fusion.4), channel_id=1, source_target_pairs={{0,3},{1,2},{2,1},{3,0},{4,7},{5,6},{6,5},{7,4},{8,11},{9,10},{10,... | collective-permute-start | bytes 208904 | tf_op jit(solution)/shard_map/ppermute | solution.py:343
  60.2 9.7 %collective-permute-start.24 = (f32[128,128]{1,0:T(8,128)S(1)}, f32[128,128]{1,0:T(8,128)S(1)}, u32[]{:S(2)}, u32[]{:S(2)}) collective-permute-start(f32[128,128]{1,0:T(8,128)S(1)} %slice.318), channel_id=1, source_target_pairs={{0,1},{1,0},{2,17},{3,16},{4,33},{5,32},{6,49},{7,48},{8,65},{9,64... | collective-permute-start | bytes 196616 | tf_op jit(solution)/shard_map/ppermute | solution.py:343

commit v2 on v1

--- a/solution.py
+++ b/solution.py
@@ -19,6 +19,8 @@
 PARTS = len(COLOURS)
 KERNEL_VMEM = 28 * 1024 * 1024
 LIST = 32
+UNROLL = 3
+STRIPS_ALWAYS = 4
 PARTNERS = ((), (1,), (0,), (0, 1))
 
 
@@ -148,7 +150,7 @@
         info[2 * LIST + r] = row_place(name, 1, my_z, my_y)
         info[3 * LIST + r] = col_place(name >> 1, my_x)
 
-    for ref in keeps + sends + (diag,):
+    for ref in (*keeps, *sends, diag):
         ref[...] = jnp.zeros_like(ref)
     for b in range(OBLK):
         coeff_copy(b).wait()
@@ -156,18 +158,17 @@
     def coeff_rows(t):
         return coeff_v[pl.ds(pl.multiple_of(lam[t] * BT, BT), BT), :]
 
-    def one_tile(r):
+    def one_tile(r, width):
         start, many = first[r], count[r]
-        one = order[start]
-        two = order[start + jnp.where(many > 1, 1, 0)]
-        left = jnp.concatenate(
-            [ints_v[one].reshape(fitting * BT, BT), ints_v[two].reshape(fitting * BT, BT)], axis=1
+        left, right = [], []
+        for i in range(width):
+            t = order[start + jnp.where(many > i, i, 0)]
+            rows = coeff_rows(t)
+            left.append(ints_v[t].reshape(fitting * BT, BT))
+            right.append(rows if i == 0 else jnp.where(many > i, rows, jnp.zeros_like(rows)))
+        value = jnp.dot(
+            jnp.concatenate(left, axis=1), jnp.concatenate(right, axis=0), preferred_element_type=jnp.float32
         )
-        rows = coeff_rows(two)
-        right = jnp.concatenate(
-            [coeff_rows(one), jnp.where(many > 1, rows, jnp.zeros_like(rows))], axis=0
-        )
-        value = jnp.dot(left, right, preferred_element_type=jnp.float32)
         for p in range(fitting):
             half[r, :, pl.ds(p * OBLK * OCC, OBLK * OCC)] = value[p * BT : (p + 1) * BT].astype(half.dtype)
 
@@ -185,25 +186,29 @@
         for p in range(fitting):
             half[r, :, pl.ds(p * OBLK * OCC, OBLK * OCC)] = acc[pl.ds(p * BT, BT), :].astype(half.dtype)
 
-    def tile_pair(k, carry):
-        ranks = (2 * k, jnp.minimum(2 * k + 1, n_tiles - 1))
+    def some_tiles(k, carry):
+        ranks = [jnp.minimum(UNROLL * k + i, n_tiles - 1) for i in range(UNROLL)]
 
         def arrive(s, inner):
             ints_copy(order[s]).wait()
             return inner
 
-        lax.fori_loop(first[ranks[0]], first[ranks[1]] + count[ranks[1]], arrive, 0)
+        lax.fori_loop(first[ranks[0]], first[ranks[-1]] + count[ranks[-1]], arrive, 0)
         for r in ranks:
-            one_tile(r)
+            one_tile(r, 2)
         for r in ranks:
 
-            @pl.when(count[r] > 2)
+            @pl.when((count[r] > 2) & (count[r] <= 4))
+            def _():
+                one_tile(r, 4)
+
+            @pl.when(count[r] > 4)
             def _():
                 crowded_tile(r)
 
         return carry
 
-    lax.fori_loop(0, (n_tiles + 1) >> 1, tile_pair, 0)
+    lax.fori_loop(0, lax.div(n_tiles + UNROLL - 1, UNROLL), some_tiles, 0)
 
     keep_spare, send_spare = packed_place(my_core, me), packed_place(1 - my_core, me)
 
@@ -229,7 +234,10 @@
             diag[jnp.where(valid, b, tiles)] = value[j * BT : (j + 1) * BT, cols]
 
     for v in range(tiles // 2):
-        pl.when(2 * v < n_tiles)(functools.partial(strip, v))
+        if v < STRIPS_ALWAYS:
+            strip(v)
+        else:
+            pl.when(2 * v < n_tiles)(functools.partial(strip, v))
 
     at_row = lax.broadcasted_iota(jnp.int32, (BT, BT), 0)
     at_col = lax.broadcasted_iota(jnp.int32, (BT, BT), 1)

time: 70.8 us -> 70.3 us (level)
  starting transfers between devices: 23.7 us -> 37.8 us
  waiting for transfers between devices: 31.5 us -> 19.8 us
  Pallas kernels: 13.7 us -> 10.2 us
    ppermute x25, starting transfers between devices: 23.7 us -> 37.8 us  [swap(): return lax.ppermute(array, AXES, pairs)]
    ppermute x25, waiting for transfers between devices: 31.5 us -> 19.8 us  [swap(): return lax.ppermute(array, AXES, pairs)]
    pallas_call x1, Pallas kernels: 13.1 us -> 9.51 us  [partial_sums(): pl.pallas_call(partial_kernel, out_shape=shares + shares, in_specs=[hbm]...]
  transfers between devices with their start and end apart: 25 -> 25, of which waited for: 19 -> 13; matrix products, arithmetic and copies ran while one was open for 2% -> 2% of each run, Pallas kernels for 0% -> 0%
where the time goes in v2:
time: 70.3 us; the launch traced here: 69.5 us
  starting transfers between devices  37.8 us (54%)
  waiting for transfers between devices  19.8 us (28%)
  Pallas kernels  10.2 us (15%)
  other arithmetic  1.23 us (2%)
    ppermute x25, starting transfers between devices, swap(): return lax.ppermute(array, AXES, pairs)  37.8 us
    ppermute x25, waiting for transfers between devices, swap(): return lax.ppermute(array, AXES, pairs)  19.8 us
    pallas_call x1, Pallas kernels, partial_sums(): pl.pallas_call(partial_kernel, out_shape=shares + shares, in_specs=[hbm]...  9.51 us
  transfers between devices with their start and end apart: 25, of which 13 were waited for; matrix products, arithmetic and copies ran while one was open for 2% of the time, Pallas kernels for 0%

profile of v2, /device:TPU:6, one launch (start us, length us, event | category | flops | bytes accessed | tf_op | source)
XLA Modules:
  0.0 69.5 jit_solution(1937412141255695634)
XLA Ops:
  0.0 9.5 %partial_sums.1 = (f32[64,24,128]{2,1,0:T(8,128)S(1)}, f32[64,24,128]{2,1,0:T(8,128)S(1)}, f32[64,24,128]{2,1,0:T(8,128)S(1)}, f32[64,32,128]{2,1,0:T(8,128)S(1)...) custom-call(s32[16]{0:T(128)} %mu_hbm.1, ...), custom_call_target="tpu_custom_call" | custom-call | flops 8000000000 | bytes 5242880 | tf_op jit(solution)/shard_map/partial_sums/pallas_call | solution.py:272
  9.5 0.1 collective-permute-start
  9.6 0.5 collective-permute-start.4
  10.1 0.1 collective-permute-start.5
  10.2 0.4 collective-permute-start.2
  10.6 0.1 collective-permute-start.3
  10.7 0.1 fusion.9
  10.8 1.0 %collective-permute-done = f32[64,24,128]{2,1,0:T(8,128)S(1)} collective-permute-done((f32[64,24,128]{2,1,0:T(8,128)S(1)}, f32[64,24,128]{2,1,0:T(8,128)S(1)}, u32[]{:S(2)}, u32[]{:S(2)}) %collective-permute-start) | collective-permute-done | bytes 786464 | tf_op jit(solution)/shard_map/ppermute | solution.py:351
  11.9 0.1 slice_add_fusion.8
  12.0 0.9 %collective-permute-start.1 = (f32[1,2,2,8,24,128]{5,4,3,2,1,0:T(8,128)S(1)}, f32[1,2,2,8,24,128]{5,4,3,2,1,0:T(8,128)S(1)}, u32[]{:S(2)}, u32[]{:S(2)}) collective-permute-start(f32[1,2,2,8,24,128]{5,4,3,2,1,0:T(8,128)S(1)} %get-tuple-element.83), channel_id=1, source_target_pairs={{0,32},{1,33},{2,34},{3,35},{4,36},{5,37},{6,38},{7,39},{8,40},{9,... | collective-permute-start | bytes 1179656 | tf_op jit(solution)/shard_map/ppermute | solution.py:351
  12.9 1.2 %collective-permute-done.5 = f32[64,24,128]{2,1,0:T(8,128)S(1)} collective-permute-done((f32[64,24,128]{2,1,0:T(8,128)S(1)}, f32[64,24,128]{2,1,0:T(8,128)S(1)}, u32[]{:S(2)}, u32[]{:S(2)}) %collective-permute-start.5) | collective-permute-done | bytes 786464 | tf_op jit(solution)/shard_map/ppermute | solution.py:351
  14.1 0.1 slice_add_fusion.4
  14.2 1.9 %collective-permute-start.10 = (f32[2,1,2,8,24,128]{5,4,3,2,1,0:T(8,128)S(1)}, f32[2,1,2,8,24,128]{5,4,3,2,1,0:T(8,128)S(1)}, u32[]{:S(2)}, u32[]{:S(2)}) collective-permute-start(f32[2,1,2,8,24,128]{5,4,3,2,1,0:T(8,128)S(1)} %get-tuple-element.66), channel_id=1, source_target_pairs={{0,4},{1,5},{2,6},{3,7},{4,0},{5,1},{6,2},{7,3},{8,12},{9,13},{10,... | collective-permute-start | bytes 1179656 | tf_op jit(solution)/shard_map/ppermute | solution.py:351
  16.1 0.1 slice_add_fusion.5
  16.2 1.1 %collective-permute-start.9 = (f32[2,2,1,8,24,128]{5,4,3,2,1,0:T(8,128)S(1)}, f32[2,2,1,8,24,128]{5,4,3,2,1,0:T(8,128)S(1)}, u32[]{:S(2)}, u32[]{:S(2)}) collective-permute-start(f32[2,2,1,8,24,128]{5,4,3,2,1,0:T(8,128)S(1)} %get-tuple-element.68), channel_id=1, source_target_pairs={{0,1},{1,0},{2,3},{3,2},{4,5},{5,4},{6,7},{7,6},{8,9},{9,8},{10,11... | collective-permute-start | bytes 1179656 | tf_op jit(solution)/shard_map/ppermute | solution.py:351
  17.3 0.3 slice_add_fusion.2
  17.6 1.3 %collective-permute-start.8 = (f32[1,2,2,8,32,128]{5,4,3,2,1,0:T(8,128)S(1)}, f32[1,2,2,8,32,128]{5,4,3,2,1,0:T(8,128)S(1)}, u32[]{:S(2)}, u32[]{:S(2)}) collective-permute-start(f32[1,2,2,8,32,128]{5,4,3,2,1,0:T(8,128)S(1)} %get-tuple-element.74), channel_id=1, source_target_pairs={{0,32},{1,33},{2,34},{3,35},{4,36},{5,37},{6,38},{7,39},{8,40},{9,... | collective-permute-start | bytes 1572872 | tf_op jit(solution)/shard_map/ppermute | solution.py:351
  18.9 0.2 slice_add_fusion
  19.2 2.5 %collective-permute-start.7 = (f32[2,1,2,8,32,128]{5,4,3,2,1,0:T(8,128)S(1)}, f32[2,1,2,8,32,128]{5,4,3,2,1,0:T(8,128)S(1)}, u32[]{:S(2)}, u32[]{:S(2)}) collective-permute-start(f32[2,1,2,8,32,128]{5,4,3,2,1,0:T(8,128)S(1)} %get-tuple-element.64), channel_id=1, source_target_pairs={{0,4},{1,5},{2,6},{3,7},{4,0},{5,1},{6,2},{7,3},{8,12},{9,13},{10,... | collective-permute-start | bytes 1572872 | tf_op jit(solution)/shard_map/ppermute | solution.py:351
  21.7 0.1 collective-permute-start.6
  21.8 0.2 collective-permute-done.10
  22.1 2.8 %collective-permute-start.15 = (f32[2,1,1,8,24,128]{5,4,3,2,1,0:T(8,128)S(1)}, f32[2,1,1,8,24,128]{5,4,3,2,1,0:T(8,128)S(1)}, u32[]{:S(2)}, u32[]{:S(2)}) collective-permute-start(f32[2,1,1,8,24,128]{5,4,3,2,1,0:T(8,128)S(1)} %get-tuple-element.78), channel_id=1, source_target_pairs={{0,1},{1,0},{2,3},{3,2},{4,5},{5,4},{6,7},{7,6},{8,9},{9,8},{10,11... | collective-permute-start | bytes 589832 | tf_op jit(solution)/shard_map/ppermute | solution.py:351
  25.0 1.3 %collective-permute-start.14 = (f32[1,2,1,8,24,128]{5,4,3,2,1,0:T(8,128)S(1)}, f32[1,2,1,8,24,128]{5,4,3,2,1,0:T(8,128)S(1)}, u32[]{:S(2)}, u32[]{:S(2)}) collective-permute-start(f32[1,2,1,8,24,128]{5,4,3,2,1,0:T(8,128)S(1)} %get-tuple-element.80), channel_id=1, source_target_pairs={{0,32},{1,33},{2,34},{3,35},{4,36},{5,37},{6,38},{7,39},{8,40},{9,... | collective-permute-start | bytes 589832 | tf_op jit(solution)/shard_map/ppermute | solution.py:351
  26.3 0.6 collective-permute-done.8
  26.9 0.1 slice_add_fusion.10
  26.9 2.0 %collective-permute-start.13 = (f32[1,1,2,8,32,128]{5,4,3,2,1,0:T(8,128)S(1)}, f32[1,1,2,8,32,128]{5,4,3,2,1,0:T(8,128)S(1)}, u32[]{:S(2)}, u32[]{:S(2)}) collective-permute-start(f32[1,1,2,8,32,128]{5,4,3,2,1,0:T(8,128)S(1)} %get-tuple-element.70), channel_id=1, source_target_pairs={{0,4},{1,5},{2,6},{3,7},{4,0},{5,1},{6,2},{7,3},{8,12},{9,13},{10,... | collective-permute-start | bytes 786440 | tf_op jit(solution)/shard_map/ppermute | solution.py:351
  28.9 0.1 slice_add_fusion.11
  29.0 1.6 %collective-permute-start.12 = (f32[2,1,1,8,32,128]{5,4,3,2,1,0:T(8,128)S(1)}, f32[2,1,1,8,32,128]{5,4,3,2,1,0:T(8,128)S(1)}, u32[]{:S(2)}, u32[]{:S(2)}) collective-permute-start(f32[2,1,1,8,32,128]{5,4,3,2,1,0:T(8,128)S(1)} %get-tuple-element.72), channel_id=1, source_target_pairs={{0,1},{1,0},{2,3},{3,2},{4,5},{5,4},{6,7},{7,6},{8,9},{9,8},{10,11... | collective-permute-start | bytes 786440 | tf_op jit(solution)/shard_map/ppermute | solution.py:351
  30.6 0.4 collective-permute-done.6
  31.0 1.7 %collective-permute-start.11 = (f32[1,1,1,8,24,128]{5,4,3,2,1,0:T(8,128)S(1)}, f32[1,1,1,8,24,128]{5,4,3,2,1,0:T(8,128)S(1)}, u32[]{:S(2)}, u32[]{:S(2)}) collective-permute-start(f32[1,1,1,8,24,128]{5,4,3,2,1,0:T(8,128)S(1)} %slice_add_fusion.28), channel_id=1, source_target_pairs={{0,1},{1,0},{2,3},{3,2},{4,5},{5,4},{6,7},{7,6},{8,9},{9,8},{10,11... | collective-permute-start | bytes 294920 | tf_op jit(solution)/shard_map/ppermute | solution.py:351
  32.6 1.4 %collective-permute-start.16 = (f32[1,1,1,8,24,128]{5,4,3,2,1,0:T(8,128)S(1)}, f32[1,1,1,8,24,128]{5,4,3,2,1,0:T(8,128)S(1)}, u32[]{:S(2)}, u32[]{:S(2)}) collective-permute-start(f32[1,1,1,8,24,128]{5,4,3,2,1,0:T(8,128)S(1)} %slice_add_fusion.26), channel_id=1, source_target_pairs={{0,32},{1,33},{2,34},{3,35},{4,36},{5,37},{6,38},{7,39},{8,40},{9,... | collective-permute-start | bytes 294920 | tf_op jit(solution)/shard_map/ppermute | solution.py:351
  34.0 0.2 collective-permute-start.17
  34.3 1.9 %collective-permute-start.18 = (f32[1,1,1,8,32,128]{5,4,3,2,1,0:T(8,128)S(1)}, f32[1,1,1,8,32,128]{5,4,3,2,1,0:T(8,128)S(1)}, u32[]{:S(2)}, u32[]{:S(2)}) collective-permute-start(f32[1,1,1,8,32,128]{5,4,3,2,1,0:T(8,128)S(1)} %slice_add_fusion.22), channel_id=1, source_target_pairs={{0,1},{1,0},{2,3},{3,2},{4,5},{5,4},{6,7},{7,6},{8,9},{9,8},{10,11... | collective-permute-start | bytes 393224 | tf_op jit(solution)/shard_map/ppermute | solution.py:351
  36.2 1.4 %collective-permute-start.19 = (f32[1,1,1,8,32,128]{5,4,3,2,1,0:T(8,128)S(1)}, f32[1,1,1,8,32,128]{5,4,3,2,1,0:T(8,128)S(1)}, u32[]{:S(2)}, u32[]{:S(2)}) collective-permute-start(f32[1,1,1,8,32,128]{5,4,3,2,1,0:T(8,128)S(1)} %slice_add_fusion.23), channel_id=1, source_target_pairs={{0,32},{1,33},{2,34},{3,35},{4,36},{5,37},{6,38},{7,39},{8,40},{9,... | collective-permute-start | bytes 393224 | tf_op jit(solution)/shard_map/ppermute | solution.py:351
  37.6 1.1 %collective-permute-done.17 = f32[1,1,1,8,24,128]{5,4,3,2,1,0:T(8,128)S(1)} collective-permute-done((f32[1,1,1,8,24,128]{5,4,3,2,1,0:T(8,128)S(1)}, f32[1,1,1,8,24,128]{5,4,3,2,1,0:T(8,128)S(1)}, u32[]{:S(2)}, u32[]{:S(2)}) %collective-permute-start.17) | collective-permute-done | bytes 98336 | tf_op jit(solution)/shard_map/ppermute | solution.py:351
  38.8 0.5 collective-permute-done.18
  39.3 1.9 %collective-permute-done.19 = f32[1,1,1,8,32,128]{5,4,3,2,1,0:T(8,128)S(1)} collective-permute-done((f32[1,1,1,8,32,128]{5,4,3,2,1,0:T(8,128)S(1)}, f32[1,1,1,8,32,128]{5,4,3,2,1,0:T(8,128)S(1)}, u32[]{:S(2)}, u32[]{:S(2)}) %collective-permute-start.19) | collective-permute-done | bytes 131104 | tf_op jit(solution)/shard_map/ppermute | solution.py:351
  41.3 4.7 %collective-permute-start.20 = (f32[2,136,128]{2,1,0:T(8,128)S(1)}, f32[2,136,128]{2,1,0:T(8,128)S(1)}, u32[]{:S(2)}, u32[]{:S(2)}) collective-permute-start(f32[2,136,128]{2,1,0:T(8,128)S(1)} %get-tuple-element.87), channel_id=1, source_target_pairs={{0,108},{1,109},{2,110},{3,111},{4,104},{5,105},{6,106},{7,107},{8... | collective-permute-start | bytes 417800 | tf_op jit(solution)/shard_map/ppermute | solution.py:351
  46.0 0.8 %collective-permute-start.22 = (f32[2,136,128]{2,1,0:T(8,128)S(1)}, f32[2,136,128]{2,1,0:T(8,128)S(1)}, u32[]{:S(2)}, u32[]{:S(2)}) collective-permute-start(f32[2,136,128]{2,1,0:T(8,128)S(1)} %get-tuple-element.88), channel_id=1, source_target_pairs={{0,12},{1,13},{2,14},{3,15},{4,8},{5,9},{6,10},{7,11},{8,4},{9,5},... | collective-permute-start | bytes 417800 | tf_op jit(solution)/shard_map/ppermute | solution.py:351
  46.8 2.6 %collective-permute-start.21 = (f32[2,136,128]{2,1,0:T(8,128)S(1)}, f32[2,136,128]{2,1,0:T(8,128)S(1)}, u32[]{:S(2)}, u32[]{:S(2)}) collective-permute-start(f32[2,136,128]{2,1,0:T(8,128)S(1)} %get-tuple-element.89), channel_id=1, source_target_pairs={{0,96},{1,97},{2,98},{3,99},{4,100},{5,101},{6,102},{7,103},{8,104... | collective-permute-start | bytes 417800 | tf_op jit(solution)/shard_map/ppermute | solution.py:351
  49.4 0.4 collective-permute-done.20
  49.8 2.5 %collective-permute-done.22 = f32[2,136,128]{2,1,0:T(8,128)S(1)} collective-permute-done((f32[2,136,128]{2,1,0:T(8,128)S(1)}, f32[2,136,128]{2,1,0:T(8,128)S(1)}, u32[]{:S(2)}, u32[]{:S(2)}) %collective-permute-start.22) | collective-permute-done | bytes 139296 | tf_op jit(solution)/shard_map/ppermute | solution.py:351
  52.3 1.7 %collective-permute-done.21 = f32[2,136,128]{2,1,0:T(8,128)S(1)} collective-permute-done((f32[2,136,128]{2,1,0:T(8,128)S(1)}, f32[2,136,128]{2,1,0:T(8,128)S(1)}, u32[]{:S(2)}, u32[]{:S(2)}) %collective-permute-start.21) | collective-permute-done | bytes 139296 | tf_op jit(solution)/shard_map/ppermute | solution.py:351
  54.0 2.0 %collective-permute-start.23 = (f32[136,128]{1,0:T(8,128)S(1)}, f32[136,128]{1,0:T(8,128)S(1)}, u32[]{:S(2)}, u32[]{:S(2)}) collective-permute-start(f32[136,128]{1,0:T(8,128)S(1)} %slice_bitcast_fusion.4), channel_id=1, source_target_pairs={{0,3},{1,2},{2,1},{3,0},{4,7},{5,6},{6,5},{7,4},{8,11},{9,10},{10,... | collective-permute-start | bytes 208904 | tf_op jit(solution)/shard_map/ppermute | solution.py:351
  56.0 3.6 %collective-permute-done.23 = f32[136,128]{1,0:T(8,128)S(1)} collective-permute-done((f32[136,128]{1,0:T(8,128)S(1)}, f32[136,128]{1,0:T(8,128)S(1)}, u32[]{:S(2)}, u32[]{:S(2)}) %collective-permute-start.23) | collective-permute-done | bytes 69664 | tf_op jit(solution)/shard_map/ppermute | solution.py:351
  59.6 4.5 %collective-permute-start.24 = (f32[128,128]{1,0:T(8,128)S(1)}, f32[128,128]{1,0:T(8,128)S(1)}, u32[]{:S(2)}, u32[]{:S(2)}) collective-permute-start(f32[128,128]{1,0:T(8,128)S(1)} %slice.318), channel_id=1, source_target_pairs={{0,1},{1,0},{2,17},{3,16},{4,33},{5,32},{6,49},{7,48},{8,65},{9,64... | collective-permute-start | bytes 196616 | tf_op jit(solution)/shard_map/ppermute | solution.py:351
  64.1 4.7 %collective-permute-done.24.theirs = f32[128,128]{1,0:T(8,128)S(1)} collective-permute-done((f32[128,128]{1,0:T(8,128)S(1)}, f32[128,128]{1,0:T(8,128)S(1)}, u32[]{:S(2)}, u32[]{:S(2)}) %collective-permute-start.24) | collective-permute-done | bytes 65568 | tf_op jit(solution)/shard_map/ppermute | solution.py:351
  68.8 0.7 finish.1
  (36 shorter events, 0.5 us)
Async XLA Ops:
  9.5 2.4 %collective-permute-start = (f32[64,24,128]{2,1,0:T(8,128)S(1)}, f32[64,24,128]{2,1,0:T(8,128)S(1)}, u32[]{:S(2)}, u32[]{:S(2)}) collective-permute-start(f32[64,24,128]{2,1,0:T(8,128)S(1)} %get-tuple-element.35), channel_id=1, source_target_pairs={{0,16},{1,17},{2,18},{3,19},{4,20},{5,21},{6,22},{7,23},{8,24},{9,... | collective-permute-start | bytes 2359304 | tf_op jit(solution)/shard_map/ppermute | solution.py:351
  9.6 6.5 %collective-permute-start.4 = (f32[64,24,128]{2,1,0:T(8,128)S(1)}, f32[64,24,128]{2,1,0:T(8,128)S(1)}, u32[]{:S(2)}, u32[]{:S(2)}) collective-permute-start(f32[64,24,128]{2,1,0:T(8,128)S(1)} %get-tuple-element.41), channel_id=1, source_target_pairs={{0,16},{1,17},{2,18},{3,19},{4,20},{5,21},{6,22},{7,23},{8,24},{9,... | collective-permute-start | bytes 2359304 | tf_op jit(solution)/shard_map/ppermute | solution.py:351
  10.1 4.0 %collective-permute-start.5 = (f32[64,24,128]{2,1,0:T(8,128)S(1)}, f32[64,24,128]{2,1,0:T(8,128)S(1)}, u32[]{:S(2)}, u32[]{:S(2)}) collective-permute-start(f32[64,24,128]{2,1,0:T(8,128)S(1)} %get-tuple-element.43), channel_id=1, source_target_pairs={{0,16},{1,17},{2,18},{3,19},{4,20},{5,21},{6,22},{7,23},{8,24},{9,... | collective-permute-start | bytes 2359304 | tf_op jit(solution)/shard_map/ppermute | solution.py:351
  10.2 8.7 %collective-permute-start.2 = (f32[64,32,128]{2,1,0:T(8,128)S(1)}, f32[64,32,128]{2,1,0:T(8,128)S(1)}, u32[]{:S(2)}, u32[]{:S(2)}) collective-permute-start(f32[64,32,128]{2,1,0:T(8,128)S(1)} %get-tuple-element.37), channel_id=1, source_target_pairs={{0,16},{1,17},{2,18},{3,19},{4,20},{5,21},{6,22},{7,23},{8,24},{9,... | collective-permute-start | bytes 3145736 | tf_op jit(solution)/shard_map/ppermute | solution.py:351
  10.6 6.7 %collective-permute-start.3 = (f32[64,32,128]{2,1,0:T(8,128)S(1)}, f32[64,32,128]{2,1,0:T(8,128)S(1)}, u32[]{:S(2)}, u32[]{:S(2)}) collective-permute-start(f32[64,32,128]{2,1,0:T(8,128)S(1)} %get-tuple-element.39), channel_id=1, source_target_pairs={{0,16},{1,17},{2,18},{3,19},{4,20},{5,21},{6,22},{7,23},{8,24},{9,... | collective-permute-start | bytes 3145736 | tf_op jit(solution)/shard_map/ppermute | solution.py:351
  12.0 9.7 %collective-permute-start.1 = (f32[1,2,2,8,24,128]{5,4,3,2,1,0:T(8,128)S(1)}, f32[1,2,2,8,24,128]{5,4,3,2,1,0:T(8,128)S(1)}, u32[]{:S(2)}, u32[]{:S(2)}) collective-permute-start(f32[1,2,2,8,24,128]{5,4,3,2,1,0:T(8,128)S(1)} %get-tuple-element.83), channel_id=1, source_target_pairs={{0,32},{1,33},{2,34},{3,35},{4,36},{5,37},{6,38},{7,39},{8,40},{9,... | collective-permute-start | bytes 1179656 | tf_op jit(solution)/shard_map/ppermute | solution.py:351
  14.2 7.9 %collective-permute-start.10 = (f32[2,1,2,8,24,128]{5,4,3,2,1,0:T(8,128)S(1)}, f32[2,1,2,8,24,128]{5,4,3,2,1,0:T(8,128)S(1)}, u32[]{:S(2)}, u32[]{:S(2)}) collective-permute-start(f32[2,1,2,8,24,128]{5,4,3,2,1,0:T(8,128)S(1)} %get-tuple-element.66), channel_id=1, source_target_pairs={{0,4},{1,5},{2,6},{3,7},{4,0},{5,1},{6,2},{7,3},{8,12},{9,13},{10,... | collective-permute-start | bytes 1179656 | tf_op jit(solution)/shard_map/ppermute | solution.py:351
  16.2 8.7 %collective-permute-start.9 = (f32[2,2,1,8,24,128]{5,4,3,2,1,0:T(8,128)S(1)}, f32[2,2,1,8,24,128]{5,4,3,2,1,0:T(8,128)S(1)}, u32[]{:S(2)}, u32[]{:S(2)}) collective-permute-start(f32[2,2,1,8,24,128]{5,4,3,2,1,0:T(8,128)S(1)} %get-tuple-element.68), channel_id=1, source_target_pairs={{0,1},{1,0},{2,3},{3,2},{4,5},{5,4},{6,7},{7,6},{8,9},{9,8},{10,11... | collective-permute-start | bytes 1179656 | tf_op jit(solution)/shard_map/ppermute | solution.py:351
  17.6 9.3 %collective-permute-start.8 = (f32[1,2,2,8,32,128]{5,4,3,2,1,0:T(8,128)S(1)}, f32[1,2,2,8,32,128]{5,4,3,2,1,0:T(8,128)S(1)}, u32[]{:S(2)}, u32[]{:S(2)}) collective-permute-start(f32[1,2,2,8,32,128]{5,4,3,2,1,0:T(8,128)S(1)} %get-tuple-element.74), channel_id=1, source_target_pairs={{0,32},{1,33},{2,34},{3,35},{4,36},{5,37},{6,38},{7,39},{8,40},{9,... | collective-permute-start | bytes 1572872 | tf_op jit(solution)/shard_map/ppermute | solution.py:351
  19.2 9.8 %collective-permute-start.7 = (f32[2,1,2,8,32,128]{5,4,3,2,1,0:T(8,128)S(1)}, f32[2,1,2,8,32,128]{5,4,3,2,1,0:T(8,128)S(1)}, u32[]{:S(2)}, u32[]{:S(2)}) collective-permute-start(f32[2,1,2,8,32,128]{5,4,3,2,1,0:T(8,128)S(1)} %get-tuple-element.64), channel_id=1, source_target_pairs={{0,4},{1,5},{2,6},{3,7},{4,0},{5,1},{6,2},{7,3},{8,12},{9,13},{10,... | collective-permute-start | bytes 1572872 | tf_op jit(solution)/shard_map/ppermute | solution.py:351
  21.7 9.2 %collective-permute-start.6 = (f32[1,1,2,8,24,128]{5,4,3,2,1,0:T(8,128)S(1)}, f32[1,1,2,8,24,128]{5,4,3,2,1,0:T(8,128)S(1)}, u32[]{:S(2)}, u32[]{:S(2)}) collective-permute-start(f32[1,1,2,8,24,128]{5,4,3,2,1,0:T(8,128)S(1)} %get-tuple-element.81), channel_id=1, source_target_pairs={{0,4},{1,5},{2,6},{3,7},{4,0},{5,1},{6,2},{7,3},{8,12},{9,13},{10,... | collective-permute-start | bytes 589832 | tf_op jit(solution)/shard_map/ppermute | solution.py:351
  22.1 10.5 %collective-permute-start.15 = (f32[2,1,1,8,24,128]{5,4,3,2,1,0:T(8,128)S(1)}, f32[2,1,1,8,24,128]{5,4,3,2,1,0:T(8,128)S(1)}, u32[]{:S(2)}, u32[]{:S(2)}) collective-permute-start(f32[2,1,1,8,24,128]{5,4,3,2,1,0:T(8,128)S(1)} %get-tuple-element.78), channel_id=1, source_target_pairs={{0,1},{1,0},{2,3},{3,2},{4,5},{5,4},{6,7},{7,6},{8,9},{9,8},{10,11... | collective-permute-start | bytes 589832 | tf_op jit(solution)/shard_map/ppermute | solution.py:351
  25.0 9.0 %collective-permute-start.14 = (f32[1,2,1,8,24,128]{5,4,3,2,1,0:T(8,128)S(1)}, f32[1,2,1,8,24,128]{5,4,3,2,1,0:T(8,128)S(1)}, u32[]{:S(2)}, u32[]{:S(2)}) collective-permute-start(f32[1,2,1,8,24,128]{5,4,3,2,1,0:T(8,128)S(1)} %get-tuple-element.80), channel_id=1, source_target_pairs={{0,32},{1,33},{2,34},{3,35},{4,36},{5,37},{6,38},{7,39},{8,40},{9,... | collective-permute-start | bytes 589832 | tf_op jit(solution)/shard_map/ppermute | solution.py:351
  26.9 7.3 %collective-permute-start.13 = (f32[1,1,2,8,32,128]{5,4,3,2,1,0:T(8,128)S(1)}, f32[1,1,2,8,32,128]{5,4,3,2,1,0:T(8,128)S(1)}, u32[]{:S(2)}, u32[]{:S(2)}) collective-permute-start(f32[1,1,2,8,32,128]{5,4,3,2,1,0:T(8,128)S(1)} %get-tuple-element.70), channel_id=1, source_target_pairs={{0,4},{1,5},{2,6},{3,7},{4,0},{5,1},{6,2},{7,3},{8,12},{9,13},{10,... | collective-permute-start | bytes 786440 | tf_op jit(solution)/shard_map/ppermute | solution.py:351
  29.0 7.1 %collective-permute-start.12 = (f32[2,1,1,8,32,128]{5,4,3,2,1,0:T(8,128)S(1)}, f32[2,1,1,8,32,128]{5,4,3,2,1,0:T(8,128)S(1)}, u32[]{:S(2)}, u32[]{:S(2)}) collective-permute-start(f32[2,1,1,8,32,128]{5,4,3,2,1,0:T(8,128)S(1)} %get-tuple-element.72), channel_id=1, source_target_pairs={{0,1},{1,0},{2,3},{3,2},{4,5},{5,4},{6,7},{7,6},{8,9},{9,8},{10,11... | collective-permute-start | bytes 786440 | tf_op jit(solution)/shard_map/ppermute | solution.py:351
  31.0 6.6 %collective-permute-start.11 = (f32[1,1,1,8,24,128]{5,4,3,2,1,0:T(8,128)S(1)}, f32[1,1,1,8,24,128]{5,4,3,2,1,0:T(8,128)S(1)}, u32[]{:S(2)}, u32[]{:S(2)}) collective-permute-start(f32[1,1,1,8,24,128]{5,4,3,2,1,0:T(8,128)S(1)} %slice_add_fusion.28), channel_id=1, source_target_pairs={{0,1},{1,0},{2,3},{3,2},{4,5},{5,4},{6,7},{7,6},{8,9},{9,8},{10,11... | collective-permute-start | bytes 294920 | tf_op jit(solution)/shard_map/ppermute | solution.py:351
  32.6 4.9 %collective-permute-start.16 = (f32[1,1,1,8,24,128]{5,4,3,2,1,0:T(8,128)S(1)}, f32[1,1,1,8,24,128]{5,4,3,2,1,0:T(8,128)S(1)}, u32[]{:S(2)}, u32[]{:S(2)}) collective-permute-start(f32[1,1,1,8,24,128]{5,4,3,2,1,0:T(8,128)S(1)} %slice_add_fusion.26), channel_id=1, source_target_pairs={{0,32},{1,33},{2,34},{3,35},{4,36},{5,37},{6,38},{7,39},{8,40},{9,... | collective-permute-start | bytes 294920 | tf_op jit(solution)/shard_map/ppermute | solution.py:351
  34.0 4.7 %collective-permute-start.17 = (f32[1,1,1,8,24,128]{5,4,3,2,1,0:T(8,128)S(1)}, f32[1,1,1,8,24,128]{5,4,3,2,1,0:T(8,128)S(1)}, u32[]{:S(2)}, u32[]{:S(2)}) collective-permute-start(f32[1,1,1,8,24,128]{5,4,3,2,1,0:T(8,128)S(1)} %slice_add_fusion.27), channel_id=1, source_target_pairs={{0,4},{1,5},{2,6},{3,7},{4,0},{5,1},{6,2},{7,3},{8,12},{9,13},{10,... | collective-permute-start | bytes 294920 | tf_op jit(solution)/shard_map/ppermute | solution.py:351
  34.3 5.0 %collective-permute-start.18 = (f32[1,1,1,8,32,128]{5,4,3,2,1,0:T(8,128)S(1)}, f32[1,1,1,8,32,128]{5,4,3,2,1,0:T(8,128)S(1)}, u32[]{:S(2)}, u32[]{:S(2)}) collective-permute-start(f32[1,1,1,8,32,128]{5,4,3,2,1,0:T(8,128)S(1)} %slice_add_fusion.22), channel_id=1, source_target_pairs={{0,1},{1,0},{2,3},{3,2},{4,5},{5,4},{6,7},{7,6},{8,9},{9,8},{10,11... | collective-permute-start | bytes 393224 | tf_op jit(solution)/shard_map/ppermute | solution.py:351
  36.2 5.0 %collective-permute-start.19 = (f32[1,1,1,8,32,128]{5,4,3,2,1,0:T(8,128)S(1)}, f32[1,1,1,8,32,128]{5,4,3,2,1,0:T(8,128)S(1)}, u32[]{:S(2)}, u32[]{:S(2)}) collective-permute-start(f32[1,1,1,8,32,128]{5,4,3,2,1,0:T(8,128)S(1)} %slice_add_fusion.23), channel_id=1, source_target_pairs={{0,32},{1,33},{2,34},{3,35},{4,36},{5,37},{6,38},{7,39},{8,40},{9,... | collective-permute-start | bytes 393224 | tf_op jit(solution)/shard_map/ppermute | solution.py:351
  41.3 8.5 %collective-permute-start.20 = (f32[2,136,128]{2,1,0:T(8,128)S(1)}, f32[2,136,128]{2,1,0:T(8,128)S(1)}, u32[]{:S(2)}, u32[]{:S(2)}) collective-permute-start(f32[2,136,128]{2,1,0:T(8,128)S(1)} %get-tuple-element.87), channel_id=1, source_target_pairs={{0,108},{1,109},{2,110},{3,111},{4,104},{5,105},{6,106},{7,107},{8... | collective-permute-start | bytes 417800 | tf_op jit(solution)/shard_map/ppermute | solution.py:351
  46.0 6.3 %collective-permute-start.22 = (f32[2,136,128]{2,1,0:T(8,128)S(1)}, f32[2,136,128]{2,1,0:T(8,128)S(1)}, u32[]{:S(2)}, u32[]{:S(2)}) collective-permute-start(f32[2,136,128]{2,1,0:T(8,128)S(1)} %get-tuple-element.88), channel_id=1, source_target_pairs={{0,12},{1,13},{2,14},{3,15},{4,8},{5,9},{6,10},{7,11},{8,4},{9,5},... | collective-permute-start | bytes 417800 | tf_op jit(solution)/shard_map/ppermute | solution.py:351
  46.8 7.1 %collective-permute-start.21 = (f32[2,136,128]{2,1,0:T(8,128)S(1)}, f32[2,136,128]{2,1,0:T(8,128)S(1)}, u32[]{:S(2)}, u32[]{:S(2)}) collective-permute-start(f32[2,136,128]{2,1,0:T(8,128)S(1)} %get-tuple-element.89), channel_id=1, source_target_pairs={{0,96},{1,97},{2,98},{3,99},{4,100},{5,101},{6,102},{7,103},{8,104... | collective-permute-start | bytes 417800 | tf_op jit(solution)/shard_map/ppermute | solution.py:351
  54.0 5.6 %collective-permute-start.23 = (f32[136,128]{1,0:T(8,128)S(1)}, f32[136,128]{1,0:T(8,128)S(1)}, u32[]{:S(2)}, u32[]{:S(2)}) collective-permute-start(f32[136,128]{1,0:T(8,128)S(1)} %slice_bitcast_fusion.4), channel_id=1, source_target_pairs={{0,3},{1,2},{2,1},{3,0},{4,7},{5,6},{6,5},{7,4},{8,11},{9,10},{10,... | collective-permute-start | bytes 208904 | tf_op jit(solution)/shard_map/ppermute | solution.py:351
  59.6 9.2 %collective-permute-start.24 = (f32[128,128]{1,0:T(8,128)S(1)}, f32[128,128]{1,0:T(8,128)S(1)}, u32[]{:S(2)}, u32[]{:S(2)}) collective-permute-start(f32[128,128]{1,0:T(8,128)S(1)} %slice.318), channel_id=1, source_target_pairs={{0,1},{1,0},{2,17},{3,16},{4,33},{5,32},{6,49},{7,48},{8,65},{9,64... | collective-permute-start | bytes 196616 | tf_op jit(solution)/shard_map/ppermute | solution.py:351

commit v3 on v2

--- a/solution.py
+++ b/solution.py
@@ -17,6 +17,7 @@
 NDEV = 128
 SHARES = NDEV // 2
 PARTS = len(COLOURS)
+LATER_ORDER = (0, 1, 2, 4, 3)
 KERNEL_VMEM = 28 * 1024 * 1024
 LIST = 32
 UNROLL = 3
@@ -357,20 +358,23 @@
     keeps, sends = partial_sums(ints, tile_mu, tile_lam, tile_live, coefficients, occ_ids)
     keeps = [v.reshape(first_bits + v.shape[1:]) for v in keeps]
     cames = [swap(v, core_pairs()).reshape(first_bits + v.shape[1:]) for v in sends]
-    tie = ()
+    tie, sent = (), []
     for step in range(3):
-        for number in range(PARTS):
+        for number in range(PARTS) if step == 0 else LATER_ORDER:
             axis = (number + step) % 3
+            if step == 0:
+                tie = tuple(sent[: (number + 1) // 2 * 2 - 1]) if number else ()
             theirs = after(cames[number], *tie)
             at = lambda v, bit: lax.index_in_dim(v, bit, axis, keepdims=True)
             out_going = at(keeps[number], 1) + at(theirs, 1)
             keeps[number] = at(keeps[number], 0) + at(theirs, 0)
             cames[number] = swap(out_going, axis_pairs((axis,), False))
+            sent.append(out_going)
             tie = (out_going,)
-    merged = []
-    for mine, theirs in zip(keeps, cames):
-        mine = (mine + after(theirs, *tie)).reshape((4, 2) + mine.shape[-2:])
-        merged.append(mine)
+    merged = [None] * PARTS
+    for number in LATER_ORDER:
+        mine = keeps[number] + after(cames[number], *tie)
+        merged[number] = mine.reshape((4, 2) + mine.shape[-2:])
         tie = (mine,)
     mine = jnp.concatenate(merged, axis=2)
 

time: 70.3 us -> 71.2 us (1.013)
  starting transfers between devices: 37.8 us -> 21 us
  waiting for transfers between devices: 19.8 us -> 34.6 us
  Pallas kernels: 10.2 us -> 12.9 us
    ppermute x25, starting transfers between devices: 37.8 us -> 21 us  [swap(): return lax.ppermute(array, AXES, pairs)]
    ppermute x25, waiting for transfers between devices: 19.8 us -> 34.6 us  [swap(): return lax.ppermute(array, AXES, pairs)]
    pallas_call x1, Pallas kernels: 9.51 us -> 12.3 us  [partial_sums(): pl.pallas_call(partial_kernel, out_shape=shares + shares, in_specs=[hbm]...]
  transfers between devices with their start and end apart: 25 -> 25, of which waited for: 13 -> 17; matrix products, arithmetic and copies ran while one was open for 2% -> 2% of each run, Pallas kernels for 0% -> 0%
where the time goes in v3:
time: 71.2 us; the launch traced here: 70.3 us
  waiting for transfers between devices  34.6 us (49%)
  starting transfers between devices  21 us (29%)
  Pallas kernels  12.9 us (18%)
  other arithmetic  1.19 us (2%)
    ppermute x25, waiting for transfers between devices, swap(): return lax.ppermute(array, AXES, pairs)  34.6 us
    ppermute x25, starting transfers between devices, swap(): return lax.ppermute(array, AXES, pairs)  21 us
    pallas_call x1, Pallas kernels, partial_sums(): pl.pallas_call(partial_kernel, out_shape=shares + shares, in_specs=[hbm]...  12.3 us
  transfers between devices with their start and end apart: 25, of which 17 were waited for; matrix products, arithmetic and copies ran while one was open for 2% of the time, Pallas kernels for 0%

profile of v3, /device:TPU:6, one launch (start us, length us, event | category | flops | bytes accessed | tf_op | source)
XLA Modules:
  0.0 70.3 jit_solution(16834590691383289819)
XLA Ops:
  0.0 12.3 %partial_sums.1 = (f32[64,24,128]{2,1,0:T(8,128)S(1)}, f32[64,24,128]{2,1,0:T(8,128)S(1)}, f32[64,24,128]{2,1,0:T(8,128)S(1)}, f32[64,32,128]{2,1,0:T(8,128)S(1)...) custom-call(s32[16]{0:T(128)} %mu_hbm.1, ...), custom_call_target="tpu_custom_call" | custom-call | flops 8000000000 | bytes 5242880 | tf_op jit(solution)/shard_map/partial_sums/pallas_call | solution.py:273
  12.3 0.1 collective-permute-start
  12.4 0.5 collective-permute-start.3
  12.9 0.1 collective-permute-start.4
  12.9 0.4 collective-permute-start.2
  13.4 0.1 collective-permute-start.6
  13.6 1.0 %collective-permute-done = f32[64,24,128]{2,1,0:T(8,128)S(1)} collective-permute-done((f32[64,24,128]{2,1,0:T(8,128)S(1)}, f32[64,24,128]{2,1,0:T(8,128)S(1)}, u32[]{:S(2)}, u32[]{:S(2)}) %collective-permute-start) | collective-permute-done | bytes 786464 | tf_op jit(solution)/shard_map/ppermute | solution.py:352
  14.6 0.1 slice_add_fusion.8
  14.7 0.4 collective-permute-start.1
  15.1 0.7 collective-permute-done.3
  15.8 0.1 slice_add_fusion.4
  15.8 0.1 collective-permute-start.10
  16.0 0.9 %collective-permute-done.4 = f32[64,24,128]{2,1,0:T(8,128)S(1)} collective-permute-done((f32[64,24,128]{2,1,0:T(8,128)S(1)}, f32[64,24,128]{2,1,0:T(8,128)S(1)}, u32[]{:S(2)}, u32[]{:S(2)}) %collective-permute-start.4) | collective-permute-done | bytes 786464 | tf_op jit(solution)/shard_map/ppermute | solution.py:352
  16.9 0.1 slice_add_fusion.5
  17.0 0.2 collective-permute-start.9
  17.2 1.2 %collective-permute-done.2 = f32[64,32,128]{2,1,0:T(8,128)S(1)} collective-permute-done((f32[64,32,128]{2,1,0:T(8,128)S(1)}, f32[64,32,128]{2,1,0:T(8,128)S(1)}, u32[]{:S(2)}, u32[]{:S(2)}) %collective-permute-start.2) | collective-permute-done | bytes 1048608 | tf_op jit(solution)/shard_map/ppermute | solution.py:352
  18.4 0.2 slice_add_fusion
  18.6 0.1 collective-permute-start.8
  18.7 1.2 %collective-permute-done.6 = f32[64,32,128]{2,1,0:T(8,128)S(1)} collective-permute-done((f32[64,32,128]{2,1,0:T(8,128)S(1)}, f32[64,32,128]{2,1,0:T(8,128)S(1)}, u32[]{:S(2)}, u32[]{:S(2)}) %collective-permute-start.6) | collective-permute-done | bytes 1048608 | tf_op jit(solution)/shard_map/ppermute | solution.py:352
  19.9 0.2 slice_add_fusion.2
  20.1 0.4 collective-permute-start.7
  20.5 2.1 %collective-permute-done.1 = f32[1,2,2,8,24,128]{5,4,3,2,1,0:T(8,128)S(1)} collective-permute-done((f32[1,2,2,8,24,128]{5,4,3,2,1,0:T(8,128)S(1)}, f32[1,2,2,8,24,128]{5,4,3,2,1,0:T(8,128)S(1)}, u32[]{:S(2)}, u32[]{:S(2)}) %collective-permute-start.1) | collective-permute-done | bytes 393248 | tf_op jit(solution)/shard_map/ppermute | solution.py:352
  22.6 0.1 collective-permute-start.5
  22.7 1.0 %collective-permute-done.10 = f32[2,1,2,8,24,128]{5,4,3,2,1,0:T(8,128)S(1)} collective-permute-done((f32[2,1,2,8,24,128]{5,4,3,2,1,0:T(8,128)S(1)}, f32[2,1,2,8,24,128]{5,4,3,2,1,0:T(8,128)S(1)}, u32[]{:S(2)}, u32[]{:S(2)}) %collective-permute-start.10) | collective-permute-done | bytes 393248 | tf_op jit(solution)/shard_map/ppermute | solution.py:352
  23.7 0.1 collective-permute-start.15
  23.8 1.0 %collective-permute-done.9 = f32[2,2,1,8,24,128]{5,4,3,2,1,0:T(8,128)S(1)} collective-permute-done((f32[2,2,1,8,24,128]{5,4,3,2,1,0:T(8,128)S(1)}, f32[2,2,1,8,24,128]{5,4,3,2,1,0:T(8,128)S(1)}, u32[]{:S(2)}, u32[]{:S(2)}) %collective-permute-start.9) | collective-permute-done | bytes 393248 | tf_op jit(solution)/shard_map/ppermute | solution.py:352
  24.9 0.4 collective-permute-start.14
  25.2 4.1 %collective-permute-done.8 = f32[2,1,2,8,32,128]{5,4,3,2,1,0:T(8,128)S(1)} collective-permute-done((f32[2,1,2,8,32,128]{5,4,3,2,1,0:T(8,128)S(1)}, f32[2,1,2,8,32,128]{5,4,3,2,1,0:T(8,128)S(1)}, u32[]{:S(2)}, u32[]{:S(2)}) %collective-permute-start.8) | collective-permute-done | bytes 524320 | tf_op jit(solution)/shard_map/ppermute | solution.py:352
  29.4 0.1 collective-permute-start.13
  29.6 1.1 %collective-permute-start.12 = (f32[1,1,2,8,32,128]{5,4,3,2,1,0:T(8,128)S(1)}, f32[1,1,2,8,32,128]{5,4,3,2,1,0:T(8,128)S(1)}, u32[]{:S(2)}, u32[]{:S(2)}) collective-permute-start(f32[1,1,2,8,32,128]{5,4,3,2,1,0:T(8,128)S(1)} %get-tuple-element.72), channel_id=1, source_target_pairs={{0,4},{1,5},{2,6},{3,7},{4,0},{5,1},{6,2},{7,3},{8,12},{9,13},{10,... | collective-permute-start | bytes 786440 | tf_op jit(solution)/shard_map/ppermute | solution.py:352
  30.7 0.7 collective-permute-done.5
  31.4 0.4 collective-permute-start.11
  31.8 1.2 %collective-permute-start.16 = (f32[1,1,1,8,24,128]{5,4,3,2,1,0:T(8,128)S(1)}, f32[1,1,1,8,24,128]{5,4,3,2,1,0:T(8,128)S(1)}, u32[]{:S(2)}, u32[]{:S(2)}) collective-permute-start(f32[1,1,1,8,24,128]{5,4,3,2,1,0:T(8,128)S(1)} %slice_add_fusion.26), channel_id=1, source_target_pairs={{0,32},{1,33},{2,34},{3,35},{4,36},{5,37},{6,38},{7,39},{8,40},{9,... | collective-permute-start | bytes 294920 | tf_op jit(solution)/shard_map/ppermute | solution.py:352
  33.0 2.1 %collective-permute-start.17 = (f32[1,1,1,8,24,128]{5,4,3,2,1,0:T(8,128)S(1)}, f32[1,1,1,8,24,128]{5,4,3,2,1,0:T(8,128)S(1)}, u32[]{:S(2)}, u32[]{:S(2)}) collective-permute-start(f32[1,1,1,8,24,128]{5,4,3,2,1,0:T(8,128)S(1)} %slice_add_fusion.27), channel_id=1, source_target_pairs={{0,4},{1,5},{2,6},{3,7},{4,0},{5,1},{6,2},{7,3},{8,12},{9,13},{10,... | collective-permute-start | bytes 294920 | tf_op jit(solution)/shard_map/ppermute | solution.py:352
  35.1 0.8 %collective-permute-done.13 = f32[2,1,1,8,32,128]{5,4,3,2,1,0:T(8,128)S(1)} collective-permute-done((f32[2,1,1,8,32,128]{5,4,3,2,1,0:T(8,128)S(1)}, f32[2,1,1,8,32,128]{5,4,3,2,1,0:T(8,128)S(1)}, u32[]{:S(2)}, u32[]{:S(2)}) %collective-permute-start.13) | collective-permute-done | bytes 262176 | tf_op jit(solution)/shard_map/ppermute | solution.py:352
  35.9 1.2 %collective-permute-start.19 = (f32[1,1,1,8,32,128]{5,4,3,2,1,0:T(8,128)S(1)}, f32[1,1,1,8,32,128]{5,4,3,2,1,0:T(8,128)S(1)}, u32[]{:S(2)}, u32[]{:S(2)}) collective-permute-start(f32[1,1,1,8,32,128]{5,4,3,2,1,0:T(8,128)S(1)} %slice_add_fusion.22), channel_id=1, source_target_pairs={{0,32},{1,33},{2,34},{3,35},{4,36},{5,37},{6,38},{7,39},{8,40},{9,... | collective-permute-start | bytes 393224 | tf_op jit(solution)/shard_map/ppermute | solution.py:352
  37.1 1.1 %collective-permute-start.18 = (f32[1,1,1,8,32,128]{5,4,3,2,1,0:T(8,128)S(1)}, f32[1,1,1,8,32,128]{5,4,3,2,1,0:T(8,128)S(1)}, u32[]{:S(2)}, u32[]{:S(2)}) collective-permute-start(f32[1,1,1,8,32,128]{5,4,3,2,1,0:T(8,128)S(1)} %slice_add_fusion.23), channel_id=1, source_target_pairs={{0,1},{1,0},{2,3},{3,2},{4,5},{5,4},{6,7},{7,6},{8,9},{9,8},{10,11... | collective-permute-start | bytes 393224 | tf_op jit(solution)/shard_map/ppermute | solution.py:352
  38.3 2.6 %collective-permute-done.19 = f32[1,1,1,8,32,128]{5,4,3,2,1,0:T(8,128)S(1)} collective-permute-done((f32[1,1,1,8,32,128]{5,4,3,2,1,0:T(8,128)S(1)}, f32[1,1,1,8,32,128]{5,4,3,2,1,0:T(8,128)S(1)}, u32[]{:S(2)}, u32[]{:S(2)}) %collective-permute-start.19) | collective-permute-done | bytes 131104 | tf_op jit(solution)/shard_map/ppermute | solution.py:352
  41.0 1.1 %collective-permute-done.18 = f32[1,1,1,8,32,128]{5,4,3,2,1,0:T(8,128)S(1)} collective-permute-done((f32[1,1,1,8,32,128]{5,4,3,2,1,0:T(8,128)S(1)}, f32[1,1,1,8,32,128]{5,4,3,2,1,0:T(8,128)S(1)}, u32[]{:S(2)}, u32[]{:S(2)}) %collective-permute-start.18) | collective-permute-done | bytes 131104 | tf_op jit(solution)/shard_map/ppermute | solution.py:352
  42.2 6.9 %collective-permute-start.20 = (f32[2,136,128]{2,1,0:T(8,128)S(1)}, f32[2,136,128]{2,1,0:T(8,128)S(1)}, u32[]{:S(2)}, u32[]{:S(2)}) collective-permute-start(f32[2,136,128]{2,1,0:T(8,128)S(1)} %get-tuple-element.87), channel_id=1, source_target_pairs={{0,108},{1,109},{2,110},{3,111},{4,104},{5,105},{6,106},{7,107},{8... | collective-permute-start | bytes 417800 | tf_op jit(solution)/shard_map/ppermute | solution.py:352
  49.1 0.7 collective-permute-start.21
  49.7 2.4 %collective-permute-done.20 = f32[2,136,128]{2,1,0:T(8,128)S(1)} collective-permute-done((f32[2,136,128]{2,1,0:T(8,128)S(1)}, f32[2,136,128]{2,1,0:T(8,128)S(1)}, u32[]{:S(2)}, u32[]{:S(2)}) %collective-permute-start.20) | collective-permute-done | bytes 139296 | tf_op jit(solution)/shard_map/ppermute | solution.py:352
  52.1 3.2 %collective-permute-done.22 = f32[2,136,128]{2,1,0:T(8,128)S(1)} collective-permute-done((f32[2,136,128]{2,1,0:T(8,128)S(1)}, f32[2,136,128]{2,1,0:T(8,128)S(1)}, u32[]{:S(2)}, u32[]{:S(2)}) %collective-permute-start.22) | collective-permute-done | bytes 139296 | tf_op jit(solution)/shard_map/ppermute | solution.py:352
  55.4 0.4 collective-permute-start.23
  55.8 5.2 %collective-permute-done.23 = f32[136,128]{1,0:T(8,128)S(1)} collective-permute-done((f32[136,128]{1,0:T(8,128)S(1)}, f32[136,128]{1,0:T(8,128)S(1)}, u32[]{:S(2)}, u32[]{:S(2)}) %collective-permute-start.23) | collective-permute-done | bytes 69664 | tf_op jit(solution)/shard_map/ppermute | solution.py:352
  61.0 3.1 %collective-permute-start.24 = (f32[128,128]{1,0:T(8,128)S(1)}, f32[128,128]{1,0:T(8,128)S(1)}, u32[]{:S(2)}, u32[]{:S(2)}) collective-permute-start(f32[128,128]{1,0:T(8,128)S(1)} %slice.318), channel_id=1, source_target_pairs={{0,1},{1,0},{2,17},{3,16},{4,33},{5,32},{6,49},{7,48},{8,65},{9,64... | collective-permute-start | bytes 196616 | tf_op jit(solution)/shard_map/ppermute | solution.py:352
  64.2 5.4 %collective-permute-done.24.theirs = f32[128,128]{1,0:T(8,128)S(1)} collective-permute-done((f32[128,128]{1,0:T(8,128)S(1)}, f32[128,128]{1,0:T(8,128)S(1)}, u32[]{:S(2)}, u32[]{:S(2)}) %collective-permute-start.24) | collective-permute-done | bytes 65568 | tf_op jit(solution)/shard_map/ppermute | solution.py:352
  69.6 0.7 finish.1
  (36 shorter events, 0.8 us)
Async XLA Ops:
  12.3 2.4 %collective-permute-start = (f32[64,24,128]{2,1,0:T(8,128)S(1)}, f32[64,24,128]{2,1,0:T(8,128)S(1)}, u32[]{:S(2)}, u32[]{:S(2)}) collective-permute-start(f32[64,24,128]{2,1,0:T(8,128)S(1)} %get-tuple-element.35), channel_id=1, source_target_pairs={{0,16},{1,17},{2,18},{3,19},{4,20},{5,21},{6,22},{7,23},{8,24},{9,... | collective-permute-start | bytes 2359304 | tf_op jit(solution)/shard_map/ppermute | solution.py:352
  12.4 3.4 %collective-permute-start.3 = (f32[64,24,128]{2,1,0:T(8,128)S(1)}, f32[64,24,128]{2,1,0:T(8,128)S(1)}, u32[]{:S(2)}, u32[]{:S(2)}) collective-permute-start(f32[64,24,128]{2,1,0:T(8,128)S(1)} %get-tuple-element.39), channel_id=1, source_target_pairs={{0,16},{1,17},{2,18},{3,19},{4,20},{5,21},{6,22},{7,23},{8,24},{9,... | collective-permute-start | bytes 2359304 | tf_op jit(solution)/shard_map/ppermute | solution.py:352
  12.9 4.0 %collective-permute-start.4 = (f32[64,24,128]{2,1,0:T(8,128)S(1)}, f32[64,24,128]{2,1,0:T(8,128)S(1)}, u32[]{:S(2)}, u32[]{:S(2)}) collective-permute-start(f32[64,24,128]{2,1,0:T(8,128)S(1)} %get-tuple-element.42), channel_id=1, source_target_pairs={{0,16},{1,17},{2,18},{3,19},{4,20},{5,21},{6,22},{7,23},{8,24},{9,... | collective-permute-start | bytes 2359304 | tf_op jit(solution)/shard_map/ppermute | solution.py:352
  12.9 5.4 %collective-permute-start.2 = (f32[64,32,128]{2,1,0:T(8,128)S(1)}, f32[64,32,128]{2,1,0:T(8,128)S(1)}, u32[]{:S(2)}, u32[]{:S(2)}) collective-permute-start(f32[64,32,128]{2,1,0:T(8,128)S(1)} %get-tuple-element.37), channel_id=1, source_target_pairs={{0,16},{1,17},{2,18},{3,19},{4,20},{5,21},{6,22},{7,23},{8,24},{9,... | collective-permute-start | bytes 3145736 | tf_op jit(solution)/shard_map/ppermute | solution.py:352
  13.4 6.5 %collective-permute-start.6 = (f32[64,32,128]{2,1,0:T(8,128)S(1)}, f32[64,32,128]{2,1,0:T(8,128)S(1)}, u32[]{:S(2)}, u32[]{:S(2)}) collective-permute-start(f32[64,32,128]{2,1,0:T(8,128)S(1)} %get-tuple-element.47), channel_id=1, source_target_pairs={{0,16},{1,17},{2,18},{3,19},{4,20},{5,21},{6,22},{7,23},{8,24},{9,... | collective-permute-start | bytes 3145736 | tf_op jit(solution)/shard_map/ppermute | solution.py:352
  14.7 7.9 %collective-permute-start.1 = (f32[1,2,2,8,24,128]{5,4,3,2,1,0:T(8,128)S(1)}, f32[1,2,2,8,24,128]{5,4,3,2,1,0:T(8,128)S(1)}, u32[]{:S(2)}, u32[]{:S(2)}) collective-permute-start(f32[1,2,2,8,24,128]{5,4,3,2,1,0:T(8,128)S(1)} %get-tuple-element.83), channel_id=1, source_target_pairs={{0,32},{1,33},{2,34},{3,35},{4,36},{5,37},{6,38},{7,39},{8,40},{9,... | collective-permute-start | bytes 1179656 | tf_op jit(solution)/shard_map/ppermute | solution.py:352
  15.8 7.9 %collective-permute-start.10 = (f32[2,1,2,8,24,128]{5,4,3,2,1,0:T(8,128)S(1)}, f32[2,1,2,8,24,128]{5,4,3,2,1,0:T(8,128)S(1)}, u32[]{:S(2)}, u32[]{:S(2)}) collective-permute-start(f32[2,1,2,8,24,128]{5,4,3,2,1,0:T(8,128)S(1)} %get-tuple-element.66), channel_id=1, source_target_pairs={{0,4},{1,5},{2,6},{3,7},{4,0},{5,1},{6,2},{7,3},{8,12},{9,13},{10,... | collective-permute-start | bytes 1179656 | tf_op jit(solution)/shard_map/ppermute | solution.py:352
  17.0 7.9 %collective-permute-start.9 = (f32[2,2,1,8,24,128]{5,4,3,2,1,0:T(8,128)S(1)}, f32[2,2,1,8,24,128]{5,4,3,2,1,0:T(8,128)S(1)}, u32[]{:S(2)}, u32[]{:S(2)}) collective-permute-start(f32[2,2,1,8,24,128]{5,4,3,2,1,0:T(8,128)S(1)} %get-tuple-element.68), channel_id=1, source_target_pairs={{0,1},{1,0},{2,3},{3,2},{4,5},{5,4},{6,7},{7,6},{8,9},{9,8},{10,11... | collective-permute-start | bytes 1179656 | tf_op jit(solution)/shard_map/ppermute | solution.py:352
  18.6 10.7 %collective-permute-start.8 = (f32[2,1,2,8,32,128]{5,4,3,2,1,0:T(8,128)S(1)}, f32[2,1,2,8,32,128]{5,4,3,2,1,0:T(8,128)S(1)}, u32[]{:S(2)}, u32[]{:S(2)}) collective-permute-start(f32[2,1,2,8,32,128]{5,4,3,2,1,0:T(8,128)S(1)} %get-tuple-element.64), channel_id=1, source_target_pairs={{0,4},{1,5},{2,6},{3,7},{4,0},{5,1},{6,2},{7,3},{8,12},{9,13},{10,... | collective-permute-start | bytes 1572872 | tf_op jit(solution)/shard_map/ppermute | solution.py:352
  20.1 9.4 %collective-permute-start.7 = (f32[1,2,2,8,32,128]{5,4,3,2,1,0:T(8,128)S(1)}, f32[1,2,2,8,32,128]{5,4,3,2,1,0:T(8,128)S(1)}, u32[]{:S(2)}, u32[]{:S(2)}) collective-permute-start(f32[1,2,2,8,32,128]{5,4,3,2,1,0:T(8,128)S(1)} %get-tuple-element.73), channel_id=1, source_target_pairs={{0,32},{1,33},{2,34},{3,35},{4,36},{5,37},{6,38},{7,39},{8,40},{9,... | collective-permute-start | bytes 1572872 | tf_op jit(solution)/shard_map/ppermute | solution.py:352
  22.6 8.8 %collective-permute-start.5 = (f32[1,1,2,8,24,128]{5,4,3,2,1,0:T(8,128)S(1)}, f32[1,1,2,8,24,128]{5,4,3,2,1,0:T(8,128)S(1)}, u32[]{:S(2)}, u32[]{:S(2)}) collective-permute-start(f32[1,1,2,8,24,128]{5,4,3,2,1,0:T(8,128)S(1)} %get-tuple-element.81), channel_id=1, source_target_pairs={{0,4},{1,5},{2,6},{3,7},{4,0},{5,1},{6,2},{7,3},{8,12},{9,13},{10,... | collective-permute-start | bytes 589832 | tf_op jit(solution)/shard_map/ppermute | solution.py:352
  23.7 8.1 %collective-permute-start.15 = (f32[2,1,1,8,24,128]{5,4,3,2,1,0:T(8,128)S(1)}, f32[2,1,1,8,24,128]{5,4,3,2,1,0:T(8,128)S(1)}, u32[]{:S(2)}, u32[]{:S(2)}) collective-permute-start(f32[2,1,1,8,24,128]{5,4,3,2,1,0:T(8,128)S(1)} %get-tuple-element.78), channel_id=1, source_target_pairs={{0,1},{1,0},{2,3},{3,2},{4,5},{5,4},{6,7},{7,6},{8,9},{9,8},{10,11... | collective-permute-start | bytes 589832 | tf_op jit(solution)/shard_map/ppermute | solution.py:352
  24.9 8.1 %collective-permute-start.14 = (f32[1,2,1,8,24,128]{5,4,3,2,1,0:T(8,128)S(1)}, f32[1,2,1,8,24,128]{5,4,3,2,1,0:T(8,128)S(1)}, u32[]{:S(2)}, u32[]{:S(2)}) collective-permute-start(f32[1,2,1,8,24,128]{5,4,3,2,1,0:T(8,128)S(1)} %get-tuple-element.80), channel_id=1, source_target_pairs={{0,32},{1,33},{2,34},{3,35},{4,36},{5,37},{6,38},{7,39},{8,40},{9,... | collective-permute-start | bytes 589832 | tf_op jit(solution)/shard_map/ppermute | solution.py:352
  29.4 6.5 %collective-permute-start.13 = (f32[2,1,1,8,32,128]{5,4,3,2,1,0:T(8,128)S(1)}, f32[2,1,1,8,32,128]{5,4,3,2,1,0:T(8,128)S(1)}, u32[]{:S(2)}, u32[]{:S(2)}) collective-permute-start(f32[2,1,1,8,32,128]{5,4,3,2,1,0:T(8,128)S(1)} %get-tuple-element.70), channel_id=1, source_target_pairs={{0,1},{1,0},{2,3},{3,2},{4,5},{5,4},{6,7},{7,6},{8,9},{9,8},{10,11... | collective-permute-start | bytes 786440 | tf_op jit(solution)/shard_map/ppermute | solution.py:352
  29.6 7.4 %collective-permute-start.12 = (f32[1,1,2,8,32,128]{5,4,3,2,1,0:T(8,128)S(1)}, f32[1,1,2,8,32,128]{5,4,3,2,1,0:T(8,128)S(1)}, u32[]{:S(2)}, u32[]{:S(2)}) collective-permute-start(f32[1,1,2,8,32,128]{5,4,3,2,1,0:T(8,128)S(1)} %get-tuple-element.72), channel_id=1, source_target_pairs={{0,4},{1,5},{2,6},{3,7},{4,0},{5,1},{6,2},{7,3},{8,12},{9,13},{10,... | collective-permute-start | bytes 786440 | tf_op jit(solution)/shard_map/ppermute | solution.py:352
  31.4 6.7 %collective-permute-start.11 = (f32[1,1,1,8,24,128]{5,4,3,2,1,0:T(8,128)S(1)}, f32[1,1,1,8,24,128]{5,4,3,2,1,0:T(8,128)S(1)}, u32[]{:S(2)}, u32[]{:S(2)}) collective-permute-start(f32[1,1,1,8,24,128]{5,4,3,2,1,0:T(8,128)S(1)} %slice_add_fusion.28), channel_id=1, source_target_pairs={{0,1},{1,0},{2,3},{3,2},{4,5},{5,4},{6,7},{7,6},{8,9},{9,8},{10,11... | collective-permute-start | bytes 294920 | tf_op jit(solution)/shard_map/ppermute | solution.py:352
  31.8 6.3 %collective-permute-start.16 = (f32[1,1,1,8,24,128]{5,4,3,2,1,0:T(8,128)S(1)}, f32[1,1,1,8,24,128]{5,4,3,2,1,0:T(8,128)S(1)}, u32[]{:S(2)}, u32[]{:S(2)}) collective-permute-start(f32[1,1,1,8,24,128]{5,4,3,2,1,0:T(8,128)S(1)} %slice_add_fusion.26), channel_id=1, source_target_pairs={{0,32},{1,33},{2,34},{3,35},{4,36},{5,37},{6,38},{7,39},{8,40},{9,... | collective-permute-start | bytes 294920 | tf_op jit(solution)/shard_map/ppermute | solution.py:352
  33.0 5.2 %collective-permute-start.17 = (f32[1,1,1,8,24,128]{5,4,3,2,1,0:T(8,128)S(1)}, f32[1,1,1,8,24,128]{5,4,3,2,1,0:T(8,128)S(1)}, u32[]{:S(2)}, u32[]{:S(2)}) collective-permute-start(f32[1,1,1,8,24,128]{5,4,3,2,1,0:T(8,128)S(1)} %slice_add_fusion.27), channel_id=1, source_target_pairs={{0,4},{1,5},{2,6},{3,7},{4,0},{5,1},{6,2},{7,3},{8,12},{9,13},{10,... | collective-permute-start | bytes 294920 | tf_op jit(solution)/shard_map/ppermute | solution.py:352
  35.9 5.0 %collective-permute-start.19 = (f32[1,1,1,8,32,128]{5,4,3,2,1,0:T(8,128)S(1)}, f32[1,1,1,8,32,128]{5,4,3,2,1,0:T(8,128)S(1)}, u32[]{:S(2)}, u32[]{:S(2)}) collective-permute-start(f32[1,1,1,8,32,128]{5,4,3,2,1,0:T(8,128)S(1)} %slice_add_fusion.22), channel_id=1, source_target_pairs={{0,32},{1,33},{2,34},{3,35},{4,36},{5,37},{6,38},{7,39},{8,40},{9,... | collective-permute-start | bytes 393224 | tf_op jit(solution)/shard_map/ppermute | solution.py:352
  37.1 5.0 %collective-permute-start.18 = (f32[1,1,1,8,32,128]{5,4,3,2,1,0:T(8,128)S(1)}, f32[1,1,1,8,32,128]{5,4,3,2,1,0:T(8,128)S(1)}, u32[]{:S(2)}, u32[]{:S(2)}) collective-permute-start(f32[1,1,1,8,32,128]{5,4,3,2,1,0:T(8,128)S(1)} %slice_add_fusion.23), channel_id=1, source_target_pairs={{0,1},{1,0},{2,3},{3,2},{4,5},{5,4},{6,7},{7,6},{8,9},{9,8},{10,11... | collective-permute-start | bytes 393224 | tf_op jit(solution)/shard_map/ppermute | solution.py:352
  42.2 9.9 %collective-permute-start.20 = (f32[2,136,128]{2,1,0:T(8,128)S(1)}, f32[2,136,128]{2,1,0:T(8,128)S(1)}, u32[]{:S(2)}, u32[]{:S(2)}) collective-permute-start(f32[2,136,128]{2,1,0:T(8,128)S(1)} %get-tuple-element.87), channel_id=1, source_target_pairs={{0,108},{1,109},{2,110},{3,111},{4,104},{5,105},{6,106},{7,107},{8... | collective-permute-start | bytes 417800 | tf_op jit(solution)/shard_map/ppermute | solution.py:352
  49.1 6.3 %collective-permute-start.22 = (f32[2,136,128]{2,1,0:T(8,128)S(1)}, f32[2,136,128]{2,1,0:T(8,128)S(1)}, u32[]{:S(2)}, u32[]{:S(2)}) collective-permute-start(f32[2,136,128]{2,1,0:T(8,128)S(1)} %get-tuple-element.88), channel_id=1, source_target_pairs={{0,12},{1,13},{2,14},{3,15},{4,8},{5,9},{6,10},{7,11},{8,4},{9,5},... | collective-permute-start | bytes 417800 | tf_op jit(solution)/shard_map/ppermute | solution.py:352
  49.1 6.3 %collective-permute-start.21 = (f32[2,136,128]{2,1,0:T(8,128)S(1)}, f32[2,136,128]{2,1,0:T(8,128)S(1)}, u32[]{:S(2)}, u32[]{:S(2)}) collective-permute-start(f32[2,136,128]{2,1,0:T(8,128)S(1)} %get-tuple-element.89), channel_id=1, source_target_pairs={{0,96},{1,97},{2,98},{3,99},{4,100},{5,101},{6,102},{7,103},{8,104... | collective-permute-start | bytes 417800 | tf_op jit(solution)/shard_map/ppermute | solution.py:352
  55.4 5.6 %collective-permute-start.23 = (f32[136,128]{1,0:T(8,128)S(1)}, f32[136,128]{1,0:T(8,128)S(1)}, u32[]{:S(2)}, u32[]{:S(2)}) collective-permute-start(f32[136,128]{1,0:T(8,128)S(1)} %slice_bitcast_fusion.4), channel_id=1, source_target_pairs={{0,3},{1,2},{2,1},{3,0},{4,7},{5,6},{6,5},{7,4},{8,11},{9,10},{10,... | collective-permute-start | bytes 208904 | tf_op jit(solution)/shard_map/ppermute | solution.py:352
  61.0 8.6 %collective-permute-start.24 = (f32[128,128]{1,0:T(8,128)S(1)}, f32[128,128]{1,0:T(8,128)S(1)}, u32[]{:S(2)}, u32[]{:S(2)}) collective-permute-start(f32[128,128]{1,0:T(8,128)S(1)} %slice.318), channel_id=1, source_target_pairs={{0,1},{1,0},{2,17},{3,16},{4,33},{5,32},{6,49},{7,48},{8,65},{9,64... | collective-permute-start | bytes 196616 | tf_op jit(solution)/shard_map/ppermute | solution.py:352

commit v4 on v3

--- a/solution.py
+++ b/solution.py
@@ -115,6 +115,8 @@
     ]
     for copy in small:
         copy.start()
+    for ref in (*keeps, *sends, diag):
+        ref[...] = jnp.zeros_like(ref)
     small[0].wait()
     for b in range(OBLK):
         coeff_copy(b).start()
@@ -151,8 +153,6 @@
         info[2 * LIST + r] = row_place(name, 1, my_z, my_y)
         info[3 * LIST + r] = col_place(name >> 1, my_x)
 
-    for ref in (*keeps, *sends, diag):
-        ref[...] = jnp.zeros_like(ref)
     for b in range(OBLK):
         coeff_copy(b).wait()
 

time: 71.2 us -> 69.2 us (0.972)
  starting transfers between devices: 21 us -> 35.2 us
  waiting for transfers between devices: 34.6 us -> 23.1 us
  Pallas kernels: 12.9 us -> 8.65 us
    ppermute x25, starting transfers between devices: 21 us -> 35.2 us  [swap(): return lax.ppermute(array, AXES, pairs)]
    ppermute x25, waiting for transfers between devices: 34.6 us -> 23.1 us  [swap(): return lax.ppermute(array, AXES, pairs)]
    pallas_call x1, Pallas kernels: 12.3 us -> 7.97 us  [partial_sums(): pl.pallas_call(partial_kernel, out_shape=shares + shares, in_specs=[hbm]...]
  transfers between devices with their start and end apart: 25 -> 25, of which waited for: 17 -> 15; matrix products, arithmetic and copies ran while one was open for 2% -> 2% of each run, Pallas kernels for 0% -> 0%
where the time goes in v4:
time: 69.2 us; the launch traced here: 68.6 us
  starting transfers between devices  35.2 us (51%)
  waiting for transfers between devices  23.1 us (33%)
  Pallas kernels  8.65 us (12%)
  other arithmetic  1.19 us (2%)
    ppermute x25, starting transfers between devices, swap(): return lax.ppermute(array, AXES, pairs)  35.2 us
    ppermute x25, waiting for transfers between devices, swap(): return lax.ppermute(array, AXES, pairs)  23.1 us
    pallas_call x1, Pallas kernels, partial_sums(): pl.pallas_call(partial_kernel, out_shape=shares + shares, in_specs=[hbm]...  7.97 us
  transfers between devices with their start and end apart: 25, of which 15 were waited for; matrix products, arithmetic and copies ran while one was open for 2% of the time, Pallas kernels for 0%

profile of v4, /device:TPU:6, one launch (start us, length us, event | category | flops | bytes accessed | tf_op | source)
XLA Modules:
  0.0 68.6 jit_solution(6620191775027542437)
XLA Ops:
  0.0 8.0 %partial_sums.1 = (f32[64,24,128]{2,1,0:T(8,128)S(1)}, f32[64,24,128]{2,1,0:T(8,128)S(1)}, f32[64,24,128]{2,1,0:T(8,128)S(1)}, f32[64,32,128]{2,1,0:T(8,128)S(1)...) custom-call(s32[16]{0:T(128)} %mu_hbm.1, ...), custom_call_target="tpu_custom_call" | custom-call | flops 8000000000 | bytes 5242880 | tf_op jit(solution)/shard_map/partial_sums/pallas_call | solution.py:273
  8.0 2.0 %collective-permute-start = (f32[64,24,128]{2,1,0:T(8,128)S(1)}, f32[64,24,128]{2,1,0:T(8,128)S(1)}, u32[]{:S(2)}, u32[]{:S(2)}) collective-permute-start(f32[64,24,128]{2,1,0:T(8,128)S(1)} %get-tuple-element.35), channel_id=1, source_target_pairs={{0,16},{1,17},{2,18},{3,19},{4,20},{5,21},{6,22},{7,23},{8,24},{9,... | collective-permute-start | bytes 2359304 | tf_op jit(solution)/shard_map/ppermute | solution.py:352
  10.0 0.1 collective-permute-start.3
  10.1 0.4 collective-permute-start.4
  10.5 0.1 collective-permute-start.2
  10.6 0.4 collective-permute-start.6
  11.1 0.8 %collective-permute-done = f32[64,24,128]{2,1,0:T(8,128)S(1)} collective-permute-done((f32[64,24,128]{2,1,0:T(8,128)S(1)}, f32[64,24,128]{2,1,0:T(8,128)S(1)}, u32[]{:S(2)}, u32[]{:S(2)}) %collective-permute-start) | collective-permute-done | bytes 786464 | tf_op jit(solution)/shard_map/ppermute | solution.py:352
  11.9 0.1 slice_add_fusion.8
  12.0 0.1 collective-permute-start.1
  12.1 0.9 %collective-permute-done.3 = f32[64,24,128]{2,1,0:T(8,128)S(1)} collective-permute-done((f32[64,24,128]{2,1,0:T(8,128)S(1)}, f32[64,24,128]{2,1,0:T(8,128)S(1)}, u32[]{:S(2)}, u32[]{:S(2)}) %collective-permute-start.3) | collective-permute-done | bytes 786464 | tf_op jit(solution)/shard_map/ppermute | solution.py:352
  13.0 0.1 slice_add_fusion.4
  13.1 4.4 %collective-permute-start.10 = (f32[2,1,2,8,24,128]{5,4,3,2,1,0:T(8,128)S(1)}, f32[2,1,2,8,24,128]{5,4,3,2,1,0:T(8,128)S(1)}, u32[]{:S(2)}, u32[]{:S(2)}) collective-permute-start(f32[2,1,2,8,24,128]{5,4,3,2,1,0:T(8,128)S(1)} %get-tuple-element.66), channel_id=1, source_target_pairs={{0,4},{1,5},{2,6},{3,7},{4,0},{5,1},{6,2},{7,3},{8,12},{9,13},{10,... | collective-permute-start | bytes 1179656 | tf_op jit(solution)/shard_map/ppermute | solution.py:352
  17.5 0.1 slice_add_fusion.5
  17.6 0.9 %collective-permute-start.9 = (f32[2,2,1,8,24,128]{5,4,3,2,1,0:T(8,128)S(1)}, f32[2,2,1,8,24,128]{5,4,3,2,1,0:T(8,128)S(1)}, u32[]{:S(2)}, u32[]{:S(2)}) collective-permute-start(f32[2,2,1,8,24,128]{5,4,3,2,1,0:T(8,128)S(1)} %get-tuple-element.68), channel_id=1, source_target_pairs={{0,1},{1,0},{2,3},{3,2},{4,5},{5,4},{6,7},{7,6},{8,9},{9,8},{10,11... | collective-permute-start | bytes 1179656 | tf_op jit(solution)/shard_map/ppermute | solution.py:352
  18.6 0.2 slice_add_fusion
  18.8 1.2 %collective-permute-start.8 = (f32[2,1,2,8,32,128]{5,4,3,2,1,0:T(8,128)S(1)}, f32[2,1,2,8,32,128]{5,4,3,2,1,0:T(8,128)S(1)}, u32[]{:S(2)}, u32[]{:S(2)}) collective-permute-start(f32[2,1,2,8,32,128]{5,4,3,2,1,0:T(8,128)S(1)} %get-tuple-element.64), channel_id=1, source_target_pairs={{0,4},{1,5},{2,6},{3,7},{4,0},{5,1},{6,2},{7,3},{8,12},{9,13},{10,... | collective-permute-start | bytes 1572872 | tf_op jit(solution)/shard_map/ppermute | solution.py:352
  19.9 0.2 slice_add_fusion.2
  20.1 1.4 %collective-permute-start.7 = (f32[1,2,2,8,32,128]{5,4,3,2,1,0:T(8,128)S(1)}, f32[1,2,2,8,32,128]{5,4,3,2,1,0:T(8,128)S(1)}, u32[]{:S(2)}, u32[]{:S(2)}) collective-permute-start(f32[1,2,2,8,32,128]{5,4,3,2,1,0:T(8,128)S(1)} %get-tuple-element.73), channel_id=1, source_target_pairs={{0,32},{1,33},{2,34},{3,35},{4,36},{5,37},{6,38},{7,39},{8,40},{9,... | collective-permute-start | bytes 1572872 | tf_op jit(solution)/shard_map/ppermute | solution.py:352
  21.6 1.7 %collective-permute-start.5 = (f32[1,1,2,8,24,128]{5,4,3,2,1,0:T(8,128)S(1)}, f32[1,1,2,8,24,128]{5,4,3,2,1,0:T(8,128)S(1)}, u32[]{:S(2)}, u32[]{:S(2)}) collective-permute-start(f32[1,1,2,8,24,128]{5,4,3,2,1,0:T(8,128)S(1)} %get-tuple-element.81), channel_id=1, source_target_pairs={{0,4},{1,5},{2,6},{3,7},{4,0},{5,1},{6,2},{7,3},{8,12},{9,13},{10,... | collective-permute-start | bytes 589832 | tf_op jit(solution)/shard_map/ppermute | solution.py:352
  23.3 2.0 %collective-permute-start.15 = (f32[2,1,1,8,24,128]{5,4,3,2,1,0:T(8,128)S(1)}, f32[2,1,1,8,24,128]{5,4,3,2,1,0:T(8,128)S(1)}, u32[]{:S(2)}, u32[]{:S(2)}) collective-permute-start(f32[2,1,1,8,24,128]{5,4,3,2,1,0:T(8,128)S(1)} %get-tuple-element.78), channel_id=1, source_target_pairs={{0,1},{1,0},{2,3},{3,2},{4,5},{5,4},{6,7},{7,6},{8,9},{9,8},{10,11... | collective-permute-start | bytes 589832 | tf_op jit(solution)/shard_map/ppermute | solution.py:352
  25.3 0.2 collective-permute-done.9
  25.5 1.0 %collective-permute-start.14 = (f32[1,2,1,8,24,128]{5,4,3,2,1,0:T(8,128)S(1)}, f32[1,2,1,8,24,128]{5,4,3,2,1,0:T(8,128)S(1)}, u32[]{:S(2)}, u32[]{:S(2)}) collective-permute-start(f32[1,2,1,8,24,128]{5,4,3,2,1,0:T(8,128)S(1)} %get-tuple-element.80), channel_id=1, source_target_pairs={{0,32},{1,33},{2,34},{3,35},{4,36},{5,37},{6,38},{7,39},{8,40},{9,... | collective-permute-start | bytes 589832 | tf_op jit(solution)/shard_map/ppermute | solution.py:352
  26.6 2.3 %collective-permute-done.8 = f32[2,1,2,8,32,128]{5,4,3,2,1,0:T(8,128)S(1)} collective-permute-done((f32[2,1,2,8,32,128]{5,4,3,2,1,0:T(8,128)S(1)}, f32[2,1,2,8,32,128]{5,4,3,2,1,0:T(8,128)S(1)}, u32[]{:S(2)}, u32[]{:S(2)}) %collective-permute-start.8) | collective-permute-done | bytes 524320 | tf_op jit(solution)/shard_map/ppermute | solution.py:352
  28.9 0.1 slice_add_fusion.10
  29.0 2.0 %collective-permute-start.13 = (f32[2,1,1,8,32,128]{5,4,3,2,1,0:T(8,128)S(1)}, f32[2,1,1,8,32,128]{5,4,3,2,1,0:T(8,128)S(1)}, u32[]{:S(2)}, u32[]{:S(2)}) collective-permute-start(f32[2,1,1,8,32,128]{5,4,3,2,1,0:T(8,128)S(1)} %get-tuple-element.70), channel_id=1, source_target_pairs={{0,1},{1,0},{2,3},{3,2},{4,5},{5,4},{6,7},{7,6},{8,9},{9,8},{10,11... | collective-permute-start | bytes 786440 | tf_op jit(solution)/shard_map/ppermute | solution.py:352
  31.0 0.1 slice_add_fusion.11
  31.1 0.2 collective-permute-start.12
  31.3 2.1 %collective-permute-start.11 = (f32[1,1,1,8,24,128]{5,4,3,2,1,0:T(8,128)S(1)}, f32[1,1,1,8,24,128]{5,4,3,2,1,0:T(8,128)S(1)}, u32[]{:S(2)}, u32[]{:S(2)}) collective-permute-start(f32[1,1,1,8,24,128]{5,4,3,2,1,0:T(8,128)S(1)} %slice_add_fusion.28), channel_id=1, source_target_pairs={{0,1},{1,0},{2,3},{3,2},{4,5},{5,4},{6,7},{7,6},{8,9},{9,8},{10,11... | collective-permute-start | bytes 294920 | tf_op jit(solution)/shard_map/ppermute | solution.py:352
  33.4 1.0 %collective-permute-start.16 = (f32[1,1,1,8,24,128]{5,4,3,2,1,0:T(8,128)S(1)}, f32[1,1,1,8,24,128]{5,4,3,2,1,0:T(8,128)S(1)}, u32[]{:S(2)}, u32[]{:S(2)}) collective-permute-start(f32[1,1,1,8,24,128]{5,4,3,2,1,0:T(8,128)S(1)} %slice_add_fusion.26), channel_id=1, source_target_pairs={{0,32},{1,33},{2,34},{3,35},{4,36},{5,37},{6,38},{7,39},{8,40},{9,... | collective-permute-start | bytes 294920 | tf_op jit(solution)/shard_map/ppermute | solution.py:352
  34.5 0.1 collective-permute-start.17
  34.6 0.9 %collective-permute-done.13 = f32[2,1,1,8,32,128]{5,4,3,2,1,0:T(8,128)S(1)} collective-permute-done((f32[2,1,1,8,32,128]{5,4,3,2,1,0:T(8,128)S(1)}, f32[2,1,1,8,32,128]{5,4,3,2,1,0:T(8,128)S(1)}, u32[]{:S(2)}, u32[]{:S(2)}) %collective-permute-start.13) | collective-permute-done | bytes 262176 | tf_op jit(solution)/shard_map/ppermute | solution.py:352
  35.5 1.0 %collective-permute-start.19 = (f32[1,1,1,8,32,128]{5,4,3,2,1,0:T(8,128)S(1)}, f32[1,1,1,8,32,128]{5,4,3,2,1,0:T(8,128)S(1)}, u32[]{:S(2)}, u32[]{:S(2)}) collective-permute-start(f32[1,1,1,8,32,128]{5,4,3,2,1,0:T(8,128)S(1)} %slice_add_fusion.22), channel_id=1, source_target_pairs={{0,32},{1,33},{2,34},{3,35},{4,36},{5,37},{6,38},{7,39},{8,40},{9,... | collective-permute-start | bytes 393224 | tf_op jit(solution)/shard_map/ppermute | solution.py:352
  36.5 1.0 %collective-permute-done.12 = f32[1,1,2,8,32,128]{5,4,3,2,1,0:T(8,128)S(1)} collective-permute-done((f32[1,1,2,8,32,128]{5,4,3,2,1,0:T(8,128)S(1)}, f32[1,1,2,8,32,128]{5,4,3,2,1,0:T(8,128)S(1)}, u32[]{:S(2)}, u32[]{:S(2)}) %collective-permute-start.12) | collective-permute-done | bytes 262176 | tf_op jit(solution)/shard_map/ppermute | solution.py:352
  37.6 1.1 %collective-permute-start.18 = (f32[1,1,1,8,32,128]{5,4,3,2,1,0:T(8,128)S(1)}, f32[1,1,1,8,32,128]{5,4,3,2,1,0:T(8,128)S(1)}, u32[]{:S(2)}, u32[]{:S(2)}) collective-permute-start(f32[1,1,1,8,32,128]{5,4,3,2,1,0:T(8,128)S(1)} %slice_add_fusion.23), channel_id=1, source_target_pairs={{0,1},{1,0},{2,3},{3,2},{4,5},{5,4},{6,7},{7,6},{8,9},{9,8},{10,11... | collective-permute-start | bytes 393224 | tf_op jit(solution)/shard_map/ppermute | solution.py:352
  38.7 0.5 collective-permute-done.17
  39.2 1.3 %collective-permute-done.19 = f32[1,1,1,8,32,128]{5,4,3,2,1,0:T(8,128)S(1)} collective-permute-done((f32[1,1,1,8,32,128]{5,4,3,2,1,0:T(8,128)S(1)}, f32[1,1,1,8,32,128]{5,4,3,2,1,0:T(8,128)S(1)}, u32[]{:S(2)}, u32[]{:S(2)}) %collective-permute-start.19) | collective-permute-done | bytes 131104 | tf_op jit(solution)/shard_map/ppermute | solution.py:352
  40.6 2.0 %collective-permute-done.18 = f32[1,1,1,8,32,128]{5,4,3,2,1,0:T(8,128)S(1)} collective-permute-done((f32[1,1,1,8,32,128]{5,4,3,2,1,0:T(8,128)S(1)}, f32[1,1,1,8,32,128]{5,4,3,2,1,0:T(8,128)S(1)}, u32[]{:S(2)}, u32[]{:S(2)}) %collective-permute-start.18) | collective-permute-done | bytes 131104 | tf_op jit(solution)/shard_map/ppermute | solution.py:352
  42.7 2.7 %collective-permute-start.20 = (f32[2,136,128]{2,1,0:T(8,128)S(1)}, f32[2,136,128]{2,1,0:T(8,128)S(1)}, u32[]{:S(2)}, u32[]{:S(2)}) collective-permute-start(f32[2,136,128]{2,1,0:T(8,128)S(1)} %get-tuple-element.87), channel_id=1, source_target_pairs={{0,108},{1,109},{2,110},{3,111},{4,104},{5,105},{6,106},{7,107},{8... | collective-permute-start | bytes 417800 | tf_op jit(solution)/shard_map/ppermute | solution.py:352
  45.5 1.0 %collective-permute-start.22 = (f32[2,136,128]{2,1,0:T(8,128)S(1)}, f32[2,136,128]{2,1,0:T(8,128)S(1)}, u32[]{:S(2)}, u32[]{:S(2)}) collective-permute-start(f32[2,136,128]{2,1,0:T(8,128)S(1)} %get-tuple-element.88), channel_id=1, source_target_pairs={{0,12},{1,13},{2,14},{3,15},{4,8},{5,9},{6,10},{7,11},{8,4},{9,5},... | collective-permute-start | bytes 417800 | tf_op jit(solution)/shard_map/ppermute | solution.py:352
  46.5 2.6 %collective-permute-start.21 = (f32[2,136,128]{2,1,0:T(8,128)S(1)}, f32[2,136,128]{2,1,0:T(8,128)S(1)}, u32[]{:S(2)}, u32[]{:S(2)}) collective-permute-start(f32[2,136,128]{2,1,0:T(8,128)S(1)} %get-tuple-element.89), channel_id=1, source_target_pairs={{0,96},{1,97},{2,98},{3,99},{4,100},{5,101},{6,102},{7,103},{8,104... | collective-permute-start | bytes 417800 | tf_op jit(solution)/shard_map/ppermute | solution.py:352
  49.1 2.2 %collective-permute-done.20 = f32[2,136,128]{2,1,0:T(8,128)S(1)} collective-permute-done((f32[2,136,128]{2,1,0:T(8,128)S(1)}, f32[2,136,128]{2,1,0:T(8,128)S(1)}, u32[]{:S(2)}, u32[]{:S(2)}) %collective-permute-start.20) | collective-permute-done | bytes 139296 | tf_op jit(solution)/shard_map/ppermute | solution.py:352
  51.3 1.4 %collective-permute-done.22 = f32[2,136,128]{2,1,0:T(8,128)S(1)} collective-permute-done((f32[2,136,128]{2,1,0:T(8,128)S(1)}, f32[2,136,128]{2,1,0:T(8,128)S(1)}, u32[]{:S(2)}, u32[]{:S(2)}) %collective-permute-start.22) | collective-permute-done | bytes 139296 | tf_op jit(solution)/shard_map/ppermute | solution.py:352
  52.7 0.9 %collective-permute-done.21 = f32[2,136,128]{2,1,0:T(8,128)S(1)} collective-permute-done((f32[2,136,128]{2,1,0:T(8,128)S(1)}, f32[2,136,128]{2,1,0:T(8,128)S(1)}, u32[]{:S(2)}, u32[]{:S(2)}) %collective-permute-start.21) | collective-permute-done | bytes 139296 | tf_op jit(solution)/shard_map/ppermute | solution.py:352
  53.6 1.1 %collective-permute-start.23 = (f32[136,128]{1,0:T(8,128)S(1)}, f32[136,128]{1,0:T(8,128)S(1)}, u32[]{:S(2)}, u32[]{:S(2)}) collective-permute-start(f32[136,128]{1,0:T(8,128)S(1)} %slice_bitcast_fusion.4), channel_id=1, source_target_pairs={{0,3},{1,2},{2,1},{3,0},{4,7},{5,6},{6,5},{7,4},{8,11},{9,10},{10,... | collective-permute-start | bytes 208904 | tf_op jit(solution)/shard_map/ppermute | solution.py:352
  54.8 4.5 %collective-permute-done.23 = f32[136,128]{1,0:T(8,128)S(1)} collective-permute-done((f32[136,128]{1,0:T(8,128)S(1)}, f32[136,128]{1,0:T(8,128)S(1)}, u32[]{:S(2)}, u32[]{:S(2)}) %collective-permute-start.23) | collective-permute-done | bytes 69664 | tf_op jit(solution)/shard_map/ppermute | solution.py:352
  59.3 4.5 %collective-permute-start.24 = (f32[128,128]{1,0:T(8,128)S(1)}, f32[128,128]{1,0:T(8,128)S(1)}, u32[]{:S(2)}, u32[]{:S(2)}) collective-permute-start(f32[128,128]{1,0:T(8,128)S(1)} %slice.318), channel_id=1, source_target_pairs={{0,1},{1,0},{2,17},{3,16},{4,33},{5,32},{6,49},{7,48},{8,65},{9,64... | collective-permute-start | bytes 196616 | tf_op jit(solution)/shard_map/ppermute | solution.py:352
  63.8 4.1 %collective-permute-done.24.theirs = f32[128,128]{1,0:T(8,128)S(1)} collective-permute-done((f32[128,128]{1,0:T(8,128)S(1)}, f32[128,128]{1,0:T(8,128)S(1)}, u32[]{:S(2)}, u32[]{:S(2)}) %collective-permute-start.24) | collective-permute-done | bytes 65568 | tf_op jit(solution)/shard_map/ppermute | solution.py:352
  67.9 0.7 finish.1
  (36 shorter events, 0.7 us)
Async XLA Ops:
  8.0 3.9 %collective-permute-start = (f32[64,24,128]{2,1,0:T(8,128)S(1)}, f32[64,24,128]{2,1,0:T(8,128)S(1)}, u32[]{:S(2)}, u32[]{:S(2)}) collective-permute-start(f32[64,24,128]{2,1,0:T(8,128)S(1)} %get-tuple-element.35), channel_id=1, source_target_pairs={{0,16},{1,17},{2,18},{3,19},{4,20},{5,21},{6,22},{7,23},{8,24},{9,... | collective-permute-start | bytes 2359304 | tf_op jit(solution)/shard_map/ppermute | solution.py:352
  10.0 3.0 %collective-permute-start.3 = (f32[64,24,128]{2,1,0:T(8,128)S(1)}, f32[64,24,128]{2,1,0:T(8,128)S(1)}, u32[]{:S(2)}, u32[]{:S(2)}) collective-permute-start(f32[64,24,128]{2,1,0:T(8,128)S(1)} %get-tuple-element.39), channel_id=1, source_target_pairs={{0,16},{1,17},{2,18},{3,19},{4,20},{5,21},{6,22},{7,23},{8,24},{9,... | collective-permute-start | bytes 2359304 | tf_op jit(solution)/shard_map/ppermute | solution.py:352
  10.1 7.5 %collective-permute-start.4 = (f32[64,24,128]{2,1,0:T(8,128)S(1)}, f32[64,24,128]{2,1,0:T(8,128)S(1)}, u32[]{:S(2)}, u32[]{:S(2)}) collective-permute-start(f32[64,24,128]{2,1,0:T(8,128)S(1)} %get-tuple-element.42), channel_id=1, source_target_pairs={{0,16},{1,17},{2,18},{3,19},{4,20},{5,21},{6,22},{7,23},{8,24},{9,... | collective-permute-start | bytes 2359304 | tf_op jit(solution)/shard_map/ppermute | solution.py:352
  10.5 8.1 %collective-permute-start.2 = (f32[64,32,128]{2,1,0:T(8,128)S(1)}, f32[64,32,128]{2,1,0:T(8,128)S(1)}, u32[]{:S(2)}, u32[]{:S(2)}) collective-permute-start(f32[64,32,128]{2,1,0:T(8,128)S(1)} %get-tuple-element.37), channel_id=1, source_target_pairs={{0,16},{1,17},{2,18},{3,19},{4,20},{5,21},{6,22},{7,23},{8,24},{9,... | collective-permute-start | bytes 3145736 | tf_op jit(solution)/shard_map/ppermute | solution.py:352
  10.6 9.3 %collective-permute-start.6 = (f32[64,32,128]{2,1,0:T(8,128)S(1)}, f32[64,32,128]{2,1,0:T(8,128)S(1)}, u32[]{:S(2)}, u32[]{:S(2)}) collective-permute-start(f32[64,32,128]{2,1,0:T(8,128)S(1)} %get-tuple-element.47), channel_id=1, source_target_pairs={{0,16},{1,17},{2,18},{3,19},{4,20},{5,21},{6,22},{7,23},{8,24},{9,... | collective-permute-start | bytes 3145736 | tf_op jit(solution)/shard_map/ppermute | solution.py:352
  12.0 9.6 %collective-permute-start.1 = (f32[1,2,2,8,24,128]{5,4,3,2,1,0:T(8,128)S(1)}, f32[1,2,2,8,24,128]{5,4,3,2,1,0:T(8,128)S(1)}, u32[]{:S(2)}, u32[]{:S(2)}) collective-permute-start(f32[1,2,2,8,24,128]{5,4,3,2,1,0:T(8,128)S(1)} %get-tuple-element.83), channel_id=1, source_target_pairs={{0,32},{1,33},{2,34},{3,35},{4,36},{5,37},{6,38},{7,39},{8,40},{9,... | collective-permute-start | bytes 1179656 | tf_op jit(solution)/shard_map/ppermute | solution.py:352
  13.1 10.2 %collective-permute-start.10 = (f32[2,1,2,8,24,128]{5,4,3,2,1,0:T(8,128)S(1)}, f32[2,1,2,8,24,128]{5,4,3,2,1,0:T(8,128)S(1)}, u32[]{:S(2)}, u32[]{:S(2)}) collective-permute-start(f32[2,1,2,8,24,128]{5,4,3,2,1,0:T(8,128)S(1)} %get-tuple-element.66), channel_id=1, source_target_pairs={{0,4},{1,5},{2,6},{3,7},{4,0},{5,1},{6,2},{7,3},{8,12},{9,13},{10,... | collective-permute-start | bytes 1179656 | tf_op jit(solution)/shard_map/ppermute | solution.py:352
  17.6 7.9 %collective-permute-start.9 = (f32[2,2,1,8,24,128]{5,4,3,2,1,0:T(8,128)S(1)}, f32[2,2,1,8,24,128]{5,4,3,2,1,0:T(8,128)S(1)}, u32[]{:S(2)}, u32[]{:S(2)}) collective-permute-start(f32[2,2,1,8,24,128]{5,4,3,2,1,0:T(8,128)S(1)} %get-tuple-element.68), channel_id=1, source_target_pairs={{0,1},{1,0},{2,3},{3,2},{4,5},{5,4},{6,7},{7,6},{8,9},{9,8},{10,11... | collective-permute-start | bytes 1179656 | tf_op jit(solution)/shard_map/ppermute | solution.py:352
  18.8 10.2 %collective-permute-start.8 = (f32[2,1,2,8,32,128]{5,4,3,2,1,0:T(8,128)S(1)}, f32[2,1,2,8,32,128]{5,4,3,2,1,0:T(8,128)S(1)}, u32[]{:S(2)}, u32[]{:S(2)}) collective-permute-start(f32[2,1,2,8,32,128]{5,4,3,2,1,0:T(8,128)S(1)} %get-tuple-element.64), channel_id=1, source_target_pairs={{0,4},{1,5},{2,6},{3,7},{4,0},{5,1},{6,2},{7,3},{8,12},{9,13},{10,... | collective-permute-start | bytes 1572872 | tf_op jit(solution)/shard_map/ppermute | solution.py:352
  20.1 10.8 %collective-permute-start.7 = (f32[1,2,2,8,32,128]{5,4,3,2,1,0:T(8,128)S(1)}, f32[1,2,2,8,32,128]{5,4,3,2,1,0:T(8,128)S(1)}, u32[]{:S(2)}, u32[]{:S(2)}) collective-permute-start(f32[1,2,2,8,32,128]{5,4,3,2,1,0:T(8,128)S(1)} %get-tuple-element.73), channel_id=1, source_target_pairs={{0,32},{1,33},{2,34},{3,35},{4,36},{5,37},{6,38},{7,39},{8,40},{9,... | collective-permute-start | bytes 1572872 | tf_op jit(solution)/shard_map/ppermute | solution.py:352
  21.6 9.7 %collective-permute-start.5 = (f32[1,1,2,8,24,128]{5,4,3,2,1,0:T(8,128)S(1)}, f32[1,1,2,8,24,128]{5,4,3,2,1,0:T(8,128)S(1)}, u32[]{:S(2)}, u32[]{:S(2)}) collective-permute-start(f32[1,1,2,8,24,128]{5,4,3,2,1,0:T(8,128)S(1)} %get-tuple-element.81), channel_id=1, source_target_pairs={{0,4},{1,5},{2,6},{3,7},{4,0},{5,1},{6,2},{7,3},{8,12},{9,13},{10,... | collective-permute-start | bytes 589832 | tf_op jit(solution)/shard_map/ppermute | solution.py:352
  23.3 10.1 %collective-permute-start.15 = (f32[2,1,1,8,24,128]{5,4,3,2,1,0:T(8,128)S(1)}, f32[2,1,1,8,24,128]{5,4,3,2,1,0:T(8,128)S(1)}, u32[]{:S(2)}, u32[]{:S(2)}) collective-permute-start(f32[2,1,1,8,24,128]{5,4,3,2,1,0:T(8,128)S(1)} %get-tuple-element.78), channel_id=1, source_target_pairs={{0,1},{1,0},{2,3},{3,2},{4,5},{5,4},{6,7},{7,6},{8,9},{9,8},{10,11... | collective-permute-start | bytes 589832 | tf_op jit(solution)/shard_map/ppermute | solution.py:352
  25.5 8.9 %collective-permute-start.14 = (f32[1,2,1,8,24,128]{5,4,3,2,1,0:T(8,128)S(1)}, f32[1,2,1,8,24,128]{5,4,3,2,1,0:T(8,128)S(1)}, u32[]{:S(2)}, u32[]{:S(2)}) collective-permute-start(f32[1,2,1,8,24,128]{5,4,3,2,1,0:T(8,128)S(1)} %get-tuple-element.80), channel_id=1, source_target_pairs={{0,32},{1,33},{2,34},{3,35},{4,36},{5,37},{6,38},{7,39},{8,40},{9,... | collective-permute-start | bytes 589832 | tf_op jit(solution)/shard_map/ppermute | solution.py:352
  29.0 6.5 %collective-permute-start.13 = (f32[2,1,1,8,32,128]{5,4,3,2,1,0:T(8,128)S(1)}, f32[2,1,1,8,32,128]{5,4,3,2,1,0:T(8,128)S(1)}, u32[]{:S(2)}, u32[]{:S(2)}) collective-permute-start(f32[2,1,1,8,32,128]{5,4,3,2,1,0:T(8,128)S(1)} %get-tuple-element.70), channel_id=1, source_target_pairs={{0,1},{1,0},{2,3},{3,2},{4,5},{5,4},{6,7},{7,6},{8,9},{9,8},{10,11... | collective-permute-start | bytes 786440 | tf_op jit(solution)/shard_map/ppermute | solution.py:352
  31.1 6.5 %collective-permute-start.12 = (f32[1,1,2,8,32,128]{5,4,3,2,1,0:T(8,128)S(1)}, f32[1,1,2,8,32,128]{5,4,3,2,1,0:T(8,128)S(1)}, u32[]{:S(2)}, u32[]{:S(2)}) collective-permute-start(f32[1,1,2,8,32,128]{5,4,3,2,1,0:T(8,128)S(1)} %get-tuple-element.72), channel_id=1, source_target_pairs={{0,4},{1,5},{2,6},{3,7},{4,0},{5,1},{6,2},{7,3},{8,12},{9,13},{10,... | collective-permute-start | bytes 786440 | tf_op jit(solution)/shard_map/ppermute | solution.py:352
  31.3 7.3 %collective-permute-start.11 = (f32[1,1,1,8,24,128]{5,4,3,2,1,0:T(8,128)S(1)}, f32[1,1,1,8,24,128]{5,4,3,2,1,0:T(8,128)S(1)}, u32[]{:S(2)}, u32[]{:S(2)}) collective-permute-start(f32[1,1,1,8,24,128]{5,4,3,2,1,0:T(8,128)S(1)} %slice_add_fusion.28), channel_id=1, source_target_pairs={{0,1},{1,0},{2,3},{3,2},{4,5},{5,4},{6,7},{7,6},{8,9},{9,8},{10,11... | collective-permute-start | bytes 294920 | tf_op jit(solution)/shard_map/ppermute | solution.py:352
  33.4 5.3 %collective-permute-start.16 = (f32[1,1,1,8,24,128]{5,4,3,2,1,0:T(8,128)S(1)}, f32[1,1,1,8,24,128]{5,4,3,2,1,0:T(8,128)S(1)}, u32[]{:S(2)}, u32[]{:S(2)}) collective-permute-start(f32[1,1,1,8,24,128]{5,4,3,2,1,0:T(8,128)S(1)} %slice_add_fusion.26), channel_id=1, source_target_pairs={{0,32},{1,33},{2,34},{3,35},{4,36},{5,37},{6,38},{7,39},{8,40},{9,... | collective-permute-start | bytes 294920 | tf_op jit(solution)/shard_map/ppermute | solution.py:352
  34.5 4.7 %collective-permute-start.17 = (f32[1,1,1,8,24,128]{5,4,3,2,1,0:T(8,128)S(1)}, f32[1,1,1,8,24,128]{5,4,3,2,1,0:T(8,128)S(1)}, u32[]{:S(2)}, u32[]{:S(2)}) collective-permute-start(f32[1,1,1,8,24,128]{5,4,3,2,1,0:T(8,128)S(1)} %slice_add_fusion.27), channel_id=1, source_target_pairs={{0,4},{1,5},{2,6},{3,7},{4,0},{5,1},{6,2},{7,3},{8,12},{9,13},{10,... | collective-permute-start | bytes 294920 | tf_op jit(solution)/shard_map/ppermute | solution.py:352
  35.5 5.0 %collective-permute-start.19 = (f32[1,1,1,8,32,128]{5,4,3,2,1,0:T(8,128)S(1)}, f32[1,1,1,8,32,128]{5,4,3,2,1,0:T(8,128)S(1)}, u32[]{:S(2)}, u32[]{:S(2)}) collective-permute-start(f32[1,1,1,8,32,128]{5,4,3,2,1,0:T(8,128)S(1)} %slice_add_fusion.22), channel_id=1, source_target_pairs={{0,32},{1,33},{2,34},{3,35},{4,36},{5,37},{6,38},{7,39},{8,40},{9,... | collective-permute-start | bytes 393224 | tf_op jit(solution)/shard_map/ppermute | solution.py:352
  37.6 5.0 %collective-permute-start.18 = (f32[1,1,1,8,32,128]{5,4,3,2,1,0:T(8,128)S(1)}, f32[1,1,1,8,32,128]{5,4,3,2,1,0:T(8,128)S(1)}, u32[]{:S(2)}, u32[]{:S(2)}) collective-permute-start(f32[1,1,1,8,32,128]{5,4,3,2,1,0:T(8,128)S(1)} %slice_add_fusion.23), channel_id=1, source_target_pairs={{0,1},{1,0},{2,3},{3,2},{4,5},{5,4},{6,7},{7,6},{8,9},{9,8},{10,11... | collective-permute-start | bytes 393224 | tf_op jit(solution)/shard_map/ppermute | solution.py:352
  42.7 8.6 %collective-permute-start.20 = (f32[2,136,128]{2,1,0:T(8,128)S(1)}, f32[2,136,128]{2,1,0:T(8,128)S(1)}, u32[]{:S(2)}, u32[]{:S(2)}) collective-permute-start(f32[2,136,128]{2,1,0:T(8,128)S(1)} %get-tuple-element.87), channel_id=1, source_target_pairs={{0,108},{1,109},{2,110},{3,111},{4,104},{5,105},{6,106},{7,107},{8... | collective-permute-start | bytes 417800 | tf_op jit(solution)/shard_map/ppermute | solution.py:352
  45.5 7.2 %collective-permute-start.22 = (f32[2,136,128]{2,1,0:T(8,128)S(1)}, f32[2,136,128]{2,1,0:T(8,128)S(1)}, u32[]{:S(2)}, u32[]{:S(2)}) collective-permute-start(f32[2,136,128]{2,1,0:T(8,128)S(1)} %get-tuple-element.88), channel_id=1, source_target_pairs={{0,12},{1,13},{2,14},{3,15},{4,8},{5,9},{6,10},{7,11},{8,4},{9,5},... | collective-permute-start | bytes 417800 | tf_op jit(solution)/shard_map/ppermute | solution.py:352
  46.5 7.1 %collective-permute-start.21 = (f32[2,136,128]{2,1,0:T(8,128)S(1)}, f32[2,136,128]{2,1,0:T(8,128)S(1)}, u32[]{:S(2)}, u32[]{:S(2)}) collective-permute-start(f32[2,136,128]{2,1,0:T(8,128)S(1)} %get-tuple-element.89), channel_id=1, source_target_pairs={{0,96},{1,97},{2,98},{3,99},{4,100},{5,101},{6,102},{7,103},{8,104... | collective-permute-start | bytes 417800 | tf_op jit(solution)/shard_map/ppermute | solution.py:352
  53.6 5.6 %collective-permute-start.23 = (f32[136,128]{1,0:T(8,128)S(1)}, f32[136,128]{1,0:T(8,128)S(1)}, u32[]{:S(2)}, u32[]{:S(2)}) collective-permute-start(f32[136,128]{1,0:T(8,128)S(1)} %slice_bitcast_fusion.4), channel_id=1, source_target_pairs={{0,3},{1,2},{2,1},{3,0},{4,7},{5,6},{6,5},{7,4},{8,11},{9,10},{10,... | collective-permute-start | bytes 208904 | tf_op jit(solution)/shard_map/ppermute | solution.py:352
  59.3 8.6 %collective-permute-start.24 = (f32[128,128]{1,0:T(8,128)S(1)}, f32[128,128]{1,0:T(8,128)S(1)}, u32[]{:S(2)}, u32[]{:S(2)}) collective-permute-start(f32[128,128]{1,0:T(8,128)S(1)} %slice.318), channel_id=1, source_target_pairs={{0,1},{1,0},{2,17},{3,16},{4,33},{5,32},{6,49},{7,48},{8,65},{9,64... | collective-permute-start | bytes 196616 | tf_op jit(solution)/shard_map/ppermute | solution.py:352

commit v5 on v4

--- a/solution.py
+++ b/solution.py
@@ -21,7 +21,7 @@
 KERNEL_VMEM = 28 * 1024 * 1024
 LIST = 32
 UNROLL = 3
-STRIPS_ALWAYS = 4
+STRIPS_ALWAYS = 5
 PARTNERS = ((), (1,), (0,), (0, 1))
 
 

time: 69.2 us -> 69 us (level); the launches traced: 68.6 us -> 69.5 us
  Pallas kernels: 8.65 us -> 10.7 us
  waiting for transfers between devices: 23.1 us -> 21.3 us
  starting transfers between devices: 35.2 us -> 35.9 us
    pallas_call x1, Pallas kernels: 7.97 us -> 10 us  [partial_sums(): pl.pallas_call(partial_kernel, out_shape=shares + shares, in_specs=[hbm]...]
    ppermute x25, waiting for transfers between devices: 23.1 us -> 21.3 us  [swap(): return lax.ppermute(array, AXES, pairs)]
    ppermute x25, starting transfers between devices: 35.2 us -> 35.9 us  [swap(): return lax.ppermute(array, AXES, pairs)]
  transfers between devices with their start and end apart: 25 -> 25, of which waited for: 15 -> 12; matrix products, arithmetic and copies ran while one was open for 2% -> 2% of each run, Pallas kernels for 0% -> 0%
where the time goes in v5:
time: 69 us; the launch traced here: 69.5 us
  starting transfers between devices  35.9 us (52%)
  waiting for transfers between devices  21.3 us (31%)
  Pallas kernels  10.7 us (16%)
  other arithmetic  1.19 us (2%)
    ppermute x25, starting transfers between devices, swap(): return lax.ppermute(array, AXES, pairs)  35.9 us
    ppermute x25, waiting for transfers between devices, swap(): return lax.ppermute(array, AXES, pairs)  21.3 us
    pallas_call x1, Pallas kernels, partial_sums(): pl.pallas_call(partial_kernel, out_shape=shares + shares, in_specs=[hbm]...  10 us
  transfers between devices with their start and end apart: 25, of which 12 were waited for; matrix products, arithmetic and copies ran while one was open for 2% of the time, Pallas kernels for 0%

profile of v5, /device:TPU:6, one launch (start us, length us, event | category | flops | bytes accessed | tf_op | source)
XLA Modules:
  0.0 69.5 jit_solution(17323741531217040305)
XLA Ops:
  0.0 10.0 %partial_sums.1 = (f32[64,24,128]{2,1,0:T(8,128)S(1)}, f32[64,24,128]{2,1,0:T(8,128)S(1)}, f32[64,24,128]{2,1,0:T(8,128)S(1)}, f32[64,32,128]{2,1,0:T(8,128)S(1)...) custom-call(s32[16]{0:T(128)} %mu_hbm.1, ...), custom_call_target="tpu_custom_call" | custom-call | flops 8000000000 | bytes 5242880 | tf_op jit(solution)/shard_map/partial_sums/pallas_call | solution.py:273
  10.0 0.1 collective-permute-start
  10.1 0.5 collective-permute-start.3
  10.6 0.1 collective-permute-start.4
  10.7 0.4 collective-permute-start.2
  11.1 0.1 collective-permute-start.6
  11.2 0.1 fusion.9
  11.3 0.1 fusion.10
  11.4 1.0 %collective-permute-done = f32[64,24,128]{2,1,0:T(8,128)S(1)} collective-permute-done((f32[64,24,128]{2,1,0:T(8,128)S(1)}, f32[64,24,128]{2,1,0:T(8,128)S(1)}, u32[]{:S(2)}, u32[]{:S(2)}) %collective-permute-start) | collective-permute-done | bytes 786464 | tf_op jit(solution)/shard_map/ppermute | solution.py:352
  12.4 0.1 slice_add_fusion.8
  12.5 0.9 %collective-permute-start.1 = (f32[1,2,2,8,24,128]{5,4,3,2,1,0:T(8,128)S(1)}, f32[1,2,2,8,24,128]{5,4,3,2,1,0:T(8,128)S(1)}, u32[]{:S(2)}, u32[]{:S(2)}) collective-permute-start(f32[1,2,2,8,24,128]{5,4,3,2,1,0:T(8,128)S(1)} %get-tuple-element.83), channel_id=1, source_target_pairs={{0,32},{1,33},{2,34},{3,35},{4,36},{5,37},{6,38},{7,39},{8,40},{9,... | collective-permute-start | bytes 1179656 | tf_op jit(solution)/shard_map/ppermute | solution.py:352
  13.4 0.1 collective-permute-done.3
  13.5 0.1 slice_add_fusion.4
  13.6 1.8 %collective-permute-start.10 = (f32[2,1,2,8,24,128]{5,4,3,2,1,0:T(8,128)S(1)}, f32[2,1,2,8,24,128]{5,4,3,2,1,0:T(8,128)S(1)}, u32[]{:S(2)}, u32[]{:S(2)}) collective-permute-start(f32[2,1,2,8,24,128]{5,4,3,2,1,0:T(8,128)S(1)} %get-tuple-element.66), channel_id=1, source_target_pairs={{0,4},{1,5},{2,6},{3,7},{4,0},{5,1},{6,2},{7,3},{8,12},{9,13},{10,... | collective-permute-start | bytes 1179656 | tf_op jit(solution)/shard_map/ppermute | solution.py:352
  15.4 0.1 slice_add_fusion.5
  15.5 1.8 %collective-permute-start.9 = (f32[2,2,1,8,24,128]{5,4,3,2,1,0:T(8,128)S(1)}, f32[2,2,1,8,24,128]{5,4,3,2,1,0:T(8,128)S(1)}, u32[]{:S(2)}, u32[]{:S(2)}) collective-permute-start(f32[2,2,1,8,24,128]{5,4,3,2,1,0:T(8,128)S(1)} %get-tuple-element.68), channel_id=1, source_target_pairs={{0,1},{1,0},{2,3},{3,2},{4,5},{5,4},{6,7},{7,6},{8,9},{9,8},{10,11... | collective-permute-start | bytes 1179656 | tf_op jit(solution)/shard_map/ppermute | solution.py:352
  17.4 0.2 slice_add_fusion
  17.6 2.1 %collective-permute-start.8 = (f32[2,1,2,8,32,128]{5,4,3,2,1,0:T(8,128)S(1)}, f32[2,1,2,8,32,128]{5,4,3,2,1,0:T(8,128)S(1)}, u32[]{:S(2)}, u32[]{:S(2)}) collective-permute-start(f32[2,1,2,8,32,128]{5,4,3,2,1,0:T(8,128)S(1)} %get-tuple-element.64), channel_id=1, source_target_pairs={{0,4},{1,5},{2,6},{3,7},{4,0},{5,1},{6,2},{7,3},{8,12},{9,13},{10,... | collective-permute-start | bytes 1572872 | tf_op jit(solution)/shard_map/ppermute | solution.py:352
  19.7 0.2 slice_add_fusion.2
  19.9 1.0 %collective-permute-start.7 = (f32[1,2,2,8,32,128]{5,4,3,2,1,0:T(8,128)S(1)}, f32[1,2,2,8,32,128]{5,4,3,2,1,0:T(8,128)S(1)}, u32[]{:S(2)}, u32[]{:S(2)}) collective-permute-start(f32[1,2,2,8,32,128]{5,4,3,2,1,0:T(8,128)S(1)} %get-tuple-element.73), channel_id=1, source_target_pairs={{0,32},{1,33},{2,34},{3,35},{4,36},{5,37},{6,38},{7,39},{8,40},{9,... | collective-permute-start | bytes 1572872 | tf_op jit(solution)/shard_map/ppermute | solution.py:352
  21.0 1.3 %collective-permute-start.5 = (f32[1,1,2,8,24,128]{5,4,3,2,1,0:T(8,128)S(1)}, f32[1,1,2,8,24,128]{5,4,3,2,1,0:T(8,128)S(1)}, u32[]{:S(2)}, u32[]{:S(2)}) collective-permute-start(f32[1,1,2,8,24,128]{5,4,3,2,1,0:T(8,128)S(1)} %get-tuple-element.81), channel_id=1, source_target_pairs={{0,4},{1,5},{2,6},{3,7},{4,0},{5,1},{6,2},{7,3},{8,12},{9,13},{10,... | collective-permute-start | bytes 589832 | tf_op jit(solution)/shard_map/ppermute | solution.py:352
  22.3 2.8 %collective-permute-start.15 = (f32[2,1,1,8,24,128]{5,4,3,2,1,0:T(8,128)S(1)}, f32[2,1,1,8,24,128]{5,4,3,2,1,0:T(8,128)S(1)}, u32[]{:S(2)}, u32[]{:S(2)}) collective-permute-start(f32[2,1,1,8,24,128]{5,4,3,2,1,0:T(8,128)S(1)} %get-tuple-element.78), channel_id=1, source_target_pairs={{0,1},{1,0},{2,3},{3,2},{4,5},{5,4},{6,7},{7,6},{8,9},{9,8},{10,11... | collective-permute-start | bytes 589832 | tf_op jit(solution)/shard_map/ppermute | solution.py:352
  25.1 1.0 %collective-permute-start.14 = (f32[1,2,1,8,24,128]{5,4,3,2,1,0:T(8,128)S(1)}, f32[1,2,1,8,24,128]{5,4,3,2,1,0:T(8,128)S(1)}, u32[]{:S(2)}, u32[]{:S(2)}) collective-permute-start(f32[1,2,1,8,24,128]{5,4,3,2,1,0:T(8,128)S(1)} %get-tuple-element.80), channel_id=1, source_target_pairs={{0,32},{1,33},{2,34},{3,35},{4,36},{5,37},{6,38},{7,39},{8,40},{9,... | collective-permute-start | bytes 589832 | tf_op jit(solution)/shard_map/ppermute | solution.py:352
  26.2 0.9 %collective-permute-done.8 = f32[2,1,2,8,32,128]{5,4,3,2,1,0:T(8,128)S(1)} collective-permute-done((f32[2,1,2,8,32,128]{5,4,3,2,1,0:T(8,128)S(1)}, f32[2,1,2,8,32,128]{5,4,3,2,1,0:T(8,128)S(1)}, u32[]{:S(2)}, u32[]{:S(2)}) %collective-permute-start.8) | collective-permute-done | bytes 524320 | tf_op jit(solution)/shard_map/ppermute | solution.py:352
  27.1 0.1 slice_add_fusion.10
  27.2 3.6 %collective-permute-start.13 = (f32[2,1,1,8,32,128]{5,4,3,2,1,0:T(8,128)S(1)}, f32[2,1,1,8,32,128]{5,4,3,2,1,0:T(8,128)S(1)}, u32[]{:S(2)}, u32[]{:S(2)}) collective-permute-start(f32[2,1,1,8,32,128]{5,4,3,2,1,0:T(8,128)S(1)} %get-tuple-element.70), channel_id=1, source_target_pairs={{0,1},{1,0},{2,3},{3,2},{4,5},{5,4},{6,7},{7,6},{8,9},{9,8},{10,11... | collective-permute-start | bytes 786440 | tf_op jit(solution)/shard_map/ppermute | solution.py:352
  30.7 0.1 slice_add_fusion.11
  30.8 0.1 collective-permute-start.12
  30.9 1.8 %collective-permute-start.11 = (f32[1,1,1,8,24,128]{5,4,3,2,1,0:T(8,128)S(1)}, f32[1,1,1,8,24,128]{5,4,3,2,1,0:T(8,128)S(1)}, u32[]{:S(2)}, u32[]{:S(2)}) collective-permute-start(f32[1,1,1,8,24,128]{5,4,3,2,1,0:T(8,128)S(1)} %slice_add_fusion.28), channel_id=1, source_target_pairs={{0,1},{1,0},{2,3},{3,2},{4,5},{5,4},{6,7},{7,6},{8,9},{9,8},{10,11... | collective-permute-start | bytes 294920 | tf_op jit(solution)/shard_map/ppermute | solution.py:352
  32.8 1.0 %collective-permute-start.16 = (f32[1,1,1,8,24,128]{5,4,3,2,1,0:T(8,128)S(1)}, f32[1,1,1,8,24,128]{5,4,3,2,1,0:T(8,128)S(1)}, u32[]{:S(2)}, u32[]{:S(2)}) collective-permute-start(f32[1,1,1,8,24,128]{5,4,3,2,1,0:T(8,128)S(1)} %slice_add_fusion.26), channel_id=1, source_target_pairs={{0,32},{1,33},{2,34},{3,35},{4,36},{5,37},{6,38},{7,39},{8,40},{9,... | collective-permute-start | bytes 294920 | tf_op jit(solution)/shard_map/ppermute | solution.py:352
  33.8 0.4 collective-permute-start.17
  34.2 0.9 %collective-permute-done.13 = f32[2,1,1,8,32,128]{5,4,3,2,1,0:T(8,128)S(1)} collective-permute-done((f32[2,1,1,8,32,128]{5,4,3,2,1,0:T(8,128)S(1)}, f32[2,1,1,8,32,128]{5,4,3,2,1,0:T(8,128)S(1)}, u32[]{:S(2)}, u32[]{:S(2)}) %collective-permute-start.13) | collective-permute-done | bytes 262176 | tf_op jit(solution)/shard_map/ppermute | solution.py:352
  35.1 1.0 %collective-permute-start.19 = (f32[1,1,1,8,32,128]{5,4,3,2,1,0:T(8,128)S(1)}, f32[1,1,1,8,32,128]{5,4,3,2,1,0:T(8,128)S(1)}, u32[]{:S(2)}, u32[]{:S(2)}) collective-permute-start(f32[1,1,1,8,32,128]{5,4,3,2,1,0:T(8,128)S(1)} %slice_add_fusion.22), channel_id=1, source_target_pairs={{0,32},{1,33},{2,34},{3,35},{4,36},{5,37},{6,38},{7,39},{8,40},{9,... | collective-permute-start | bytes 393224 | tf_op jit(solution)/shard_map/ppermute | solution.py:352
  36.1 1.1 %collective-permute-done.12 = f32[1,1,2,8,32,128]{5,4,3,2,1,0:T(8,128)S(1)} collective-permute-done((f32[1,1,2,8,32,128]{5,4,3,2,1,0:T(8,128)S(1)}, f32[1,1,2,8,32,128]{5,4,3,2,1,0:T(8,128)S(1)}, u32[]{:S(2)}, u32[]{:S(2)}) %collective-permute-start.12) | collective-permute-done | bytes 262176 | tf_op jit(solution)/shard_map/ppermute | solution.py:352
  37.3 1.0 %collective-permute-start.18 = (f32[1,1,1,8,32,128]{5,4,3,2,1,0:T(8,128)S(1)}, f32[1,1,1,8,32,128]{5,4,3,2,1,0:T(8,128)S(1)}, u32[]{:S(2)}, u32[]{:S(2)}) collective-permute-start(f32[1,1,1,8,32,128]{5,4,3,2,1,0:T(8,128)S(1)} %slice_add_fusion.23), channel_id=1, source_target_pairs={{0,1},{1,0},{2,3},{3,2},{4,5},{5,4},{6,7},{7,6},{8,9},{9,8},{10,11... | collective-permute-start | bytes 393224 | tf_op jit(solution)/shard_map/ppermute | solution.py:352
  38.3 0.2 collective-permute-done.17
  38.6 1.5 %collective-permute-done.19 = f32[1,1,1,8,32,128]{5,4,3,2,1,0:T(8,128)S(1)} collective-permute-done((f32[1,1,1,8,32,128]{5,4,3,2,1,0:T(8,128)S(1)}, f32[1,1,1,8,32,128]{5,4,3,2,1,0:T(8,128)S(1)}, u32[]{:S(2)}, u32[]{:S(2)}) %collective-permute-start.19) | collective-permute-done | bytes 131104 | tf_op jit(solution)/shard_map/ppermute | solution.py:352
  40.2 2.2 %collective-permute-done.18 = f32[1,1,1,8,32,128]{5,4,3,2,1,0:T(8,128)S(1)} collective-permute-done((f32[1,1,1,8,32,128]{5,4,3,2,1,0:T(8,128)S(1)}, f32[1,1,1,8,32,128]{5,4,3,2,1,0:T(8,128)S(1)}, u32[]{:S(2)}, u32[]{:S(2)}) %collective-permute-start.18) | collective-permute-done | bytes 131104 | tf_op jit(solution)/shard_map/ppermute | solution.py:352
  42.5 2.6 %collective-permute-start.20 = (f32[2,136,128]{2,1,0:T(8,128)S(1)}, f32[2,136,128]{2,1,0:T(8,128)S(1)}, u32[]{:S(2)}, u32[]{:S(2)}) collective-permute-start(f32[2,136,128]{2,1,0:T(8,128)S(1)} %get-tuple-element.87), channel_id=1, source_target_pairs={{0,108},{1,109},{2,110},{3,111},{4,104},{5,105},{6,106},{7,107},{8... | collective-permute-start | bytes 417800 | tf_op jit(solution)/shard_map/ppermute | solution.py:352
  45.1 1.1 %collective-permute-start.22 = (f32[2,136,128]{2,1,0:T(8,128)S(1)}, f32[2,136,128]{2,1,0:T(8,128)S(1)}, u32[]{:S(2)}, u32[]{:S(2)}) collective-permute-start(f32[2,136,128]{2,1,0:T(8,128)S(1)} %get-tuple-element.88), channel_id=1, source_target_pairs={{0,12},{1,13},{2,14},{3,15},{4,8},{5,9},{6,10},{7,11},{8,4},{9,5},... | collective-permute-start | bytes 417800 | tf_op jit(solution)/shard_map/ppermute | solution.py:352
  46.2 2.3 %collective-permute-start.21 = (f32[2,136,128]{2,1,0:T(8,128)S(1)}, f32[2,136,128]{2,1,0:T(8,128)S(1)}, u32[]{:S(2)}, u32[]{:S(2)}) collective-permute-start(f32[2,136,128]{2,1,0:T(8,128)S(1)} %get-tuple-element.89), channel_id=1, source_target_pairs={{0,96},{1,97},{2,98},{3,99},{4,100},{5,101},{6,102},{7,103},{8,104... | collective-permute-start | bytes 417800 | tf_op jit(solution)/shard_map/ppermute | solution.py:352
  48.4 2.6 %collective-permute-done.20 = f32[2,136,128]{2,1,0:T(8,128)S(1)} collective-permute-done((f32[2,136,128]{2,1,0:T(8,128)S(1)}, f32[2,136,128]{2,1,0:T(8,128)S(1)}, u32[]{:S(2)}, u32[]{:S(2)}) %collective-permute-start.20) | collective-permute-done | bytes 139296 | tf_op jit(solution)/shard_map/ppermute | solution.py:352
  51.0 1.4 %collective-permute-done.22 = f32[2,136,128]{2,1,0:T(8,128)S(1)} collective-permute-done((f32[2,136,128]{2,1,0:T(8,128)S(1)}, f32[2,136,128]{2,1,0:T(8,128)S(1)}, u32[]{:S(2)}, u32[]{:S(2)}) %collective-permute-start.22) | collective-permute-done | bytes 139296 | tf_op jit(solution)/shard_map/ppermute | solution.py:352
  52.5 3.7 %collective-permute-start.23 = (f32[136,128]{1,0:T(8,128)S(1)}, f32[136,128]{1,0:T(8,128)S(1)}, u32[]{:S(2)}, u32[]{:S(2)}) collective-permute-start(f32[136,128]{1,0:T(8,128)S(1)} %slice_bitcast_fusion.4), channel_id=1, source_target_pairs={{0,3},{1,2},{2,1},{3,0},{4,7},{5,6},{6,5},{7,4},{8,11},{9,10},{10,... | collective-permute-start | bytes 208904 | tf_op jit(solution)/shard_map/ppermute | solution.py:352
  56.2 2.3 %collective-permute-done.23 = f32[136,128]{1,0:T(8,128)S(1)} collective-permute-done((f32[136,128]{1,0:T(8,128)S(1)}, f32[136,128]{1,0:T(8,128)S(1)}, u32[]{:S(2)}, u32[]{:S(2)}) %collective-permute-start.23) | collective-permute-done | bytes 69664 | tf_op jit(solution)/shard_map/ppermute | solution.py:352
  58.5 3.4 %collective-permute-start.24 = (f32[128,128]{1,0:T(8,128)S(1)}, f32[128,128]{1,0:T(8,128)S(1)}, u32[]{:S(2)}, u32[]{:S(2)}) collective-permute-start(f32[128,128]{1,0:T(8,128)S(1)} %slice.318), channel_id=1, source_target_pairs={{0,1},{1,0},{2,17},{3,16},{4,33},{5,32},{6,49},{7,48},{8,65},{9,64... | collective-permute-start | bytes 196616 | tf_op jit(solution)/shard_map/ppermute | solution.py:352
  61.9 7.0 %collective-permute-done.24.theirs = f32[128,128]{1,0:T(8,128)S(1)} collective-permute-done((f32[128,128]{1,0:T(8,128)S(1)}, f32[128,128]{1,0:T(8,128)S(1)}, u32[]{:S(2)}, u32[]{:S(2)}) %collective-permute-start.24) | collective-permute-done | bytes 65568 | tf_op jit(solution)/shard_map/ppermute | solution.py:352
  68.9 0.7 finish.1
  (36 shorter events, 0.5 us)
Async XLA Ops:
  10.0 2.4 %collective-permute-start = (f32[64,24,128]{2,1,0:T(8,128)S(1)}, f32[64,24,128]{2,1,0:T(8,128)S(1)}, u32[]{:S(2)}, u32[]{:S(2)}) collective-permute-start(f32[64,24,128]{2,1,0:T(8,128)S(1)} %get-tuple-element.35), channel_id=1, source_target_pairs={{0,16},{1,17},{2,18},{3,19},{4,20},{5,21},{6,22},{7,23},{8,24},{9,... | collective-permute-start | bytes 2359304 | tf_op jit(solution)/shard_map/ppermute | solution.py:352
  10.1 3.4 %collective-permute-start.3 = (f32[64,24,128]{2,1,0:T(8,128)S(1)}, f32[64,24,128]{2,1,0:T(8,128)S(1)}, u32[]{:S(2)}, u32[]{:S(2)}) collective-permute-start(f32[64,24,128]{2,1,0:T(8,128)S(1)} %get-tuple-element.39), channel_id=1, source_target_pairs={{0,16},{1,17},{2,18},{3,19},{4,20},{5,21},{6,22},{7,23},{8,24},{9,... | collective-permute-start | bytes 2359304 | tf_op jit(solution)/shard_map/ppermute | solution.py:352
  10.6 4.8 %collective-permute-start.4 = (f32[64,24,128]{2,1,0:T(8,128)S(1)}, f32[64,24,128]{2,1,0:T(8,128)S(1)}, u32[]{:S(2)}, u32[]{:S(2)}) collective-permute-start(f32[64,24,128]{2,1,0:T(8,128)S(1)} %get-tuple-element.42), channel_id=1, source_target_pairs={{0,16},{1,17},{2,18},{3,19},{4,20},{5,21},{6,22},{7,23},{8,24},{9,... | collective-permute-start | bytes 2359304 | tf_op jit(solution)/shard_map/ppermute | solution.py:352
  10.7 6.7 %collective-permute-start.2 = (f32[64,32,128]{2,1,0:T(8,128)S(1)}, f32[64,32,128]{2,1,0:T(8,128)S(1)}, u32[]{:S(2)}, u32[]{:S(2)}) collective-permute-start(f32[64,32,128]{2,1,0:T(8,128)S(1)} %get-tuple-element.37), channel_id=1, source_target_pairs={{0,16},{1,17},{2,18},{3,19},{4,20},{5,21},{6,22},{7,23},{8,24},{9,... | collective-permute-start | bytes 3145736 | tf_op jit(solution)/shard_map/ppermute | solution.py:352
  11.1 8.5 %collective-permute-start.6 = (f32[64,32,128]{2,1,0:T(8,128)S(1)}, f32[64,32,128]{2,1,0:T(8,128)S(1)}, u32[]{:S(2)}, u32[]{:S(2)}) collective-permute-start(f32[64,32,128]{2,1,0:T(8,128)S(1)} %get-tuple-element.47), channel_id=1, source_target_pairs={{0,16},{1,17},{2,18},{3,19},{4,20},{5,21},{6,22},{7,23},{8,24},{9,... | collective-permute-start | bytes 3145736 | tf_op jit(solution)/shard_map/ppermute | solution.py:352
  12.5 8.4 %collective-permute-start.1 = (f32[1,2,2,8,24,128]{5,4,3,2,1,0:T(8,128)S(1)}, f32[1,2,2,8,24,128]{5,4,3,2,1,0:T(8,128)S(1)}, u32[]{:S(2)}, u32[]{:S(2)}) collective-permute-start(f32[1,2,2,8,24,128]{5,4,3,2,1,0:T(8,128)S(1)} %get-tuple-element.83), channel_id=1, source_target_pairs={{0,32},{1,33},{2,34},{3,35},{4,36},{5,37},{6,38},{7,39},{8,40},{9,... | collective-permute-start | bytes 1179656 | tf_op jit(solution)/shard_map/ppermute | solution.py:352
  13.6 8.6 %collective-permute-start.10 = (f32[2,1,2,8,24,128]{5,4,3,2,1,0:T(8,128)S(1)}, f32[2,1,2,8,24,128]{5,4,3,2,1,0:T(8,128)S(1)}, u32[]{:S(2)}, u32[]{:S(2)}) collective-permute-start(f32[2,1,2,8,24,128]{5,4,3,2,1,0:T(8,128)S(1)} %get-tuple-element.66), channel_id=1, source_target_pairs={{0,4},{1,5},{2,6},{3,7},{4,0},{5,1},{6,2},{7,3},{8,12},{9,13},{10,... | collective-permute-start | bytes 1179656 | tf_op jit(solution)/shard_map/ppermute | solution.py:352
  15.5 9.5 %collective-permute-start.9 = (f32[2,2,1,8,24,128]{5,4,3,2,1,0:T(8,128)S(1)}, f32[2,2,1,8,24,128]{5,4,3,2,1,0:T(8,128)S(1)}, u32[]{:S(2)}, u32[]{:S(2)}) collective-permute-start(f32[2,2,1,8,24,128]{5,4,3,2,1,0:T(8,128)S(1)} %get-tuple-element.68), channel_id=1, source_target_pairs={{0,1},{1,0},{2,3},{3,2},{4,5},{5,4},{6,7},{7,6},{8,9},{9,8},{10,11... | collective-permute-start | bytes 1179656 | tf_op jit(solution)/shard_map/ppermute | solution.py:352
  17.6 9.5 %collective-permute-start.8 = (f32[2,1,2,8,32,128]{5,4,3,2,1,0:T(8,128)S(1)}, f32[2,1,2,8,32,128]{5,4,3,2,1,0:T(8,128)S(1)}, u32[]{:S(2)}, u32[]{:S(2)}) collective-permute-start(f32[2,1,2,8,32,128]{5,4,3,2,1,0:T(8,128)S(1)} %get-tuple-element.64), channel_id=1, source_target_pairs={{0,4},{1,5},{2,6},{3,7},{4,0},{5,1},{6,2},{7,3},{8,12},{9,13},{10,... | collective-permute-start | bytes 1572872 | tf_op jit(solution)/shard_map/ppermute | solution.py:352
  19.9 10.9 %collective-permute-start.7 = (f32[1,2,2,8,32,128]{5,4,3,2,1,0:T(8,128)S(1)}, f32[1,2,2,8,32,128]{5,4,3,2,1,0:T(8,128)S(1)}, u32[]{:S(2)}, u32[]{:S(2)}) collective-permute-start(f32[1,2,2,8,32,128]{5,4,3,2,1,0:T(8,128)S(1)} %get-tuple-element.73), channel_id=1, source_target_pairs={{0,32},{1,33},{2,34},{3,35},{4,36},{5,37},{6,38},{7,39},{8,40},{9,... | collective-permute-start | bytes 1572872 | tf_op jit(solution)/shard_map/ppermute | solution.py:352
  21.0 10.0 %collective-permute-start.5 = (f32[1,1,2,8,24,128]{5,4,3,2,1,0:T(8,128)S(1)}, f32[1,1,2,8,24,128]{5,4,3,2,1,0:T(8,128)S(1)}, u32[]{:S(2)}, u32[]{:S(2)}) collective-permute-start(f32[1,1,2,8,24,128]{5,4,3,2,1,0:T(8,128)S(1)} %get-tuple-element.81), channel_id=1, source_target_pairs={{0,4},{1,5},{2,6},{3,7},{4,0},{5,1},{6,2},{7,3},{8,12},{9,13},{10,... | collective-permute-start | bytes 589832 | tf_op jit(solution)/shard_map/ppermute | solution.py:352
  22.3 10.5 %collective-permute-start.15 = (f32[2,1,1,8,24,128]{5,4,3,2,1,0:T(8,128)S(1)}, f32[2,1,1,8,24,128]{5,4,3,2,1,0:T(8,128)S(1)}, u32[]{:S(2)}, u32[]{:S(2)}) collective-permute-start(f32[2,1,1,8,24,128]{5,4,3,2,1,0:T(8,128)S(1)} %get-tuple-element.78), channel_id=1, source_target_pairs={{0,1},{1,0},{2,3},{3,2},{4,5},{5,4},{6,7},{7,6},{8,9},{9,8},{10,11... | collective-permute-start | bytes 589832 | tf_op jit(solution)/shard_map/ppermute | solution.py:352
  25.1 8.7 %collective-permute-start.14 = (f32[1,2,1,8,24,128]{5,4,3,2,1,0:T(8,128)S(1)}, f32[1,2,1,8,24,128]{5,4,3,2,1,0:T(8,128)S(1)}, u32[]{:S(2)}, u32[]{:S(2)}) collective-permute-start(f32[1,2,1,8,24,128]{5,4,3,2,1,0:T(8,128)S(1)} %get-tuple-element.80), channel_id=1, source_target_pairs={{0,32},{1,33},{2,34},{3,35},{4,36},{5,37},{6,38},{7,39},{8,40},{9,... | collective-permute-start | bytes 589832 | tf_op jit(solution)/shard_map/ppermute | solution.py:352
  27.2 7.9 %collective-permute-start.13 = (f32[2,1,1,8,32,128]{5,4,3,2,1,0:T(8,128)S(1)}, f32[2,1,1,8,32,128]{5,4,3,2,1,0:T(8,128)S(1)}, u32[]{:S(2)}, u32[]{:S(2)}) collective-permute-start(f32[2,1,1,8,32,128]{5,4,3,2,1,0:T(8,128)S(1)} %get-tuple-element.70), channel_id=1, source_target_pairs={{0,1},{1,0},{2,3},{3,2},{4,5},{5,4},{6,7},{7,6},{8,9},{9,8},{10,11... | collective-permute-start | bytes 786440 | tf_op jit(solution)/shard_map/ppermute | solution.py:352
  30.8 6.5 %collective-permute-start.12 = (f32[1,1,2,8,32,128]{5,4,3,2,1,0:T(8,128)S(1)}, f32[1,1,2,8,32,128]{5,4,3,2,1,0:T(8,128)S(1)}, u32[]{:S(2)}, u32[]{:S(2)}) collective-permute-start(f32[1,1,2,8,32,128]{5,4,3,2,1,0:T(8,128)S(1)} %get-tuple-element.72), channel_id=1, source_target_pairs={{0,4},{1,5},{2,6},{3,7},{4,0},{5,1},{6,2},{7,3},{8,12},{9,13},{10,... | collective-permute-start | bytes 786440 | tf_op jit(solution)/shard_map/ppermute | solution.py:352
  30.9 7.3 %collective-permute-start.11 = (f32[1,1,1,8,24,128]{5,4,3,2,1,0:T(8,128)S(1)}, f32[1,1,1,8,24,128]{5,4,3,2,1,0:T(8,128)S(1)}, u32[]{:S(2)}, u32[]{:S(2)}) collective-permute-start(f32[1,1,1,8,24,128]{5,4,3,2,1,0:T(8,128)S(1)} %slice_add_fusion.28), channel_id=1, source_target_pairs={{0,1},{1,0},{2,3},{3,2},{4,5},{5,4},{6,7},{7,6},{8,9},{9,8},{10,11... | collective-permute-start | bytes 294920 | tf_op jit(solution)/shard_map/ppermute | solution.py:352
  32.8 5.5 %collective-permute-start.16 = (f32[1,1,1,8,24,128]{5,4,3,2,1,0:T(8,128)S(1)}, f32[1,1,1,8,24,128]{5,4,3,2,1,0:T(8,128)S(1)}, u32[]{:S(2)}, u32[]{:S(2)}) collective-permute-start(f32[1,1,1,8,24,128]{5,4,3,2,1,0:T(8,128)S(1)} %slice_add_fusion.26), channel_id=1, source_target_pairs={{0,32},{1,33},{2,34},{3,35},{4,36},{5,37},{6,38},{7,39},{8,40},{9,... | collective-permute-start | bytes 294920 | tf_op jit(solution)/shard_map/ppermute | solution.py:352
  33.8 4.7 %collective-permute-start.17 = (f32[1,1,1,8,24,128]{5,4,3,2,1,0:T(8,128)S(1)}, f32[1,1,1,8,24,128]{5,4,3,2,1,0:T(8,128)S(1)}, u32[]{:S(2)}, u32[]{:S(2)}) collective-permute-start(f32[1,1,1,8,24,128]{5,4,3,2,1,0:T(8,128)S(1)} %slice_add_fusion.27), channel_id=1, source_target_pairs={{0,4},{1,5},{2,6},{3,7},{4,0},{5,1},{6,2},{7,3},{8,12},{9,13},{10,... | collective-permute-start | bytes 294920 | tf_op jit(solution)/shard_map/ppermute | solution.py:352
  35.1 5.0 %collective-permute-start.19 = (f32[1,1,1,8,32,128]{5,4,3,2,1,0:T(8,128)S(1)}, f32[1,1,1,8,32,128]{5,4,3,2,1,0:T(8,128)S(1)}, u32[]{:S(2)}, u32[]{:S(2)}) collective-permute-start(f32[1,1,1,8,32,128]{5,4,3,2,1,0:T(8,128)S(1)} %slice_add_fusion.22), channel_id=1, source_target_pairs={{0,32},{1,33},{2,34},{3,35},{4,36},{5,37},{6,38},{7,39},{8,40},{9,... | collective-permute-start | bytes 393224 | tf_op jit(solution)/shard_map/ppermute | solution.py:352
  37.3 5.0 %collective-permute-start.18 = (f32[1,1,1,8,32,128]{5,4,3,2,1,0:T(8,128)S(1)}, f32[1,1,1,8,32,128]{5,4,3,2,1,0:T(8,128)S(1)}, u32[]{:S(2)}, u32[]{:S(2)}) collective-permute-start(f32[1,1,1,8,32,128]{5,4,3,2,1,0:T(8,128)S(1)} %slice_add_fusion.23), channel_id=1, source_target_pairs={{0,1},{1,0},{2,3},{3,2},{4,5},{5,4},{6,7},{7,6},{8,9},{9,8},{10,11... | collective-permute-start | bytes 393224 | tf_op jit(solution)/shard_map/ppermute | solution.py:352
  42.5 8.6 %collective-permute-start.20 = (f32[2,136,128]{2,1,0:T(8,128)S(1)}, f32[2,136,128]{2,1,0:T(8,128)S(1)}, u32[]{:S(2)}, u32[]{:S(2)}) collective-permute-start(f32[2,136,128]{2,1,0:T(8,128)S(1)} %get-tuple-element.87), channel_id=1, source_target_pairs={{0,108},{1,109},{2,110},{3,111},{4,104},{5,105},{6,106},{7,107},{8... | collective-permute-start | bytes 417800 | tf_op jit(solution)/shard_map/ppermute | solution.py:352
  45.1 7.3 %collective-permute-start.22 = (f32[2,136,128]{2,1,0:T(8,128)S(1)}, f32[2,136,128]{2,1,0:T(8,128)S(1)}, u32[]{:S(2)}, u32[]{:S(2)}) collective-permute-start(f32[2,136,128]{2,1,0:T(8,128)S(1)} %get-tuple-element.88), channel_id=1, source_target_pairs={{0,12},{1,13},{2,14},{3,15},{4,8},{5,9},{6,10},{7,11},{8,4},{9,5},... | collective-permute-start | bytes 417800 | tf_op jit(solution)/shard_map/ppermute | solution.py:352
  46.2 6.3 %collective-permute-start.21 = (f32[2,136,128]{2,1,0:T(8,128)S(1)}, f32[2,136,128]{2,1,0:T(8,128)S(1)}, u32[]{:S(2)}, u32[]{:S(2)}) collective-permute-start(f32[2,136,128]{2,1,0:T(8,128)S(1)} %get-tuple-element.89), channel_id=1, source_target_pairs={{0,96},{1,97},{2,98},{3,99},{4,100},{5,101},{6,102},{7,103},{8,104... | collective-permute-start | bytes 417800 | tf_op jit(solution)/shard_map/ppermute | solution.py:352
  52.5 6.0 %collective-permute-start.23 = (f32[136,128]{1,0:T(8,128)S(1)}, f32[136,128]{1,0:T(8,128)S(1)}, u32[]{:S(2)}, u32[]{:S(2)}) collective-permute-start(f32[136,128]{1,0:T(8,128)S(1)} %slice_bitcast_fusion.4), channel_id=1, source_target_pairs={{0,3},{1,2},{2,1},{3,0},{4,7},{5,6},{6,5},{7,4},{8,11},{9,10},{10,... | collective-permute-start | bytes 208904 | tf_op jit(solution)/shard_map/ppermute | solution.py:352
  58.5 10.4 %collective-permute-start.24 = (f32[128,128]{1,0:T(8,128)S(1)}, f32[128,128]{1,0:T(8,128)S(1)}, u32[]{:S(2)}, u32[]{:S(2)}) collective-permute-start(f32[128,128]{1,0:T(8,128)S(1)} %slice.318), channel_id=1, source_target_pairs={{0,1},{1,0},{2,17},{3,16},{4,33},{5,32},{6,49},{7,48},{8,65},{9,64... | collective-permute-start | bytes 196616 | tf_op jit(solution)/shard_map/ppermute | solution.py:352
